TPU v7x, 256 devices: a whole 4x4x8 slice. The times are simulated.
256 devices in a mesh: batch: 8 (over z_lo, y), seq: 32 (over x, z_hi, core).
Axes of the slice: x: 4, y: 4, z: 8 (z_hi: 4, z_lo: 2; z = z_hi * 2 + z_lo), core: 2. Of those that a mesh axis runs over, the one named last changes fastest.
Arguments:
- history: bfloat16 [8, 4096, 1024], P('batch', 'seq'), may hold values from -6 to 6
- candidates: bfloat16 [8, 1024, 1024], P('batch', 'seq'), may hold values from -6 to 6
- event_times: int32 [8, 4096], P('batch', 'seq'), may hold values from 0 to 8382465, as said below
- request_times: int32 [8, 1024], P('batch', 'seq'), may hold values from 8382466 to 8448000, as said below
- w_proj: bfloat16 [1024, 4096], P(None, 'batch'), may hold values from -0.1875 to 0.1875
- w_out: bfloat16 [1024, 1024], P('batch'), may hold values from -0.1875 to 0.1875
- bias_steps: float32 [24, 8], replicated, may hold values from -1 to 1
Outputs:
- history_out: bfloat16 [8, 4096, 1024], P('batch', 'seq')
- cand_out: bfloat16 [8, 1024, 1024], P('batch', 'seq')
Inputs may be any that keep to these rules, and one draw needn't show every extreme that they name: `event_times`: Non-decreasing along each user's history; each user's first event is at time 0 and its last at 8382465. `request_times`: every candidate's time is later than all events of its user's history, by 1 to 65535.
All inputs are finite; a program needn't handle non-finite values.
Results may differ from a plain program's by a relative error of at most 0.012.
Values may be sent and summed in bfloat16 or wider, within the bound.
No kernel may reach another device: no remote copies, remote signals or barrier semaphores. Data moves between devices by JAX's collectives and lax.ppermute only.
A program may use at most 128 MiB of HBM per device.

v0:
```python
import math

import jax
import jax.numpy as jnp
from jax import lax
from jax.sharding import PartitionSpec as P


def layer_norm(tensor):
    center = jnp.mean(tensor, axis=-1, keepdims=True)
    shifted = tensor - center
    spread = jnp.mean(shifted * shifted, axis=-1, keepdims=True)
    return shifted * lax.rsqrt(spread + 1e-06)


def pair_bias(query_pos, query_time, key_pos, key_time, bias_steps):
    levels = bias_steps.shape[0] // 2
    time_gap = query_time[:, None] - key_time[None, :]
    place_gap = query_pos[:, None] - key_pos[None, :]
    total = jnp.zeros((bias_steps.shape[1], time_gap.shape[0], time_gap.shape[1]), jnp.float32)
    for level in range(levels):
        time_mark = time_gap >= jnp.int32(4**level)
        place_mark = place_gap >= jnp.int32(2**level)
        total = total + jnp.where(
            time_mark[None], bias_steps[level][:, None, None], jnp.float32(0.0)
        )
        total = total + jnp.where(
            place_mark[None], bias_steps[levels + level][:, None, None], jnp.float32(0.0)
        )
    return total


def attend(queries, keys, values, query_pos, query_time, key_pos, key_time, bias_steps):
    heads = bias_steps.shape[1]
    head_dim = queries.shape[1] // heads
    query_heads = queries.reshape(queries.shape[0], heads, head_dim)
    key_heads = keys.reshape(keys.shape[0], heads, head_dim)
    value_heads = values.reshape(values.shape[0], heads, head_dim)
    scores = jnp.einsum(
        "rhd,khd->hrk", query_heads, key_heads, preferred_element_type=jnp.float32
    ) * head_dim ** (-0.5)
    scores = scores + pair_bias(query_pos, query_time, key_pos, key_time, bias_steps)
    allowed = key_pos[None, :] <= query_pos[:, None]
    weights = jnp.where(allowed[None], jax.nn.silu(scores), 0.0).astype(jnp.bfloat16)
    mixed = jnp.einsum("hrk,khd->rhd", weights, value_heads, preferred_element_type=jnp.float32)
    return mixed.reshape(queries.shape[0], heads * head_dim)


def own_term(queries, keys, values, heads):
    head_dim = queries.shape[1] // heads
    query_heads = queries.reshape(queries.shape[0], heads, head_dim).astype(jnp.float32)
    key_heads = keys.reshape(keys.shape[0], heads, head_dim).astype(jnp.float32)
    value_heads = values.reshape(values.shape[0], heads, head_dim).astype(jnp.float32)
    dots = jnp.sum(query_heads * key_heads, axis=-1) * head_dim ** (-0.5)
    weights = lax.optimization_barrier(jax.nn.silu(dots).astype(jnp.bfloat16)).astype(jnp.float32)
    return (weights[:, :, None] * value_heads).reshape(queries.shape[0], heads * head_dim)


def visit(running, group, keys, values, key_pos, key_time, bias_steps):
    queries, query_pos, query_time, latest = group

    def compute(accum):
        return accum + attend(
            queries, keys, values, query_pos, query_time, key_pos, key_time, bias_steps
        )

    def keep(accum):
        return accum

    return lax.cond(key_pos[0] <= latest, compute, keep, running)


def key_sweep(groups, keys, values, all_times, bias_steps):
    inits = tuple((jnp.zeros((group[0].shape[0], keys.shape[1]), jnp.float32) for group in groups))
    totals = inits
    piece_keys = lax.all_gather(keys, "seq", axis=0, tiled=True)
    piece_values = lax.all_gather(values, "seq", axis=0, tiled=True)
    count = piece_keys.shape[0]
    tile_size = math.gcd(count, 512)
    tile_count = count // tile_size
    tiled_keys = piece_keys.reshape(tile_count, tile_size, piece_keys.shape[1])
    tiled_values = piece_values.reshape(tile_count, tile_size, piece_values.shape[1])

    def tile_step(carry, tile_item):
        tile_index, tile_keys, tile_values = tile_item
        first = tile_index * tile_size
        key_pos = first + jnp.arange(tile_size, dtype=jnp.int32)
        key_time = lax.dynamic_slice_in_dim(all_times, first, tile_size)
        updated = tuple(
            (
                visit(running, group, tile_keys, tile_values, key_pos, key_time, bias_steps)
                for running, group in zip(carry, groups)
            )
        )
        return (updated, None)

    totals, _ = lax.scan(
        tile_step, totals, (jnp.arange(tile_count, dtype=jnp.int32), tiled_keys, tiled_values)
    )
    return totals


def body(history, candidates, event_times, request_times, w_proj, w_out, bias_steps):
    heads = bias_steps.shape[1]
    hist_rows = history.shape[1]
    cand_rows = candidates.shape[1]
    seq_count = lax.axis_size("seq")
    place = lax.axis_index("seq")
    length = hist_rows * seq_count
    all_rows = jnp.concatenate([history[0], candidates[0]], axis=0)
    normed = layer_norm(all_rows.astype(jnp.float32)).astype(jnp.bfloat16)
    mixed = jax.nn.silu(
        jnp.dot(
            normed,
            lax.all_gather(w_proj, "batch", axis=1, tiled=True),
            preferred_element_type=jnp.float32,
        )
    ).astype(jnp.bfloat16)
    width = mixed.shape[1] // 4
    gate = mixed[:, :width]
    values = mixed[:, width : 2 * width]
    queries = mixed[:, 2 * width : 3 * width]
    keys = mixed[:, 3 * width :]
    hist_time = event_times[0]
    cand_time = request_times[0]
    all_times = lax.all_gather(hist_time, "seq", axis=0, tiled=True)
    hist_pos = place * hist_rows + jnp.arange(hist_rows, dtype=jnp.int32)
    cand_pos = jnp.full((cand_rows,), length, jnp.int32)
    hist_keys = keys[:hist_rows]
    hist_values = values[:hist_rows]
    hist_queries = queries[:hist_rows]
    cand_queries = queries[hist_rows:]
    cand_last = jnp.int32(length)
    groups = [
        (hist_queries, hist_pos, hist_time, place * hist_rows + hist_rows - 1),
        (cand_queries, cand_pos, cand_time, cand_last),
    ]
    sums = key_sweep(groups, hist_keys, hist_values, all_times, bias_steps)
    hist_attended = sums[0].astype(jnp.bfloat16)
    cand_sums = sums[1]
    own = own_term(cand_queries, keys[hist_rows:], values[hist_rows:], heads)
    attended = jnp.concatenate([hist_attended, (cand_sums + own).astype(jnp.bfloat16)], axis=0)
    gated = (layer_norm(attended.astype(jnp.float32)) * gate.astype(jnp.float32)).astype(
        jnp.bfloat16
    )
    projected = jnp.dot(
        gated,
        lax.all_gather(w_out, "batch", axis=0, tiled=True),
        preferred_element_type=jnp.float32,
    )
    result = (all_rows.astype(jnp.float32) + projected).astype(jnp.bfloat16)
    return (result[None, :hist_rows], result[None, hist_rows:])


def solution(mesh):
    in_specs = (
        P("batch", "seq", None),
        P("batch", "seq", None),
        P("batch", "seq"),
        P("batch", "seq"),
        P(None, "batch"),
        P("batch", None),
        P(),
    )
    out_specs = (P("batch", "seq", None), P("batch", "seq", None))
    return jax.shard_map(body, mesh=mesh, in_specs=in_specs, out_specs=out_specs, check_vma=False)
```

profile of v0, /device:TPU:199, one launch (start us, length us, event | category | flops | bytes accessed | tf_op | source)
XLA Modules:
  0.0 473.4 jit_solution(16721378898934839067)
XLA Ops:
  10.3 93.9 %all-gather.6.cloned.1.call-done = bf16[1024,4096]{1,0:T(8,128)(2,1)} async-done(((bf16[1024,512]{1,0:T(8,128)(2,1)}), bf16[1024,4096]{1,0:T(8,128)(2,1)}) %all-gather.6.cloned.1.call-update) | async-done | bytes 8388624 | tf_op jit(solution)/shard_map/all_gather | solution.py:115
  104.2 5.2 %multiply_convert_fusion = bf16[160,4096]{1,0:T(8,128)(2,1)S(1)} fusion(bf16[1024,4096]{1,0:T(8,128)(2,1)} %all-gather.6.cloned.1.call-done, f32[160]{0:T(256)S(1)} %add_rsqrt_fusion.1, f32[160]{0:T(256)S(1)} %broadcast_multiply_fusion.1, bf16[32,1024]{1,0:T(8,128)(2,1)} %bitcast.199, bf16[128,1024]{1,0:T(8,128)(2,1)} %bitcast.193), kind=kOutput, calls=%fused_computation.279 | convolution fusion | flops 1346600960 | bytes 10028288 | tf_op jit(solution)/shard_map/dot_general | solution.py:113
  111.8 40.5 %all-gather = s32[1,4096]{1,0:T(1,128)} all-gather(s32[1,128]{1,0:T(1,128)} %param.15), channel_id=2, replica_groups=mesh['batch'=8,'seq'=32] {'seq'}, dimensions={1}, use_global_device_ids=true | all-gather | bytes 16896 | tf_op jit(solution)/shard_map/all_gather | solution.py:126
  153.9 33.9 %all-gather.8.cloned.1.call-done = bf16[4096,1024]{1,0:T(8,128)(2,1)} async-done(((bf16[128,1024]{1,0:T(8,128)(2,1)}), bf16[4096,1024]{1,0:T(8,128)(2,1)}) %all-gather.8.cloned.1.call-update) | async-done | bytes 8388624 | tf_op jit(solution)/shard_map/all_gather | solution.py:76
  187.8 79.6 %all-gather.10.cloned.1.call-done = bf16[4096,1024]{1,0:T(8,128)(2,1)} async-done(((bf16[128,1024]{1,0:T(8,128)(2,1)}), bf16[4096,1024]{1,0:T(8,128)(2,1)}) %all-gather.10.cloned.1.call-update) | async-done | bytes 8388624 | tf_op jit(solution)/shard_map/all_gather | solution.py:77
  268.8 191.1 %while.19 = (s32[]{:T(128)}, f32[128,1024]{0,1:T(8,128)}, f32[32,1024]{1,0:T(8,128)S(1)}, s32[8]{0:T(128)}, s32[]{:T(128)}, /*index=5*/bf16[8,512,1024]{2,1,0:T(...) while((s32[]{:T(128)}, f32[128,1024]{0,1:T(8,128)}, ...), condition=%wide.region_7.8_spmd.clone, body=%wide.region_2.7_spmd.clone.sunk | while | flops 373743232 | bytes 17140276 | solution.py:97
  278.5 14.3 %conditional.6 = (f32[128,1024]{0,1:T(8,128)}) conditional(s32[]{:T(128)} %convert_element_type.124, f32[128,1024]{0,1:T(8,128)} %get-tuple-element.514, (s32[512]{0:T(512)S(1)}, s32[]{:T(128)}, bf16[128,1024]{1,0:T(8,128)(2,1)}, bf16[512,1024]{1,0:T(8,128)(2,1)S(1)}, s32[1,128]{1,0:T(1,128)}, /*index=5*/s32[512]{0:T(512)S(1)}, ...), branch_computations={%region_3.3_spmd, %region_4.4_spmd} | conditional | flops 299171968 | bytes 9838860 | solution.py:70
  282.9 8.0 %fusion.2 = f32[8,128,128]{1,2,0:T(8,128)S(1)} fusion(bf16[512,8,128]{0,2,1:T(8,128)(2,1)S(1)} %bitcast.188, f32[8]{0:T(128)} %get-tuple-element.313, f32[8]{0:T(128)} %get-tuple-element.291, f32[8]{0:T(128)} %get-tuple-element.292, f32[8]{0:T(128)} %get-tuple-element.293, f32[8]{0:T(128)} %get-tuple-element.294, f32[8]{0:T(128)} %get-tuple-element.295, ...), kind=kOutput, calls=%fused_computation.26 | convolution fusion | flops 297271296 | bytes 4522752 | tf_op jit(solution)/shard_map/while/body/eval_jaxpr/cond/branch_1_fun/hrk,khd->rhd/dot_general | solution.py:45
  298.3 3.4 conditional.7
  302.4 14.3 %conditional.6 = (f32[128,1024]{0,1:T(8,128)}) conditional(s32[]{:T(128)} %convert_element_type.124, f32[128,1024]{0,1:T(8,128)} %get-tuple-element.514, (s32[512]{0:T(512)S(1)}, s32[]{:T(128)}, bf16[128,1024]{1,0:T(8,128)(2,1)}, bf16[512,1024]{1,0:T(8,128)(2,1)S(1)}, s32[1,128]{1,0:T(1,128)}, /*index=5*/s32[512]{0:T(512)S(1)}, ...), branch_computations={%region_3.3_spmd, %region_4.4_spmd} | conditional | flops 299171968 | bytes 9838860 | solution.py:70
  306.8 7.9 %fusion.2 = f32[8,128,128]{1,2,0:T(8,128)S(1)} fusion(bf16[512,8,128]{0,2,1:T(8,128)(2,1)S(1)} %bitcast.188, f32[8]{0:T(128)} %get-tuple-element.313, f32[8]{0:T(128)} %get-tuple-element.291, f32[8]{0:T(128)} %get-tuple-element.292, f32[8]{0:T(128)} %get-tuple-element.293, f32[8]{0:T(128)} %get-tuple-element.294, f32[8]{0:T(128)} %get-tuple-element.295, ...), kind=kOutput, calls=%fused_computation.26 | convolution fusion | flops 297271296 | bytes 4522752 | tf_op jit(solution)/shard_map/while/body/eval_jaxpr/cond/branch_1_fun/hrk,khd->rhd/dot_general | solution.py:45
  322.2 3.4 conditional.7
  326.3 14.3 %conditional.6 = (f32[128,1024]{0,1:T(8,128)}) conditional(s32[]{:T(128)} %convert_element_type.124, f32[128,1024]{0,1:T(8,128)} %get-tuple-element.514, (s32[512]{0:T(512)S(1)}, s32[]{:T(128)}, bf16[128,1024]{1,0:T(8,128)(2,1)}, bf16[512,1024]{1,0:T(8,128)(2,1)S(1)}, s32[1,128]{1,0:T(1,128)}, /*index=5*/s32[512]{0:T(512)S(1)}, ...), branch_computations={%region_3.3_spmd, %region_4.4_spmd} | conditional | flops 299171968 | bytes 9838860 | solution.py:70
  330.7 7.9 %fusion.2 = f32[8,128,128]{1,2,0:T(8,128)S(1)} fusion(bf16[512,8,128]{0,2,1:T(8,128)(2,1)S(1)} %bitcast.188, f32[8]{0:T(128)} %get-tuple-element.313, f32[8]{0:T(128)} %get-tuple-element.291, f32[8]{0:T(128)} %get-tuple-element.292, f32[8]{0:T(128)} %get-tuple-element.293, f32[8]{0:T(128)} %get-tuple-element.294, f32[8]{0:T(128)} %get-tuple-element.295, ...), kind=kOutput, calls=%fused_computation.26 | convolution fusion | flops 297271296 | bytes 4522752 | tf_op jit(solution)/shard_map/while/body/eval_jaxpr/cond/branch_1_fun/hrk,khd->rhd/dot_general | solution.py:45
  350.1 14.3 %conditional.6 = (f32[128,1024]{0,1:T(8,128)}) conditional(s32[]{:T(128)} %convert_element_type.124, f32[128,1024]{0,1:T(8,128)} %get-tuple-element.514, (s32[512]{0:T(512)S(1)}, s32[]{:T(128)}, bf16[128,1024]{1,0:T(8,128)(2,1)}, bf16[512,1024]{1,0:T(8,128)(2,1)S(1)}, s32[1,128]{1,0:T(1,128)}, /*index=5*/s32[512]{0:T(512)S(1)}, ...), branch_computations={%region_3.3_spmd, %region_4.4_spmd} | conditional | flops 299171968 | bytes 9838860 | solution.py:70
  354.6 7.9 %fusion.2 = f32[8,128,128]{1,2,0:T(8,128)S(1)} fusion(bf16[512,8,128]{0,2,1:T(8,128)(2,1)S(1)} %bitcast.188, f32[8]{0:T(128)} %get-tuple-element.313, f32[8]{0:T(128)} %get-tuple-element.291, f32[8]{0:T(128)} %get-tuple-element.292, f32[8]{0:T(128)} %get-tuple-element.293, f32[8]{0:T(128)} %get-tuple-element.294, f32[8]{0:T(128)} %get-tuple-element.295, ...), kind=kOutput, calls=%fused_computation.26 | convolution fusion | flops 297271296 | bytes 4522752 | tf_op jit(solution)/shard_map/while/body/eval_jaxpr/cond/branch_1_fun/hrk,khd->rhd/dot_general | solution.py:45
  374.0 14.3 %conditional.6 = (f32[128,1024]{0,1:T(8,128)}) conditional(s32[]{:T(128)} %convert_element_type.124, f32[128,1024]{0,1:T(8,128)} %get-tuple-element.514, (s32[512]{0:T(512)S(1)}, s32[]{:T(128)}, bf16[128,1024]{1,0:T(8,128)(2,1)}, bf16[512,1024]{1,0:T(8,128)(2,1)S(1)}, s32[1,128]{1,0:T(1,128)}, /*index=5*/s32[512]{0:T(512)S(1)}, ...), branch_computations={%region_3.3_spmd, %region_4.4_spmd} | conditional | flops 299171968 | bytes 9838860 | solution.py:70
  378.5 7.9 %fusion.2 = f32[8,128,128]{1,2,0:T(8,128)S(1)} fusion(bf16[512,8,128]{0,2,1:T(8,128)(2,1)S(1)} %bitcast.188, f32[8]{0:T(128)} %get-tuple-element.313, f32[8]{0:T(128)} %get-tuple-element.291, f32[8]{0:T(128)} %get-tuple-element.292, f32[8]{0:T(128)} %get-tuple-element.293, f32[8]{0:T(128)} %get-tuple-element.294, f32[8]{0:T(128)} %get-tuple-element.295, ...), kind=kOutput, calls=%fused_computation.26 | convolution fusion | flops 297271296 | bytes 4522752 | tf_op jit(solution)/shard_map/while/body/eval_jaxpr/cond/branch_1_fun/hrk,khd->rhd/dot_general | solution.py:45
  397.9 14.3 %conditional.6 = (f32[128,1024]{0,1:T(8,128)}) conditional(s32[]{:T(128)} %convert_element_type.124, f32[128,1024]{0,1:T(8,128)} %get-tuple-element.514, (s32[512]{0:T(512)S(1)}, s32[]{:T(128)}, bf16[128,1024]{1,0:T(8,128)(2,1)}, bf16[512,1024]{1,0:T(8,128)(2,1)S(1)}, s32[1,128]{1,0:T(1,128)}, /*index=5*/s32[512]{0:T(512)S(1)}, ...), branch_computations={%region_3.3_spmd, %region_4.4_spmd} | conditional | flops 299171968 | bytes 9838860 | solution.py:70
  402.3 7.9 %fusion.2 = f32[8,128,128]{1,2,0:T(8,128)S(1)} fusion(bf16[512,8,128]{0,2,1:T(8,128)(2,1)S(1)} %bitcast.188, f32[8]{0:T(128)} %get-tuple-element.313, f32[8]{0:T(128)} %get-tuple-element.291, f32[8]{0:T(128)} %get-tuple-element.292, f32[8]{0:T(128)} %get-tuple-element.293, f32[8]{0:T(128)} %get-tuple-element.294, f32[8]{0:T(128)} %get-tuple-element.295, ...), kind=kOutput, calls=%fused_computation.26 | convolution fusion | flops 297271296 | bytes 4522752 | tf_op jit(solution)/shard_map/while/body/eval_jaxpr/cond/branch_1_fun/hrk,khd->rhd/dot_general | solution.py:45
  421.8 14.3 %conditional.6 = (f32[128,1024]{0,1:T(8,128)}) conditional(s32[]{:T(128)} %convert_element_type.124, f32[128,1024]{0,1:T(8,128)} %get-tuple-element.514, (s32[512]{0:T(512)S(1)}, s32[]{:T(128)}, bf16[128,1024]{1,0:T(8,128)(2,1)}, bf16[512,1024]{1,0:T(8,128)(2,1)S(1)}, s32[1,128]{1,0:T(1,128)}, /*index=5*/s32[512]{0:T(512)S(1)}, ...), branch_computations={%region_3.3_spmd, %region_4.4_spmd} | conditional | flops 299171968 | bytes 9838860 | solution.py:70
  426.2 7.9 %fusion.2 = f32[8,128,128]{1,2,0:T(8,128)S(1)} fusion(bf16[512,8,128]{0,2,1:T(8,128)(2,1)S(1)} %bitcast.188, f32[8]{0:T(128)} %get-tuple-element.313, f32[8]{0:T(128)} %get-tuple-element.291, f32[8]{0:T(128)} %get-tuple-element.292, f32[8]{0:T(128)} %get-tuple-element.293, f32[8]{0:T(128)} %get-tuple-element.294, f32[8]{0:T(128)} %get-tuple-element.295, ...), kind=kOutput, calls=%fused_computation.26 | convolution fusion | flops 297271296 | bytes 4522752 | tf_op jit(solution)/shard_map/while/body/eval_jaxpr/cond/branch_1_fun/hrk,khd->rhd/dot_general | solution.py:45
  445.7 14.3 %conditional.6 = (f32[128,1024]{0,1:T(8,128)}) conditional(s32[]{:T(128)} %convert_element_type.124, f32[128,1024]{0,1:T(8,128)} %get-tuple-element.514, (s32[512]{0:T(512)S(1)}, s32[]{:T(128)}, bf16[128,1024]{1,0:T(8,128)(2,1)}, bf16[512,1024]{1,0:T(8,128)(2,1)S(1)}, s32[1,128]{1,0:T(1,128)}, /*index=5*/s32[512]{0:T(512)S(1)}, ...), branch_computations={%region_3.3_spmd, %region_4.4_spmd} | conditional | flops 299171968 | bytes 9838860 | solution.py:70
  450.1 7.9 %fusion.2 = f32[8,128,128]{1,2,0:T(8,128)S(1)} fusion(bf16[512,8,128]{0,2,1:T(8,128)(2,1)S(1)} %bitcast.188, f32[8]{0:T(128)} %get-tuple-element.313, f32[8]{0:T(128)} %get-tuple-element.291, f32[8]{0:T(128)} %get-tuple-element.292, f32[8]{0:T(128)} %get-tuple-element.293, f32[8]{0:T(128)} %get-tuple-element.294, f32[8]{0:T(128)} %get-tuple-element.295, ...), kind=kOutput, calls=%fused_computation.26 | convolution fusion | flops 297271296 | bytes 4522752 | tf_op jit(solution)/shard_map/while/body/eval_jaxpr/cond/branch_1_fun/hrk,khd->rhd/dot_general | solution.py:45
  (189 shorter events, 147.1 us)
Async XLA Ops:
  7.2 97.0 %all-gather.6.cloned.1.call-start = ((), (), s32[]{:S(2)}) async-start(), calls=%async_computation | async-start | bytes 9437184 | tf_op jit(solution)/shard_map/all_gather | solution.py:115
  7.9 179.9 %all-gather.8.cloned.1.call-start = ((), (), s32[]{:S(2)}) async-start(), calls=%async_computation.1 | async-start | bytes 8650752 | tf_op jit(solution)/shard_map/all_gather | solution.py:76
  109.4 158.6 %copy-start = (bf16[160,4096]{1,0:T(8,128)(2,1)}, bf16[160,4096]{1,0:T(8,128)(2,1)S(1)}, u32[]{:S(2)}) copy-start(bf16[160,4096]{1,0:T(8,128)(2,1)S(1)} %multiply_convert_fusion) | copy-start | bytes 3932164
  109.4 2.3 copy-start.1
  110.4 157.1 %all-gather.10.cloned.1.call-start = ((), (), s32[]{:S(2)}) async-start(), calls=%async_computation.2 | async-start | bytes 8650752 | tf_op jit(solution)/shard_map/all_gather | solution.py:77
  111.1 352.1 %all-gather.12.cloned.1.call-start = ((), (), s32[]{:S(2)}) async-start(), calls=%async_computation.3 | async-start | bytes 2359296 | tf_op jit(solution)/shard_map/all_gather | solution.py:148
Sparse Core Ops, SparseCore 0:
  9.8 94.3 all-gather.5
  110.5 77.2 all-gather.7
  190.4 77.0 all-gather.9
  269.1 37.3 all-gather.11
where the time goes:
time: 476 us; the launch traced here: 473 us
  waiting for transfers between devices  209 us (44%)
  matrix products  90.7 us (19%)
  local copies, waits for them, and re-layouts  55.9 us (12%)
  other arithmetic  46.7 us (10%)
  blocking collectives  40.5 us (9%)
  loops' own time  16.2 us (3%)
  between operations  13.9 us (3%)
    all_gather x1, waiting for transfers between devices, body(): lax.all_gather(w_proj, 'batch', axis=1, tiled=True)  93.9 us
    dot_general x16, matrix products, attend(): jnp.einsum('hrk,khd->rhd', weights, value_heads, preferred_element_type=j...  83.2 us
    all_gather x1, waiting for transfers between devices, key_sweep(): piece_values = lax.all_gather(values, 'seq', axis=0, tiled=True)  79.6 us
    all_gather x1, blocking collectives, body(): all_times = lax.all_gather(hist_time, 'seq', axis=0, tiled=True)  40.5 us
    all_gather x1, waiting for transfers between devices, key_sweep(): piece_keys = lax.all_gather(keys, 'seq', axis=0, tiled=True)  33.9 us
    ge x16, other arithmetic, pair_bias(): time_mark = time_gap >= jnp.int32(4 ** level)  27.3 us
    add x16, other arithmetic, compute(): accum + attend(queries, keys, values, query_pos, query_time, key_pos, key...  15.5 us
    another operation x1, loops' own time, key_sweep(): lax.scan(tile_step, totals, (jnp.arange(tile_count, dtype=jnp.int32), til...  15.4 us
  transfers between devices with their start and end apart: 4, of which 3 were waited for; matrix products, arithmetic and copies ran while one was open for 39% of the time, Pallas kernels for 0%

commit v1 on v0

v1 whole, which is shorter than its diff:
```python
import functools

import jax
import jax.numpy as jnp
from jax import lax
from jax.experimental import pallas as pl
from jax.experimental.pallas import tpu as pltpu
from jax.sharding import PartitionSpec as P

F32, BF16, I32 = jnp.float32, jnp.bfloat16, jnp.int32
ZL, NY, NX, ZH, NC = 2, 4, 4, 4, 2
NB, NS = ZL * NY, NX * ZH * NC
OFF = (0, -1, 1, 2)
HEADS, HD, D = 8, 128, 1024
HIST, CAND = 128, 32
ROWS = HIST + CAND
NP = ZH * NC
QH, QC = NP * HIST, NP * CAND
QROWS = QH + QC
KEYS = NP * HIST
LENGTH = NS * HIST
LEVELS = 12
MASKED = -1e30
VM = pl.BlockSpec(memory_space=pltpu.VMEM)
SM = pl.BlockSpec(memory_space=pltpu.SMEM)


def params(mib):
    return pltpu.CompilerParams(vmem_limit_bytes=mib << 20)


def seq_perm(dx=0, dz=0, flip=False):
    pairs = []
    for s in range(NS):
        x, z, c = s // (ZH * NC), s // NC % ZH, s % NC
        t = ((x + dx) % NX * ZH + (z + dz) % ZH) * NC + (c ^ int(flip))
        pairs.append((s, t))
    return pairs


def shift(array, dx=0, dz=0, flip=False):
    return lax.ppermute(array, "seq", seq_perm(dx, dz, flip))


def source_perm(dzl=0, dy=0):
    pairs = []
    for b in range(NB):
        zl, y = b // NY, b % NY
        t = (zl + dzl) % ZL * NY + (y + dy) % NY
        for s in range(NS):
            if y % 2 == s // NC % ZH // 2:
                pairs.append((b * NS + s, t * NS + s))
    return pairs


def from_sources(array, dzl=0, dy=0):
    return lax.ppermute(array, ("batch", "seq"), source_perm(dzl, dy))


def norm_kernel(hist_ref, cand_ref, out_ref):
    for ref, first, count in ((hist_ref, 0, HIST), (cand_ref, HIST, CAND)):
        rows = ref[0].astype(F32)
        rows = rows - jnp.mean(rows, axis=-1, keepdims=True)
        spread = jnp.mean(rows * rows, axis=-1, keepdims=True)
        out_ref[first : first + count, :] = (rows * lax.rsqrt(spread + 1e-6)).astype(BF16)


def norm_rows(hist, cand):
    return pl.pallas_call(
        norm_kernel,
        out_shape=jax.ShapeDtypeStruct((ROWS, D), BF16),
        in_specs=[VM, VM],
        out_specs=VM,
        cost_estimate=pl.CostEstimate(flops=8 * ROWS * D, bytes_accessed=4 * ROWS * D, transcendentals=0),
        name="norm_rows",
    )(hist, cand)


def bias_kernel(gap_ref, flat_ref, value_ref, kpos_ref, later_ref, tq_ref, tk_ref, ttab_ref, ptab_ref, hist_ref, cand_ref, col_ref):
    m = pl.program_id(0)
    g = pl.program_id(1)

    @pl.when((m == 0) & (g == 0))
    def _():
        for i in range(QROWS // 128):
            col_ref[i * 128 : (i + 1) * 128, :] = jnp.transpose(jnp.broadcast_to(tq_ref[i : i + 1, :], (128, 128)))

    ttab = jnp.broadcast_to(ttab_ref[0:1, :], (128, 128))
    ptab = jnp.broadcast_to(ptab_ref[0:1, :], (128, 128))
    row = lax.broadcasted_iota(I32, (128, 128), 0)
    lane = lax.broadcasted_iota(I32, (128, 128), 1)

    def time_tile(first, j):
        gap = col_ref[pl.ds(first, 128), :] - tk_ref[0, j : j + 1, :]
        return jnp.take_along_axis(ttab, lax.clz(gap), axis=1)

    for i in range(QC // 128):
        for j in range(4):
            kpos = kpos_ref[m * NP + g * 4 + j]
            gap = (LENGTH - kpos) - lax.broadcasted_iota(I32, (8, 128), 1)
            place = jnp.take_along_axis(ptab[0:8], lax.clz(gap), axis=1)
            cand_ref[i * 128 : (i + 1) * 128, j * 128 : (j + 1) * 128] = time_tile(QH + i * 128, j) + place[0:1, :]

    @pl.when(later_ref[m] == 0)
    def _():
        def hist_block(i, carry):
            first = pl.multiple_of(i * 128, 128)
            at = (i * NX + m) * NP + g * 4
            for j in range(4):
                hist_ref[pl.ds(first, 128), j * 128 : (j + 1) * 128] = time_tile(first, j) + value_ref[at + j]
            for j in range(4):

                @pl.when(flat_ref[at + j] == 0)
                def _():
                    gap = gap_ref[at + j] + row - lane
                    place = jnp.take_along_axis(ptab, lax.clz(gap), axis=1)
                    tile = hist_ref[pl.ds(first, 128), j * 128 : (j + 1) * 128] + place
                    hist_ref[pl.ds(first, 128), j * 128 : (j + 1) * 128] = jnp.where(gap >= 0, tile, MASKED)

            return carry

        lax.fori_loop(0, NP, hist_block, 0)


def make_bias(gap, flat, value, kpos, later, tq, tk, ttab, ptab):
    return pl.pallas_call(
        bias_kernel,
        grid=(NX, 2),
        out_shape=[
            jax.ShapeDtypeStruct((NX, QH, KEYS), F32),
            jax.ShapeDtypeStruct((NX, QC, KEYS), F32),
        ],
        in_specs=[SM] * 5
        + [
            pl.BlockSpec((16, 128), lambda m, g: (0, 0)),
            pl.BlockSpec((1, 4, 128), lambda m, g: (m * 2 + g, 0, 0)),
            pl.BlockSpec((8, 128), lambda m, g: (0, 0)),
            pl.BlockSpec((8, 128), lambda m, g: (0, 0)),
        ],
        out_specs=[
            pl.BlockSpec((None, QH, 512), lambda m, g: (m, 0, g)),
            pl.BlockSpec((None, QC, 512), lambda m, g: (m, 0, g)),
        ],
        scratch_shapes=[pltpu.VMEM((QROWS, 128), I32)],
        compiler_params=params(32),
        cost_estimate=pl.CostEstimate(flops=20 * QROWS * LENGTH, bytes_accessed=4 * QROWS * LENGTH, transcendentals=0),
        name="make_bias",
    )(gap, flat, value, kpos, later, tq, tk, ttab, ptab)


def half_silu(half):
    return half + half * jnp.tanh(half)


def project_kernel(x_ref, n0, n1, n2, n3a, n3b, s0, s1, s2, s3a, s3b, w0, w1, w2, w3a, w3b, q_ref, kv_ref, own_ref, *rest):
    gates, (rows, weights) = rest[:NP], rest[NP:]
    for place, piece in enumerate(((n0,), (n1,), (n2,), (n3a, n3b), (s0,), (s1,), (s2,), (s3a, s3b))):
        if len(piece) == 1:
            rows[place * HIST : (place + 1) * HIST, :] = piece[0][:HIST, :]
            rows[QH + place * CAND : QH + (place + 1) * CAND, :] = piece[0][HIST:, :]
        else:
            half = ROWS // 2
            rows[place * HIST : place * HIST + half, :] = piece[0][...]
            rows[place * HIST + half : (place + 1) * HIST, :] = piece[1][: HIST - half, :]
            rows[QH + place * CAND : QH + (place + 1) * CAND, :] = piece[1][HIST - half :, :]
    depth = D // NX
    for m, part in enumerate((w0, w1, w2)):
        at = pl.multiple_of(x_ref[m] * depth, depth)
        for kind in range(4):
            weights[pl.ds(at, depth), kind * HD : (kind + 1) * HD] = part[kind]
    at = pl.multiple_of(x_ref[3] * depth, depth)
    for kind in range(4):
        weights[pl.ds(at, depth), kind * HD : (kind + 1) * HD] = (w3a, w3b)[kind // 2][kind % 2]
    mixed = jnp.dot(rows[...], weights[:, 2 * HD :], preferred_element_type=F32)
    mixed = half_silu(0.5 * mixed)
    queries, keys = mixed[:, :HD], mixed[:, HD:]
    q_ref[...] = (queries * (0.5 * HD**-0.5)).astype(BF16)
    kv_ref[:, :HD] = keys[:QH].astype(BF16)
    dots = jnp.sum(queries[QH:].astype(BF16).astype(F32) * keys[QH:].astype(BF16).astype(F32), axis=-1, keepdims=True)
    own = half_silu(dots * (0.5 * HD**-0.5)).astype(BF16).astype(F32)
    mixed = jnp.dot(rows[...], weights[:, : 2 * HD], preferred_element_type=F32)
    mixed = half_silu(0.5 * mixed).astype(BF16)
    kv_ref[:, HD:] = mixed[:QH, HD:]
    own_ref[...] = own * mixed[QH:, HD:].astype(F32)
    for place, gate in enumerate(gates):
        gate[:HIST, :] = mixed[place * HIST : (place + 1) * HIST, :HD]
        gate[HIST:, :] = mixed[QH + place * CAND : QH + (place + 1) * CAND, :HD]


def project(x_of, pieces, parts):
    return pl.pallas_call(
        project_kernel,
        out_shape=[
            jax.ShapeDtypeStruct((QROWS, HD), BF16),
            jax.ShapeDtypeStruct((KEYS, 2 * HD), BF16),
            jax.ShapeDtypeStruct((QC, HD), F32),
        ]
        + [jax.ShapeDtypeStruct((ROWS, HD), BF16)] * NP,
        in_specs=[SM] + [VM] * 15,
        out_specs=[VM] * (3 + NP),
        scratch_shapes=[pltpu.VMEM((QROWS, D), BF16), pltpu.VMEM((D, 4 * HD), BF16)],
        compiler_params=params(48),
        cost_estimate=pl.CostEstimate(flops=2 * QROWS * D * 4 * HD, bytes_accessed=6 << 20, transcendentals=QROWS * 4 * HD),
        name="project",
    )(x_of, *pieces, *parts)


def attend_kernel(flag_ref, q_ref, kv_ref, hist_ref, cand_ref, sums_in, sums_ref, *, fresh, block):
    g = pl.program_id(0)

    @pl.when(g == 0)
    def _():
        if fresh:
            sums_ref[:QH, :] = jnp.zeros((QH, HD), F32)
            sums_ref[QH:, :] = sums_in[...]
        else:
            sums_ref[...] = sums_in[...]

    def step(first, count, bias_ref):
        half = lax.dot_general(
            q_ref[first : first + count, :], kv_ref[:, :HD], (((1,), (1,)), ((), ())), preferred_element_type=F32
        )
        weights = half_silu(half + bias_ref[...]).astype(BF16)
        sums_ref[first : first + count, :] += jnp.dot(weights, kv_ref[:, HD:], preferred_element_type=F32)

    step(QH, QC, cand_ref)

    @pl.when(flag_ref[0] == 0)
    def _():
        step(0, QH, hist_ref)


def attend(flag, q, kv, hist_bias, cand_bias, sums, m, first, fresh):
    keys, block = kv.shape[0], 256
    return pl.pallas_call(
        functools.partial(attend_kernel, fresh=fresh, block=block),
        grid_spec=pltpu.PrefetchScalarGridSpec(
            num_scalar_prefetch=1,
            grid=(keys // block,),
            in_specs=[
                pl.BlockSpec((QROWS, HD), lambda g, flag: (0, 0)),
                pl.BlockSpec((block, 2 * HD), lambda g, flag: (g, 0)),
                pl.BlockSpec((None, QH, block), lambda g, flag: (m, 0, jnp.where(flag[0] == 0, first // block + g, 0))),
                pl.BlockSpec((None, QC, block), lambda g, flag: (m, 0, first // block + g)),
                pl.BlockSpec((QC if fresh else QROWS, HD), lambda g, flag: (0, 0)),
            ],
            out_specs=pl.BlockSpec((QROWS, HD), lambda g, flag: (0, 0)),
        ),
        out_shape=jax.ShapeDtypeStruct((QROWS, HD), F32),
        compiler_params=params(40),
        cost_estimate=pl.CostEstimate(
            flops=4 * QROWS * keys * HD, bytes_accessed=4 * QROWS * keys, transcendentals=QROWS * keys
        ),
        name="attend",
    )(flag, q, kv, hist_bias, cand_bias, sums)


def split_kernel(sums_ref, *outs):
    for place, out in enumerate(outs):
        out[:HIST, :] = sums_ref[place * HIST : (place + 1) * HIST, :].astype(BF16)
        out[HIST:, :] = sums_ref[QH + place * CAND : QH + (place + 1) * CAND, :].astype(BF16)


def split_sums(sums):
    return pl.pallas_call(
        split_kernel,
        out_shape=[jax.ShapeDtypeStruct((ROWS, HD), BF16)] * NP,
        in_specs=[VM],
        out_specs=[VM] * NP,
        cost_estimate=pl.CostEstimate(flops=QROWS * HD, bytes_accessed=6 * QROWS * HD, transcendentals=0),
        name="split_sums",
    )(sums)


def finish_kernel(z_ref, core_ref, hist_ref, cand_ref, w_ref, *rest):
    atts, gates, (hist_out, cand_out) = rest[:NP], rest[NP : 2 * NP], rest[2 * NP :]
    parts = [att[...].astype(F32) for att in atts]
    center = sum(jnp.sum(part, axis=-1, keepdims=True) for part in parts) * (1.0 / D)
    parts = [part - center for part in parts]
    spread = sum(jnp.sum(part * part, axis=-1, keepdims=True) for part in parts) * (1.0 / D)
    scale = lax.rsqrt(spread + 1e-6)
    parts = [(part * scale * gate[...].astype(F32)).astype(BF16) for part, gate in zip(parts, gates)]
    total = jnp.zeros((ROWS, D), F32)
    for r in range(ZH):
        mine, other = parts[r], parts[ZH + r]
        first = core_ref[0] == 0
        pair = jnp.concatenate([jnp.where(first, mine, other), jnp.where(first, other, mine)], axis=1)
        at = pl.multiple_of(z_ref[r] * (2 * HD), 2 * HD)
        total = total + jnp.dot(pair, w_ref[pl.ds(at, 2 * HD), :], preferred_element_type=F32)
    hist_out[0] = (hist_ref[0].astype(F32) + total[:HIST]).astype(BF16)
    cand_out[0] = (cand_ref[0].astype(F32) + total[HIST:]).astype(BF16)


def finish(z_from, core, hist, cand, w_out, atts, gates):
    return pl.pallas_call(
        finish_kernel,
        out_shape=[
            jax.ShapeDtypeStruct((1, HIST, D), BF16),
            jax.ShapeDtypeStruct((1, CAND, D), BF16),
        ],
        in_specs=[SM, SM] + [VM] * (3 + 2 * NP),
        out_specs=[VM, VM],
        compiler_params=params(32),
        cost_estimate=pl.CostEstimate(flops=2 * ROWS * D * D, bytes_accessed=4 << 20, transcendentals=0),
        name="finish",
    )(z_from, core, hist, cand, w_out, *atts, *gates)


def gather_weights(w_proj, x, z, core, batch):
    depth = D // NX
    z_lo, y = batch // NY, batch % NY
    head = NC * z + core
    mine = lax.dynamic_slice(w_proj, (x * depth, head % 4 * HD), (depth, HD))
    other = from_sources(mine, dzl=1)
    pair = jnp.stack([mine, other])
    up, down, across = from_sources(pair, dy=1), from_sources(pair, dy=-1), from_sources(pair, dy=2)
    is_source = y % 2 == z // 2
    halves = []
    for f in range(2):
        source = jnp.where(y // 2 == f, pair, across)
        sink = jnp.where((y - 1) % NY // 2 == f, up, down)
        halves.append(jnp.where(is_source, source, sink))
    low = [jnp.where(z_lo == 0, half[0], half[1]) for half in halves]
    high = [jnp.where(z_lo == 0, half[1], half[0]) for half in halves]
    return jnp.stack(low + high)


def body(history, candidates, event_times, request_times, w_proj, w_out, bias_steps):
    seq, batch = lax.axis_index("seq"), lax.axis_index("batch")
    x, z, core = seq // (ZH * NC), seq // NC % ZH, seq % NC
    head = NC * z + core
    zs = jnp.stack([(z + off) % ZH for off in OFF])
    back = jnp.stack([(z - off) % ZH for off in OFF])
    xs = jnp.stack([(x + off) % NX for off in OFF])

    n0 = norm_rows(history, candidates)
    n1, n2 = shift(n0, dz=1), shift(n0, dz=-1)
    half = ROWS // 2
    n3a, n3b = shift(n1[:half], dz=1), shift(n2[half:], dz=-1)
    own = [n0, n1, n2, n3a, n3b]
    pieces = own + [shift(piece, flip=True) for piece in own]

    w0 = gather_weights(w_proj, x, z, core, batch)
    w1, w2 = shift(w0, dx=1), shift(w0, dx=-1)
    w3a, w3b = shift(w1[:2], dx=1), shift(w2[2:], dx=-1)
    w_full = lax.all_gather(w_out, "batch", axis=0, tiled=True)

    t0 = jnp.concatenate([event_times, request_times], axis=1)
    t4 = jnp.concatenate([t0, shift(t0, dz=1), shift(t0, dz=-1), shift(t0, dz=2)], axis=0)
    t8 = jnp.concatenate([t4, shift(t4, flip=True)], axis=0)
    k0 = t8[:, :HIST]
    tk = jnp.stack([k0, shift(k0, dx=1), shift(k0, dx=-1), shift(k0, dx=2)])
    tq = jnp.concatenate([k0, t8[:, HIST:].reshape(QC // 128, 128), jnp.zeros((6, 128), I32)], axis=0)

    places = (zs[None, :] * NC + jnp.stack([core, 1 - core])[:, None]).reshape(NP)
    qpos = (x * NP + places) * HIST
    kpos = (xs[:, None] * NP + places[None, :]) * HIST
    gap = qpos[:, None, None] - kpos[None]
    steps = 0.5 * lax.dynamic_slice(bias_steps, (0, head), (2 * LEVELS, 1))[:, 0]
    bits = 32 - jnp.arange(128, dtype=I32)
    level = jnp.arange(LEVELS, dtype=I32)
    ttab = jnp.sum(jnp.where(bits[None, :] >= 2 * level[:, None] + 1, steps[:LEVELS, None], 0.0), axis=0)
    ptab = jnp.sum(jnp.where(bits[None, :] >= level[:, None] + 1, steps[LEVELS:, None], 0.0), axis=0)
    low, top = gap - (HIST - 1), gap + (HIST - 1)
    marks = 2**level
    flat = (low >= 1) & ~jnp.any((low[..., None] < marks) & (top[..., None] >= marks), axis=-1)
    value = jnp.sum(jnp.where(low[..., None] >= marks, steps[LEVELS:], 0.0), axis=-1)
    value = jnp.where(flat, value, 0.0)
    later = (xs > x).astype(I32)
    hist_bias, cand_bias = make_bias(
        gap.reshape(-1),
        flat.astype(I32).reshape(-1),
        value.reshape(-1),
        kpos.reshape(-1),
        later,
        tq,
        tk.reshape(NX * 2, 4, 128),
        jnp.broadcast_to(ttab, (8, 128)),
        jnp.broadcast_to(ptab, (8, 128)),
    )

    q, kv0, sums, *gates = project(xs, pieces, [w0, w1, w2, w3a, w3b])
    kv1, kv2 = shift(kv0, dx=1), shift(kv0, dx=-1)
    part = KEYS // 2
    kv3a, kv3b = shift(kv1[:part], dx=1), shift(kv2[part:], dx=-1)
    chunks = [(kv0, 0, 0), (kv1, 1, 0), (kv2, 2, 0), (kv3a, 3, 0), (kv3b, 3, part)]
    for kv, m, first in chunks:
        sums = attend(later[m : m + 1], q, kv, hist_bias, cand_bias, sums, m, first, m == 0)

    def send_back(arrays):
        out = []
        for place, array in enumerate(arrays):
            flip, r = place // ZH, place % ZH
            out.append(array if place == 0 else shift(array, dz=OFF[r], flip=bool(flip)))
        return out

    gates = send_back(gates)
    atts = send_back(split_sums(sums))
    return tuple(finish(back, core[None], history, candidates, w_full, atts, gates))


def solution(mesh):
    in_specs = (
        P("batch", "seq", None),
        P("batch", "seq", None),
        P("batch", "seq"),
        P("batch", "seq"),
        P(None, "batch"),
        P("batch", None),
        P(),
    )
    out_specs = (P("batch", "seq", None), P("batch", "seq", None))
    return jax.shard_map(body, mesh=mesh, in_specs=in_specs, out_specs=out_specs, check_vma=False)
```

time: 476 us -> 210 us (0.44)
  the two profiles are of different devices: /device:TPU:199 before, /device:TPU:30 now
where the time goes in v1:
time: 210 us; the launch traced here: 209 us
  Pallas kernels  64.8 us (31%)
  starting transfers between devices  59.4 us (28%)
  waiting for transfers between devices  53.5 us (25%)
  between operations  14.8 us (7%)
  local copies, waits for them, and re-layouts  14.4 us (7%)
  other arithmetic  2.51 us (1%)
    ppermute x38, starting transfers between devices, shift(): return lax.ppermute(array, 'seq', seq_perm(dx, dz, flip))  55.4 us
    ppermute x38, waiting for transfers between devices, shift(): return lax.ppermute(array, 'seq', seq_perm(dx, dz, flip))  45 us
    pallas_call x1, Pallas kernels, make_bias(): pl.pallas_call(bias_kernel, grid=(NX, 2), out_shape=[jax.ShapeDtypeStruct...  31 us
    pallas_call x5, Pallas kernels, attend(): pl.pallas_call(functools.partial(attend_kernel, fresh=fresh, block=block)...  25.3 us
    unnamed x15, local copies, waits for them, and re-layouts  10.6 us
    ppermute x4, waiting for transfers between devices, from_sources(): return lax.ppermute(array, ('batch', 'seq'), source_perm(dzl, dy))  8.51 us
  transfers between devices with their start and end apart: 43, of which 10 were waited for; matrix products, arithmetic and copies ran while one was open for 3% of the time, Pallas kernels for 30%

profile of v1, /device:TPU:30, one launch (start us, length us, event | category | flops | bytes accessed | tf_op | source)
XLA Modules:
  0.0 209.4 jit_solution(17226345636127898768)
XLA Ops:
  8.5 3.3 %collective-permute-start.19 = (s32[1,160]{1,0:T(1,128)S(1)}, s32[1,160]{1,0:T(1,128)S(1)}, u32[]{:S(2)}, u32[]{:S(2)}) collective-permute-start(s32[1,160]{1,0:T(1,128)S(1)} %constant_dynamic-update-slice_fusion), channel_id=1, source_target_pairs={{0,2},{1,3},{2,4},{3,5},{4,6},{5,7},{6,0},{7,1},{8,10},{9,11},{10,... | collective-permute-start | bytes 1928 | tf_op jit(solution)/shard_map/ppermute | solution.py:42
  11.8 3.0 %collective-permute-start.20 = (s32[1,160]{1,0:T(1,128)S(1)}, s32[1,160]{1,0:T(1,128)S(1)}, u32[]{:S(2)}, u32[]{:S(2)}) collective-permute-start(s32[1,160]{1,0:T(1,128)S(1)} %constant_dynamic-update-slice_fusion), channel_id=1, source_target_pairs={{0,6},{1,7},{2,0},{3,1},{4,2},{5,3},{6,4},{7,5},{8,14},{9,15},{10,... | collective-permute-start | bytes 1928 | tf_op jit(solution)/shard_map/ppermute | solution.py:42
  26.5 7.6 %collective-permute-done.11 = bf16[2,256,128]{2,1,0:T(8,128)(2,1)S(1)} collective-permute-done((bf16[2,256,128]{2,1,0:T(8,128)(2,1)S(1)}, bf16[2,256,128]{2,1,0:T(8,128)(2,1)S(1)}, u32[]{:S(2)}, u32[]{:S(2)}) %collective-permute-start.11) | collective-permute-done | bytes 131104 | tf_op jit(solution)/shard_map/ppermute | solution.py:57
  38.3 18.1 %collective-permute-done.n1 = bf16[160,1024]{1,0:T(8,128)(2,1)S(1)} collective-permute-done((bf16[160,1024]{1,0:T(8,128)(2,1)}, bf16[160,1024]{1,0:T(8,128)(2,1)S(1)}, u32[]{:S(2)}, u32[]{:S(2)}) %collective-permute-start) | collective-permute-done | bytes 327712 | tf_op jit(solution)/shard_map/ppermute | solution.py:42
  56.4 2.5 %collective-permute-start.21 = (s32[1,160]{1,0:T(1,128)S(1)}, s32[1,160]{1,0:T(1,128)S(1)}, u32[]{:S(2)}, u32[]{:S(2)}) collective-permute-start(s32[1,160]{1,0:T(1,128)S(1)} %constant_dynamic-update-slice_fusion), channel_id=1, source_target_pairs={{0,4},{1,5},{2,6},{3,7},{4,0},{5,1},{6,2},{7,3},{8,12},{9,13},{10,... | collective-permute-start | bytes 1928 | tf_op jit(solution)/shard_map/ppermute | solution.py:42
  59.9 3.2 %collective-permute-start.2 = (bf16[80,1024]{1,0:T(8,128)(2,1)S(1)}, bf16[80,1024]{1,0:T(8,128)(2,1)S(1)}, u32[]{:S(2)}, u32[]{:S(2)}) collective-permute-start(bf16[80,1024]{1,0:T(8,128)(2,1)S(1)} %slice.86), channel_id=1, source_target_pairs={{0,2},{1,3},{2,4},{3,5},{4,6},{5,7},{6,0},{7,1},{8,10},{9,11},{10,... | collective-permute-start | bytes 491528 | tf_op jit(solution)/shard_map/ppermute | solution.py:42
  68.9 6.1 %collective-permute-done.2.n3a = bf16[80,1024]{1,0:T(8,128)(2,1)S(1)} collective-permute-done((bf16[80,1024]{1,0:T(8,128)(2,1)S(1)}, bf16[80,1024]{1,0:T(8,128)(2,1)S(1)}, u32[]{:S(2)}, u32[]{:S(2)}) %collective-permute-start.2) | collective-permute-done | bytes 163872 | tf_op jit(solution)/shard_map/ppermute | solution.py:42
  76.2 5.3 %collective-permute-done.16.w3b = bf16[2,256,128]{2,1,0:T(8,128)(2,1)S(1)} collective-permute-done((bf16[2,256,128]{2,1,0:T(8,128)(2,1)S(1)}, bf16[2,256,128]{2,1,0:T(8,128)(2,1)S(1)}, u32[]{:S(2)}, u32[]{:S(2)}) %collective-permute-start.16) | collective-permute-done | bytes 131104 | tf_op jit(solution)/shard_map/ppermute | solution.py:42
  82.5 2.7 %project.1 = (bf16[1280,128]{1,0:T(8,128)(2,1)S(1)}, bf16[1024,256]{1,0:T(8,128)(2,1)S(1)}, f32[256,128]{1,0:T(8,128)S(1)}, bf16[160,128]{1,0:T(8,128)(2,1)S(1)}...) custom-call(s32[4]{0:T(128)S(1)} %get-tuple-element.47.x_ref, ...), custom_call_target="tpu_custom_call" | custom-call | flops 1342177280 | bytes 6291456 | tf_op jit(solution)/shard_map/project/pallas_call | solution.py:191
  92.2 7.5 %collective-permute-done.26.kv_ref = bf16[1024,256]{1,0:T(8,128)(2,1)S(1)} collective-permute-done((bf16[1024,256]{1,0:T(8,128)(2,1)S(1)}, bf16[1024,256]{1,0:T(8,128)(2,1)S(1)}, u32[]{:S(2)}, u32[]{:S(2)}) %collective-permute-start.26) | collective-permute-done | bytes 524320 | tf_op jit(solution)/shard_map/ppermute | solution.py:42
  102.1 31.0 %make_bias.1 = (f32[4,1024,1024]{2,1,0:T(8,128)S(1)}, f32[4,256,1024]{2,1,0:T(8,128)S(1)}) custom-call(s32[256]{0:T(256)S(1)} %sub.94.gap_ref, s32[256]{0:T(256)S(1)} %fusion.2.flat_ref, f32[256]{0:T(256)S(1)} %broadcast_select_fusion.4.value_ref, s32[32]{0:T(128)S(1)} %mul.122.kpos_ref, s32[4]{0:T(128)S(1)} %compare_convert_fusion.later_ref, ...), custom_call_target="tpu_custom_call" | custom-call | flops 104857600 | bytes 20971520 | tf_op jit(solution)/shard_map/make_bias/pallas_call | solution.py:126
  133.2 5.8 %copy-done = f32[4,1024,1024]{2,1,0:T(8,128)} copy-done((f32[4,1024,1024]{2,1,0:T(8,128)}, f32[4,1024,1024]{2,1,0:T(8,128)S(1)}, u32[]{:S(2)}) %copy-start) | copy-done | bytes 16777240
  141.8 3.1 %collective-permute-start.37 = (bf16[160,128]{1,0:T(8,128)(2,1)S(1)}, bf16[160,128]{1,0:T(8,128)(2,1)S(1)}, u32[]{:S(2)}, u32[]{:S(2)}) collective-permute-start(bf16[160,128]{1,0:T(8,128)(2,1)S(1)} %get-tuple-element.39), channel_id=1, source_target_pairs={{0,4},{1,5},{2,6},{3,7},{4,0},{5,1},{6,2},{7,3},{8,12},{9,13},{10,... | collective-permute-start | bytes 122888 | tf_op jit(solution)/shard_map/ppermute | solution.py:42
  144.9 5.9 %attend.5.sums_in = f32[1280,128]{1,0:T(8,128)S(1)} custom-call(s32[1]{0:T(128)} %get-tuple-element.59.flag_ref, bf16[1280,128]{1,0:T(8,128)(2,1)S(1)} %get-tuple-element.23.q_ref, bf16[1024,256]{1,0:T(8,128)(2,1)S(1)} %get-tuple-element.24.kv_ref, f32[4,1024,1024]{2,1,0:T(8,128)} %copy-done, f32[4,256,1024]{2,1,0:T(8,128)S(1)} %get-tuple-element.26.cand_ref, ...), custom_call_target="tpu_custom_call" | custom-call | flops 671088640 | bytes 5242880 | tf_op jit(solution)/shard_map/attend/pallas_call | solution.py:235
  150.8 5.9 %attend.6.sums_in = f32[1280,128]{1,0:T(8,128)S(1)} custom-call(s32[1]{0:T(128)} %get-tuple-element.60.flag_ref, bf16[1280,128]{1,0:T(8,128)(2,1)S(1)} %get-tuple-element.23.q_ref, bf16[1024,256]{1,0:T(8,128)(2,1)S(1)} %collective-permute-done.26.kv_ref, f32[4,1024,1024]{2,1,0:T(8,128)} %copy-done, f32[4,256,1024]{2,1,0:T(8,128)S(1)} %get-tuple-element.26.cand_ref, ...), custom_call_target="tpu_custom_call" | custom-call | flops 671088640 | bytes 5242880 | tf_op jit(solution)/shard_map/attend/pallas_call | solution.py:235
  156.7 5.9 %attend.7.sums_in = f32[1280,128]{1,0:T(8,128)S(1)} custom-call(s32[1]{0:T(128)} %get-tuple-element.61.flag_ref, bf16[1280,128]{1,0:T(8,128)(2,1)S(1)} %get-tuple-element.23.q_ref, bf16[1024,256]{1,0:T(8,128)(2,1)S(1)} %collective-permute-done.17.kv_ref, f32[4,1024,1024]{2,1,0:T(8,128)} %copy-done, f32[4,256,1024]{2,1,0:T(8,128)S(1)} %get-tuple-element.26.cand_ref, ...), custom_call_target="tpu_custom_call" | custom-call | flops 671088640 | bytes 5242880 | tf_op jit(solution)/shard_map/attend/pallas_call | solution.py:235
  162.7 3.8 %attend.8.sums_in = f32[1280,128]{1,0:T(8,128)S(1)} custom-call(s32[1]{0:T(128)} %get-tuple-element.62.flag_ref, bf16[1280,128]{1,0:T(8,128)(2,1)S(1)} %get-tuple-element.23.q_ref, bf16[512,256]{1,0:T(8,128)(2,1)S(1)} %collective-permute-done.27.kv_ref, f32[4,1024,1024]{2,1,0:T(8,128)} %copy-done, f32[4,256,1024]{2,1,0:T(8,128)S(1)} %get-tuple-element.26.cand_ref, ...), custom_call_target="tpu_custom_call" | custom-call | flops 335544320 | bytes 2621440 | tf_op jit(solution)/shard_map/attend/pallas_call | solution.py:235
  166.5 3.8 %attend.9.sums_ref = f32[1280,128]{1,0:T(8,128)S(1)} custom-call(s32[1]{0:T(128)} %get-tuple-element.62.flag_ref, bf16[1280,128]{1,0:T(8,128)(2,1)S(1)} %get-tuple-element.23.q_ref, bf16[512,256]{1,0:T(8,128)(2,1)S(1)} %collective-permute-done.18.kv_ref, f32[4,1024,1024]{2,1,0:T(8,128)} %copy-done, f32[4,256,1024]{2,1,0:T(8,128)S(1)} %get-tuple-element.26.cand_ref, ...), custom_call_target="tpu_custom_call" | custom-call | flops 335544320 | bytes 2621440 | tf_op jit(solution)/shard_map/attend/pallas_call | solution.py:235
  171.2 3.0 %collective-permute-start.39 = (bf16[160,128]{1,0:T(8,128)(2,1)S(1)}, bf16[160,128]{1,0:T(8,128)(2,1)S(1)}, u32[]{:S(2)}, u32[]{:S(2)}) collective-permute-start(bf16[160,128]{1,0:T(8,128)(2,1)S(1)} %get-tuple-element.41), channel_id=1, source_target_pairs={{0,7},{1,6},{2,1},{3,0},{4,3},{5,2},{6,5},{7,4},{8,15},{9,14},{10,... | collective-permute-start | bytes 122888 | tf_op jit(solution)/shard_map/ppermute | solution.py:42
  176.1 2.6 %collective-permute-start.41 = (bf16[160,128]{1,0:T(8,128)(2,1)S(1)}, bf16[160,128]{1,0:T(8,128)(2,1)S(1)}, u32[]{:S(2)}, u32[]{:S(2)}) collective-permute-start(bf16[160,128]{1,0:T(8,128)(2,1)S(1)} %get-tuple-element.43), channel_id=1, source_target_pairs={{0,5},{1,4},{2,7},{3,6},{4,1},{5,0},{6,3},{7,2},{8,13},{9,12},{10,... | collective-permute-start | bytes 122888 | tf_op jit(solution)/shard_map/ppermute | solution.py:42
  178.7 2.9 %collective-permute-start.28 = (bf16[160,128]{1,0:T(8,128)(2,1)}, bf16[160,128]{1,0:T(8,128)(2,1)S(1)}, u32[]{:S(2)}, u32[]{:S(2)}) collective-permute-start(bf16[160,128]{1,0:T(8,128)(2,1)} %get-tuple-element.29), channel_id=1, source_target_pairs={{0,6},{1,7},{2,0},{3,1},{4,2},{5,3},{6,4},{7,5},{8,14},{9,15},{10,... | collective-permute-start | bytes 122888 | tf_op jit(solution)/shard_map/ppermute | solution.py:42
  182.4 3.6 %collective-permute-start.30 = (bf16[160,128]{1,0:T(8,128)(2,1)}, bf16[160,128]{1,0:T(8,128)(2,1)S(1)}, u32[]{:S(2)}, u32[]{:S(2)}) collective-permute-start(bf16[160,128]{1,0:T(8,128)(2,1)} %get-tuple-element.31), channel_id=1, source_target_pairs={{0,4},{1,5},{2,6},{3,7},{4,0},{5,1},{6,2},{7,3},{8,12},{9,13},{10,... | collective-permute-start | bytes 122888 | tf_op jit(solution)/shard_map/ppermute | solution.py:42
  186.0 4.2 %collective-permute-start.32 = (bf16[160,128]{1,0:T(8,128)(2,1)}, bf16[160,128]{1,0:T(8,128)(2,1)S(1)}, u32[]{:S(2)}, u32[]{:S(2)}) collective-permute-start(bf16[160,128]{1,0:T(8,128)(2,1)} %get-tuple-element.33), channel_id=1, source_target_pairs={{0,7},{1,6},{2,1},{3,0},{4,3},{5,2},{6,5},{7,4},{8,15},{9,14},{10,... | collective-permute-start | bytes 122888 | tf_op jit(solution)/shard_map/ppermute | solution.py:42
  192.7 3.4 %collective-permute-done.33.rest_6_ = bf16[160,128]{1,0:T(8,128)(2,1)S(1)} collective-permute-done((bf16[160,128]{1,0:T(8,128)(2,1)}, bf16[160,128]{1,0:T(8,128)(2,1)S(1)}, u32[]{:S(2)}, u32[]{:S(2)}) %collective-permute-start.33) | collective-permute-done | bytes 40992 | tf_op jit(solution)/shard_map/ppermute | solution.py:42
  (138 shorter events, 50.7 us)
Async XLA Ops:
  7.2 190.9 %all-gather.2.cloned.1.call-start = ((), (), s32[]{:S(2)}) async-start(), calls=%async_computation | async-start | bytes 2359296 | tf_op jit(solution)/shard_map/all_gather | solution.py:346
  8.5 51.4 %collective-permute-start.19 = (s32[1,160]{1,0:T(1,128)S(1)}, s32[1,160]{1,0:T(1,128)S(1)}, u32[]{:S(2)}, u32[]{:S(2)}) collective-permute-start(s32[1,160]{1,0:T(1,128)S(1)} %constant_dynamic-update-slice_fusion), channel_id=1, source_target_pairs={{0,2},{1,3},{2,4},{3,5},{4,6},{5,7},{6,0},{7,1},{8,10},{9,11},{10,... | collective-permute-start | bytes 1928 | tf_op jit(solution)/shard_map/ppermute | solution.py:42
  11.8 51.3 %collective-permute-start.20 = (s32[1,160]{1,0:T(1,128)S(1)}, s32[1,160]{1,0:T(1,128)S(1)}, u32[]{:S(2)}, u32[]{:S(2)}) collective-permute-start(s32[1,160]{1,0:T(1,128)S(1)} %constant_dynamic-update-slice_fusion), channel_id=1, source_target_pairs={{0,6},{1,7},{2,0},{3,1},{4,2},{5,3},{6,4},{7,5},{8,14},{9,15},{10,... | collective-permute-start | bytes 1928 | tf_op jit(solution)/shard_map/ppermute | solution.py:42
  22.4 11.8 %collective-permute-start.11 = (bf16[2,256,128]{2,1,0:T(8,128)(2,1)S(1)}, bf16[2,256,128]{2,1,0:T(8,128)(2,1)S(1)}, u32[]{:S(2)}, u32[]{:S(2)}) collective-permute-start(bf16[2,256,128]{2,1,0:T(8,128)(2,1)S(1)} %pad_maximum_fusion.1), channel_id=1, source_target_pairs={{0,32},{1,33},{2,34},{3,35},{8,40},{9,41},{10,42},{11,43},{16,48},... | collective-permute-start | bytes 393224 | tf_op jit(solution)/shard_map/ppermute | solution.py:57
  23.7 13.7 %collective-permute-start.12 = (bf16[2,256,128]{2,1,0:T(8,128)(2,1)S(1)}, bf16[2,256,128]{2,1,0:T(8,128)(2,1)S(1)}, u32[]{:S(2)}, u32[]{:S(2)}) collective-permute-start(bf16[2,256,128]{2,1,0:T(8,128)(2,1)S(1)} %pad_maximum_fusion.1), channel_id=1, source_target_pairs={{0,96},{1,97},{2,98},{3,99},{8,104},{9,105},{10,106},{11,107},{16,... | collective-permute-start | bytes 393224 | tf_op jit(solution)/shard_map/ppermute | solution.py:57
  25.0 31.4 %collective-permute-start = (bf16[160,1024]{1,0:T(8,128)(2,1)}, bf16[160,1024]{1,0:T(8,128)(2,1)S(1)}, u32[]{:S(2)}, u32[]{:S(2)}) collective-permute-start(bf16[160,1024]{1,0:T(8,128)(2,1)} %norm_rows.1.n0), channel_id=1, source_target_pairs={{0,2},{1,3},{2,4},{3,5},{4,6},{5,7},{6,0},{7,1},{8,10},{9,11},{10,... | collective-permute-start | bytes 983048 | tf_op jit(solution)/shard_map/ppermute | solution.py:42
  34.1 24.8 %collective-permute-start.1 = (bf16[160,1024]{1,0:T(8,128)(2,1)}, bf16[160,1024]{1,0:T(8,128)(2,1)S(1)}, u32[]{:S(2)}, u32[]{:S(2)}) collective-permute-start(bf16[160,1024]{1,0:T(8,128)(2,1)} %norm_rows.1.n0), channel_id=1, source_target_pairs={{0,6},{1,7},{2,0},{3,1},{4,2},{5,3},{6,4},{7,5},{8,14},{9,15},{10,... | collective-permute-start | bytes 983048 | tf_op jit(solution)/shard_map/ppermute | solution.py:42
  37.5 21.5 %collective-permute-start.13 = (bf16[4,256,128]{2,1,0:T(8,128)(2,1)S(1)}, bf16[4,256,128]{2,1,0:T(8,128)(2,1)S(1)}, u32[]{:S(2)}, u32[]{:S(2)}) collective-permute-start(bf16[4,256,128]{2,1,0:T(8,128)(2,1)S(1)} %pad_maximum_fusion.w0), channel_id=1, source_target_pairs={{0,8},{1,9},{2,10},{3,11},{4,12},{5,13},{6,14},{7,15},{8,16},{9,17... | collective-permute-start | bytes 786440 | tf_op jit(solution)/shard_map/ppermute | solution.py:42
  59.9 15.0 %collective-permute-start.2 = (bf16[80,1024]{1,0:T(8,128)(2,1)S(1)}, bf16[80,1024]{1,0:T(8,128)(2,1)S(1)}, u32[]{:S(2)}, u32[]{:S(2)}) collective-permute-start(bf16[80,1024]{1,0:T(8,128)(2,1)S(1)} %slice.86), channel_id=1, source_target_pairs={{0,2},{1,3},{2,4},{3,5},{4,6},{5,7},{6,0},{7,1},{8,10},{9,11},{10,... | collective-permute-start | bytes 491528 | tf_op jit(solution)/shard_map/ppermute | solution.py:42
  63.1 12.5 %collective-permute-start.3 = (bf16[80,1024]{1,0:T(8,128)(2,1)S(1)}, bf16[80,1024]{1,0:T(8,128)(2,1)S(1)}, u32[]{:S(2)}, u32[]{:S(2)}) collective-permute-start(bf16[80,1024]{1,0:T(8,128)(2,1)S(1)} %slice.87), channel_id=1, source_target_pairs={{0,6},{1,7},{2,0},{3,1},{4,2},{5,3},{6,4},{7,5},{8,14},{9,15},{10,... | collective-permute-start | bytes 491528 | tf_op jit(solution)/shard_map/ppermute | solution.py:42
  64.1 11.5 %collective-permute-start.15 = (bf16[2,256,128]{2,1,0:T(8,128)(2,1)S(1)}, bf16[2,256,128]{2,1,0:T(8,128)(2,1)S(1)}, u32[]{:S(2)}, u32[]{:S(2)}) collective-permute-start(bf16[2,256,128]{2,1,0:T(8,128)(2,1)S(1)} %slice.92), channel_id=1, source_target_pairs={{0,8},{1,9},{2,10},{3,11},{4,12},{5,13},{6,14},{7,15},{8,16},{9,17... | collective-permute-start | bytes 393224 | tf_op jit(solution)/shard_map/ppermute | solution.py:42
  66.5 15.0 %collective-permute-start.5 = (bf16[160,1024]{1,0:T(8,128)(2,1)S(1)}, bf16[160,1024]{1,0:T(8,128)(2,1)S(1)}, u32[]{:S(2)}, u32[]{:S(2)}) collective-permute-start(bf16[160,1024]{1,0:T(8,128)(2,1)S(1)} %collective-permute-done.n1), channel_id=1, source_target_pairs={{0,1},{1,0},{2,3},{3,2},{4,5},{5,4},{6,7},{7,6},{8,9},{9,8},{10,11... | collective-permute-start | bytes 983048 | tf_op jit(solution)/shard_map/ppermute | solution.py:42
  68.9 12.7 %collective-permute-start.6 = (bf16[160,1024]{1,0:T(8,128)(2,1)S(1)}, bf16[160,1024]{1,0:T(8,128)(2,1)S(1)}, u32[]{:S(2)}, u32[]{:S(2)}) collective-permute-start(bf16[160,1024]{1,0:T(8,128)(2,1)S(1)} %collective-permute-done.1.n2), channel_id=1, source_target_pairs={{0,1},{1,0},{2,3},{3,2},{4,5},{5,4},{6,7},{7,6},{8,9},{9,8},{10,11... | collective-permute-start | bytes 983048 | tf_op jit(solution)/shard_map/ppermute | solution.py:42
  85.2 14.5 %collective-permute-start.26 = (bf16[1024,256]{1,0:T(8,128)(2,1)S(1)}, bf16[1024,256]{1,0:T(8,128)(2,1)S(1)}, u32[]{:S(2)}, u32[]{:S(2)}) collective-permute-start(bf16[1024,256]{1,0:T(8,128)(2,1)S(1)} %get-tuple-element.24.kv_ref), channel_id=1, source_target_pairs={{0,8},{1,9},{2,10},{3,11},{4,12},{5,13},{6,14},{7,15},{8,16},{9,17... | collective-permute-start | bytes 1572872 | tf_op jit(solution)/shard_map/ppermute | solution.py:42
  86.3 15.7 %collective-permute-start.17 = (bf16[1024,256]{1,0:T(8,128)(2,1)S(1)}, bf16[1024,256]{1,0:T(8,128)(2,1)S(1)}, u32[]{:S(2)}, u32[]{:S(2)}) collective-permute-start(bf16[1024,256]{1,0:T(8,128)(2,1)S(1)} %get-tuple-element.24.kv_ref), channel_id=1, source_target_pairs={{0,24},{1,25},{2,26},{3,27},{4,28},{5,29},{6,30},{7,31},{8,0},{9,1... | collective-permute-start | bytes 1572872 | tf_op jit(solution)/shard_map/ppermute | solution.py:42
  88.2 13.9 %collective-permute-start.23 = (s32[8,128]{1,0:T(8,128)S(1)}, s32[8,128]{1,0:T(8,128)S(1)}, u32[]{:S(2)}, u32[]{:S(2)}) collective-permute-start(s32[8,128]{1,0:T(8,128)S(1)} %get-tuple-element.55), channel_id=1, source_target_pairs={{0,8},{1,9},{2,10},{3,11},{4,12},{5,13},{6,14},{7,15},{8,16},{9,17... | collective-permute-start | bytes 12296 | tf_op jit(solution)/shard_map/ppermute | solution.py:42
  90.5 11.6 %collective-permute-start.24 = (s32[8,128]{1,0:T(8,128)S(1)}, s32[8,128]{1,0:T(8,128)S(1)}, u32[]{:S(2)}, u32[]{:S(2)}) collective-permute-start(s32[8,128]{1,0:T(8,128)S(1)} %get-tuple-element.55), channel_id=1, source_target_pairs={{0,24},{1,25},{2,26},{3,27},{4,28},{5,29},{6,30},{7,31},{8,0},{9,1... | collective-permute-start | bytes 12296 | tf_op jit(solution)/shard_map/ppermute | solution.py:42
  90.5 11.6 %collective-permute-start.25 = (s32[8,128]{1,0:T(8,128)S(1)}, s32[8,128]{1,0:T(8,128)S(1)}, u32[]{:S(2)}, u32[]{:S(2)}) collective-permute-start(s32[8,128]{1,0:T(8,128)S(1)} %get-tuple-element.55), channel_id=1, source_target_pairs={{0,16},{1,17},{2,18},{3,19},{4,20},{5,21},{6,22},{7,23},{8,24},{9,... | collective-permute-start | bytes 12296 | tf_op jit(solution)/shard_map/ppermute | solution.py:42
  99.7 62.9 %collective-permute-start.27 = (bf16[512,256]{1,0:T(8,128)(2,1)S(1)}, bf16[512,256]{1,0:T(8,128)(2,1)S(1)}, u32[]{:S(2)}, u32[]{:S(2)}) collective-permute-start(bf16[512,256]{1,0:T(8,128)(2,1)S(1)} %slice.97), channel_id=1, source_target_pairs={{0,8},{1,9},{2,10},{3,11},{4,12},{5,13},{6,14},{7,15},{8,16},{9,17... | collective-permute-start | bytes 786440 | tf_op jit(solution)/shard_map/ppermute | solution.py:42
  102.0 64.5 %collective-permute-start.18 = (bf16[512,256]{1,0:T(8,128)(2,1)S(1)}, bf16[512,256]{1,0:T(8,128)(2,1)S(1)}, u32[]{:S(2)}, u32[]{:S(2)}) collective-permute-start(bf16[512,256]{1,0:T(8,128)(2,1)S(1)} %slice.94), channel_id=1, source_target_pairs={{0,24},{1,25},{2,26},{3,27},{4,28},{5,29},{6,30},{7,31},{8,0},{9,1... | collective-permute-start | bytes 786440 | tf_op jit(solution)/shard_map/ppermute | solution.py:42
  138.9 37.1 %collective-permute-start.35 = (bf16[160,128]{1,0:T(8,128)(2,1)S(1)}, bf16[160,128]{1,0:T(8,128)(2,1)S(1)}, u32[]{:S(2)}, u32[]{:S(2)}) collective-permute-start(bf16[160,128]{1,0:T(8,128)(2,1)S(1)} %get-tuple-element.37), channel_id=1, source_target_pairs={{0,6},{1,7},{2,0},{3,1},{4,2},{5,3},{6,4},{7,5},{8,14},{9,15},{10,... | collective-permute-start | bytes 122888 | tf_op jit(solution)/shard_map/ppermute | solution.py:42
  139.4 36.7 %collective-permute-start.36 = (bf16[160,128]{1,0:T(8,128)(2,1)S(1)}, bf16[160,128]{1,0:T(8,128)(2,1)S(1)}, u32[]{:S(2)}, u32[]{:S(2)}) collective-permute-start(bf16[160,128]{1,0:T(8,128)(2,1)S(1)} %get-tuple-element.38), channel_id=1, source_target_pairs={{0,2},{1,3},{2,4},{3,5},{4,6},{5,7},{6,0},{7,1},{8,10},{9,11},{10,... | collective-permute-start | bytes 122888 | tf_op jit(solution)/shard_map/ppermute | solution.py:42
  141.8 36.9 %collective-permute-start.37 = (bf16[160,128]{1,0:T(8,128)(2,1)S(1)}, bf16[160,128]{1,0:T(8,128)(2,1)S(1)}, u32[]{:S(2)}, u32[]{:S(2)}) collective-permute-start(bf16[160,128]{1,0:T(8,128)(2,1)S(1)} %get-tuple-element.39), channel_id=1, source_target_pairs={{0,4},{1,5},{2,6},{3,7},{4,0},{5,1},{6,2},{7,3},{8,12},{9,13},{10,... | collective-permute-start | bytes 122888 | tf_op jit(solution)/shard_map/ppermute | solution.py:42
  162.6 19.0 %collective-permute-start.38 = (bf16[160,128]{1,0:T(8,128)(2,1)S(1)}, bf16[160,128]{1,0:T(8,128)(2,1)S(1)}, u32[]{:S(2)}, u32[]{:S(2)}) collective-permute-start(bf16[160,128]{1,0:T(8,128)(2,1)S(1)} %get-tuple-element.40), channel_id=1, source_target_pairs={{0,1},{1,0},{2,3},{3,2},{4,5},{5,4},{6,7},{7,6},{8,9},{9,8},{10,11... | collective-permute-start | bytes 122888 | tf_op jit(solution)/shard_map/ppermute | solution.py:42
  (26 other events, 220.5 us)
Sparse Core Ops, SparseCore 0:
  16.5 60.3 all-gather.1

commit v2 on v1

v2 whole, which is shorter than its diff:
```python
import functools

import jax
import jax.numpy as jnp
from jax import lax
from jax.experimental import pallas as pl
from jax.experimental.pallas import tpu as pltpu
from jax.sharding import PartitionSpec as P

F32, BF16, I32 = jnp.float32, jnp.bfloat16, jnp.int32
ZL, NY, NX, ZH, NC = 2, 4, 4, 4, 2
NB, NS = ZL * NY, NX * ZH * NC
OFF = (0, -1, 1, 2)
HEADS, HD, D = 8, 128, 1024
HIST, CAND = 128, 32
ROWS = HIST + CAND
NP = ZH * NC
QH, QC = NP * HIST, NP * CAND
QROWS = QH + QC
KEYS = NP * HIST
LENGTH = NS * HIST
LEVELS = 12
MASKED = -1e30
SAME_X = [[x * NP + p for p in range(NP)] for x in range(NX)]
VM = pl.BlockSpec(memory_space=pltpu.VMEM)
SM = pl.BlockSpec(memory_space=pltpu.SMEM)


def params(mib):
    return pltpu.CompilerParams(vmem_limit_bytes=mib << 20)


def seq_perm(dx=0, dz=0, flip=False):
    pairs = []
    for s in range(NS):
        x, z, c = s // (ZH * NC), s // NC % ZH, s % NC
        t = ((x + dx) % NX * ZH + (z + dz) % ZH) * NC + (c ^ int(flip))
        pairs.append((s, t))
    return pairs


def shift(array, dx=0, dz=0, flip=False):
    return lax.ppermute(array, "seq", seq_perm(dx, dz, flip))


def source_perm(dzl=0, dy=0):
    pairs = []
    for b in range(NB):
        zl, y = b // NY, b % NY
        t = (zl + dzl) % ZL * NY + (y + dy) % NY
        for s in range(NS):
            if y % 2 == s // NC % ZH // 2:
                pairs.append((b * NS + s, t * NS + s))
    return pairs


def from_sources(array, dzl=0, dy=0):
    return lax.ppermute(array, ("batch", "seq"), source_perm(dzl, dy))


def norm_kernel(hist_ref, cand_ref, out_ref):
    for ref, first, count in ((hist_ref, 0, HIST), (cand_ref, HIST, CAND)):
        rows = ref[0].astype(F32)
        rows = rows - jnp.mean(rows, axis=-1, keepdims=True)
        spread = jnp.mean(rows * rows, axis=-1, keepdims=True)
        out_ref[first : first + count, :] = (rows * lax.rsqrt(spread + 1e-6)).astype(BF16)


def norm_rows(hist, cand):
    return pl.pallas_call(
        norm_kernel,
        out_shape=jax.ShapeDtypeStruct((ROWS, D), BF16),
        in_specs=[VM, VM],
        out_specs=VM,
        cost_estimate=pl.CostEstimate(flops=8 * ROWS * D, bytes_accessed=4 * ROWS * D, transcendentals=0),
        name="norm_rows",
    )(hist, cand)


def bias_kernel(kpos_ref, flat_ref, value_ref, later_ref, tq_ref, tk_ref, ttab_ref, ptab_ref, out_ref, col_ref, *, fresh):
    for i in range(QROWS // 128):
        col_ref[i * 128 : (i + 1) * 128, :] = jnp.transpose(jnp.broadcast_to(tq_ref[i : i + 1, :], (128, 128)))
    ttab = jnp.broadcast_to(ttab_ref[0:1, :], (128, 128))
    ptab = jnp.broadcast_to(ptab_ref[0:1, :], (128, 128))
    row = lax.broadcasted_iota(I32, (128, 128), 0)
    lane = lax.broadcasted_iota(I32, (128, 128), 1)

    def time_tile(first, j):
        gap = col_ref[pl.ds(first, 128), :] - tk_ref[j : j + 1, :]
        return jnp.take_along_axis(ttab, lax.clz(gap), axis=1)

    for i in range(QC // 128):
        for j in range(NP):
            gap = (LENGTH - kpos_ref[0] - j * HIST) - lax.broadcasted_iota(I32, (8, 128), 1)
            place = jnp.take_along_axis(ptab[0:8], lax.clz(gap), axis=1)
            out_ref[QH + i * 128 : QH + (i + 1) * 128, j * 128 : (j + 1) * 128] = time_tile(QH + i * 128, j) + place[0:1, :]

    @pl.when(later_ref[0] == 0)
    def _():
        def hist_block(i, carry):
            first = pl.multiple_of(i * 128, 128)
            for j in range(NP):
                at = kpos_ref[1] + i - j + NP - 1
                out_ref[pl.ds(first, 128), j * 128 : (j + 1) * 128] = time_tile(first, j) + value_ref[at]
            for j in range(NP):
                at = kpos_ref[1] + i - j + NP - 1

                @pl.when(flat_ref[at] == 0)
                def _():
                    gap = (at - (NP - 1)) * HIST + row - lane
                    place = jnp.take_along_axis(ptab, lax.clz(gap), axis=1)
                    tile = out_ref[pl.ds(first, 128), j * 128 : (j + 1) * 128] + place
                    out_ref[pl.ds(first, 128), j * 128 : (j + 1) * 128] = jnp.where(gap >= 0, tile, MASKED)

            return carry

        lax.fori_loop(0, NP, hist_block, 0)


def make_bias(kpos, flat, value, later, tq, tk, ttab, ptab):
    return pl.pallas_call(
        functools.partial(bias_kernel, fresh=True),
        out_shape=jax.ShapeDtypeStruct((QROWS, KEYS), F32),
        in_specs=[SM] * 4 + [VM] * 4,
        out_specs=VM,
        scratch_shapes=[pltpu.VMEM((QROWS, 128), I32)],
        compiler_params=params(20),
        cost_estimate=pl.CostEstimate(flops=2000 * QROWS * KEYS, bytes_accessed=4 * QROWS * KEYS, transcendentals=0),
        name="make_bias",
    )(kpos, flat, value, later, tq, tk, ttab, ptab)


def half_silu(half):
    return half + half * jnp.tanh(half)


def project_kernel(x_ref, tie_ref, rows_ref, wout_ref, w0, w1, w2, w3a, w3b, q_ref, kv_ref, own_ref, gate_ref, wout_out, rows, weights):
    for place in range(NP):
        rows[place * HIST : (place + 1) * HIST, :] = rows_ref[place, :HIST, :]
        rows[QH + place * CAND : QH + (place + 1) * CAND, :] = rows_ref[place, HIST:, :]
    wout_out[...] = wout_ref[...]
    depth = D // NX
    for m, part in enumerate((w0, w1, w2)):
        at = pl.multiple_of(x_ref[m] * depth, depth)
        for kind in range(4):
            weights[pl.ds(at, depth), kind * HD : (kind + 1) * HD] = part[kind]
    at = pl.multiple_of(x_ref[3] * depth, depth)
    for kind in range(4):
        weights[pl.ds(at, depth), kind * HD : (kind + 1) * HD] = (w3a, w3b)[kind // 2][kind % 2]
    mixed = jnp.dot(rows[...], weights[:, 2 * HD :], preferred_element_type=F32)
    mixed = half_silu(0.5 * mixed)
    queries, keys = mixed[:, :HD], mixed[:, HD:]
    q_ref[...] = (queries * (0.5 * HD**-0.5)).astype(BF16)
    kv_ref[:, :HD] = keys[:QH].astype(BF16)
    dots = jnp.sum(queries[QH:].astype(BF16).astype(F32) * keys[QH:].astype(BF16).astype(F32), axis=-1, keepdims=True)
    own = half_silu(dots * (0.5 * HD**-0.5)).astype(BF16).astype(F32)
    mixed = jnp.dot(rows[...], weights[:, : 2 * HD], preferred_element_type=F32)
    mixed = half_silu(0.5 * mixed).astype(BF16)
    kv_ref[:, HD:] = mixed[:QH, HD:]
    own_ref[...] = own * mixed[QH:, HD:].astype(F32)
    for place in range(NP):
        gate_ref[place, :HIST, :] = mixed[place * HIST : (place + 1) * HIST, :HD]
        gate_ref[place, HIST:, :] = mixed[QH + place * CAND : QH + (place + 1) * CAND, :HD]


def project(x_of, tie, rows, w_out, parts):
    return pl.pallas_call(
        project_kernel,
        out_shape=[
            jax.ShapeDtypeStruct((QROWS, HD), BF16),
            jax.ShapeDtypeStruct((KEYS, 2 * HD), BF16),
            jax.ShapeDtypeStruct((QC, HD), F32),
            jax.ShapeDtypeStruct((NP, ROWS, HD), BF16),
            jax.ShapeDtypeStruct(w_out.shape, BF16),
        ],
        in_specs=[SM, pl.BlockSpec(memory_space=pl.ANY)] + [VM] * 7,
        out_specs=[VM] * 5,
        scratch_shapes=[pltpu.VMEM((QROWS, D), BF16), pltpu.VMEM((D, 4 * HD), BF16)],
        compiler_params=params(32),
        cost_estimate=pl.CostEstimate(flops=2 * QROWS * D * 4 * HD, bytes_accessed=6 << 20, transcendentals=QROWS * 4 * HD),
        name="project",
    )(x_of, tie, rows, w_out, *parts)


def attend_kernel(flag_ref, tie_ref, q_ref, sums_in, *rest, fresh, last, counts):
    kvs, biases, (out_ref, sums_ref) = rest[: len(counts)], rest[len(counts) : -2], rest[-2:]
    if fresh:
        sums_ref[:QH, :] = jnp.zeros((QH, HD), F32)
        sums_ref[QH:, :] = sums_in[...]
    else:
        sums_ref[...] = sums_in[...]

    def step(n, first, count):
        bias_ref, begin = biases[counts[n][1]], counts[n][2]
        for piece in range(0, count, 256):
            at = first + piece
            half = lax.dot_general(
                q_ref[at : at + 256, :], kvs[n][:, :HD], (((1,), (1,)), ((), ())), preferred_element_type=F32
            )
            weights = half_silu(half + bias_ref[at : at + 256, begin : begin + counts[n][0]]).astype(BF16)
            sums_ref[at : at + 256, :] += jnp.dot(weights, kvs[n][:, HD:], preferred_element_type=F32)

    for n in range(len(counts)):
        step(n, QH, QC)

        @pl.when(flag_ref[counts[n][1]] == 0)
        def _():
            step(n, 0, QH)

    if last:
        for place in range(NP):
            out_ref[place, :HIST, :] = sums_ref[place * HIST : (place + 1) * HIST, :].astype(BF16)
            out_ref[place, HIST:, :] = sums_ref[QH + place * CAND : QH + (place + 1) * CAND, :].astype(BF16)
    else:
        out_ref[...] = sums_ref[...]


def attend(flags, tie, q, sums, kvs, biases, counts, fresh=False, last=False):
    keys = sum(count[0] for count in counts)
    return pl.pallas_call(
        functools.partial(attend_kernel, fresh=fresh, last=last, counts=counts),
        in_specs=[SM, pl.BlockSpec(memory_space=pl.ANY)] + [VM] * (2 + len(kvs) + len(biases)),
        out_specs=VM,
        out_shape=jax.ShapeDtypeStruct((NP, ROWS, HD), BF16) if last else jax.ShapeDtypeStruct((QROWS, HD), F32),
        scratch_shapes=[pltpu.VMEM((QROWS, HD), F32)],
        compiler_params=params(24),
        cost_estimate=pl.CostEstimate(
            flops=8 * QROWS * keys * HD, bytes_accessed=4 * QROWS * keys, transcendentals=QROWS * keys
        ),
        name="attend",
    )(flags, tie, q, sums, *kvs, *biases)


def finish_kernel(hist_ref, cand_ref, w_ref, att_ref, gate_ref, hist_out, cand_out):
    parts = [att_ref[h].astype(F32) for h in range(HEADS)]
    center = sum(jnp.sum(part, axis=-1, keepdims=True) for part in parts) * (1.0 / D)
    parts = [part - center for part in parts]
    spread = sum(jnp.sum(part * part, axis=-1, keepdims=True) for part in parts) * (1.0 / D)
    scale = lax.rsqrt(spread + 1e-6)
    parts = [(part * scale * gate_ref[h].astype(F32)).astype(BF16) for h, part in enumerate(parts)]
    total = jnp.dot(jnp.concatenate(parts, axis=1), w_ref[...], preferred_element_type=F32)
    hist_out[0] = (hist_ref[0].astype(F32) + total[:HIST]).astype(BF16)
    cand_out[0] = (cand_ref[0].astype(F32) + total[HIST:]).astype(BF16)


def finish(hist, cand, w_out, att, gate):
    return pl.pallas_call(
        finish_kernel,
        out_shape=[
            jax.ShapeDtypeStruct((1, HIST, D), BF16),
            jax.ShapeDtypeStruct((1, CAND, D), BF16),
        ],
        in_specs=[VM] * 5,
        out_specs=[VM, VM],
        compiler_params=params(24),
        cost_estimate=pl.CostEstimate(flops=2 * ROWS * D * D, bytes_accessed=4 << 20, transcendentals=0),
        name="finish",
    )(hist, cand, w_out, att, gate)


def gather_weights(w_proj, x, z, core, batch):
    depth = D // NX
    z_lo, y = batch // NY, batch % NY
    head = NC * z + core
    mine = lax.dynamic_slice(w_proj, (x * depth, head % 4 * HD), (depth, HD))
    other = from_sources(mine, dzl=1)
    pair = jnp.stack([mine, other])
    up, down, across = from_sources(pair, dy=1), from_sources(pair, dy=-1), from_sources(pair, dy=2)
    is_source = y % 2 == z // 2
    halves = []
    for f in range(2):
        source = jnp.where(y // 2 == f, pair, across)
        sink = jnp.where((y - 1) % NY // 2 == f, up, down)
        halves.append(jnp.where(is_source, source, sink))
    low = [jnp.where(z_lo == 0, half[0], half[1]) for half in halves]
    high = [jnp.where(z_lo == 0, half[1], half[0]) for half in halves]
    return jnp.stack(low + high)


def body(history, candidates, event_times, request_times, w_proj, w_out, bias_steps):
    seq, batch = lax.axis_index("seq"), lax.axis_index("batch")
    x, z, core = seq // (ZH * NC), seq // NC % ZH, seq % NC
    head = NC * z + core
    zs = [(z + off) % ZH for off in OFF]
    xs = jnp.stack([(x + off) % NX for off in OFF])

    rows = lax.all_gather(norm_rows(history, candidates), "seq", axis_index_groups=SAME_X)

    t0 = jnp.concatenate([event_times, request_times], axis=1)
    near = [t0, shift(t0, dz=1), shift(t0, dz=-1), shift(t0, dz=2)]
    t4 = jnp.concatenate([sum(jnp.where(zs[r] == j, near[r], 0) for r in range(ZH)) for j in range(ZH)], axis=0)
    other = shift(t4, flip=True)
    t8 = jnp.stack([jnp.where(core == 0, t4, other), jnp.where(core == 0, other, t4)], axis=1).reshape(NP, ROWS)
    k0 = t8[:, :HIST]
    tk = [k0, shift(k0, dx=1), shift(k0, dx=-1), shift(k0, dx=2)]
    tq = jnp.concatenate([k0, t8[:, HIST:].reshape(QC // 128, 128), jnp.zeros((6, 128), I32)], axis=0)

    w0 = gather_weights(w_proj, x, z, core, batch)
    w1, w2 = shift(w0, dx=1), shift(w0, dx=-1)
    w3a, w3b = shift(w1[:2], dx=1), shift(w2[2:], dx=-1)

    steps = 0.5 * lax.dynamic_slice(bias_steps, (0, head), (2 * LEVELS, 1))[:, 0]
    bits = 32 - jnp.arange(128, dtype=I32)
    level = jnp.arange(LEVELS, dtype=I32)
    ttab = jnp.sum(jnp.where(bits[None, :] >= 2 * level[:, None] + 1, steps[:LEVELS, None], 0.0), axis=0)
    ptab = jnp.sum(jnp.where(bits[None, :] >= level[:, None] + 1, steps[LEVELS:, None], 0.0), axis=0)
    ttab, ptab = jnp.broadcast_to(ttab, (8, 128)), jnp.broadcast_to(ptab, (8, 128))
    gap = (jnp.arange(NS + NP, dtype=I32) - (NP - 1)) * HIST
    low, top = gap - (HIST - 1), gap + (HIST - 1)
    marks = 2**level
    flat = (low >= 1) & ~jnp.any((low[:, None] < marks) & (top[:, None] >= marks), axis=-1)
    value = jnp.sum(jnp.where(low[:, None] >= marks, steps[LEVELS:], 0.0), axis=-1)
    value = jnp.where(flat, value, 0.0)
    later = (xs > x).astype(I32)
    biases = [
        make_bias(
            jnp.stack([xs[m] * KEYS, (x - xs[m]) * NP]), flat.astype(I32), value, later[m : m + 1], tq, tk[m], ttab, ptab
        )
        for m in range(NX)
    ]

    q, kv0, own, gate, w_mine = project(xs, biases[3], rows, w_out, [w0, w1, w2, w3a, w3b])
    w_full = lax.all_gather(w_mine, "batch", axis=0, tiled=True)
    kv1, kv2 = shift(kv0, dx=1), shift(kv0, dx=-1)
    part = KEYS // 2
    kv3a, kv3b = shift(kv1[:part], dx=1), shift(kv2[part:], dx=-1)
    gates = lax.all_to_all(gate, "seq", 0, 0, axis_index_groups=SAME_X)
    sums = attend(later[:1], q, q, own, [kv0], biases[:1], ((KEYS, 0, 0),), fresh=True)
    sums = attend(later[1:3], gates, q, sums, [kv1, kv2], biases[1:3], ((KEYS, 0, 0), (KEYS, 1, 0)))
    att = attend(later[3:], q, q, sums, [kv3a, kv3b], biases[3:], ((part, 0, 0), (part, 0, part)), last=True)
    atts = lax.all_to_all(att, "seq", 0, 0, axis_index_groups=SAME_X)
    return tuple(finish(history, candidates, w_full, atts, gates))


def solution(mesh):
    in_specs = (
        P("batch", "seq", None),
        P("batch", "seq", None),
        P("batch", "seq"),
        P("batch", "seq"),
        P(None, "batch"),
        P("batch", None),
        P(),
    )
    out_specs = (P("batch", "seq", None), P("batch", "seq", None))
    return jax.shard_map(body, mesh=mesh, in_specs=in_specs, out_specs=out_specs, check_vma=False)
```

time: 210 us -> 162 us (0.77)
  waiting for transfers between devices: 53.5 us -> 14.7 us
  starting transfers between devices: 59.4 us -> 30.8 us
  blocking collectives: 0 us -> 20.8 us
  Pallas kernels: 64.8 us -> 50.4 us
  local copies, waits for them, and re-layouts: 14.4 us -> 28 us
    ppermute x38 -> x15, waiting for transfers between devices: 45 us -> 2.9 us  [shift(): return lax.ppermute(array, 'seq', seq_perm(dx, dz, flip))]
    ppermute x38 -> x15, starting transfers between devices: 55.4 us -> 23.4 us  [shift(): return lax.ppermute(array, 'seq', seq_perm(dx, dz, flip))]
    all_to_all x0 -> x1, blocking collectives: none -> 20.8 us  [body(): atts = lax.all_to_all(att, 'seq', 0, 0, axis_index_groups=SAME_X)]
    pallas_call x7, Pallas kernels: 58 us -> 43.5 us  [the longest x4 33 us: make_bias(): pl.pallas_call(functools.partial(bias_kernel, fresh=True), out_shape=jax....]
    unnamed x15 -> x31, local copies, waits for them, and re-layouts: 10.6 us -> 23.2 us
    all_to_all x0 -> x1, starting transfers between devices: none -> 3.43 us  [body(): gates = lax.all_to_all(gate, 'seq', 0, 0, axis_index_groups=SAME_X)]
    ppermute x4, waiting for transfers between devices: 8.51 us -> 11.8 us  [from_sources(): return lax.ppermute(array, ('batch', 'seq'), source_perm(dzl, dy))]
  transfers between devices with their start and end apart: 43 -> 22, of which waited for: 10 -> 3; matrix products, arithmetic and copies ran while one was open for 3% -> 4% of each run, Pallas kernels for 30% -> 27%
where the time goes in v2:
time: 162 us; the launch traced here: 161 us
  Pallas kernels  50.4 us (31%)
  starting transfers between devices  30.8 us (19%)
  local copies, waits for them, and re-layouts  28 us (17%)
  blocking collectives  20.8 us (13%)
  waiting for transfers between devices  14.7 us (9%)
  between operations  14.7 us (9%)
  other arithmetic  1.64 us (1%)
    pallas_call x4, Pallas kernels, make_bias(): pl.pallas_call(functools.partial(bias_kernel, fresh=True), out_shape=jax....  33 us
    ppermute x15, starting transfers between devices, shift(): return lax.ppermute(array, 'seq', seq_perm(dx, dz, flip))  23.4 us
    unnamed x31, local copies, waits for them, and re-layouts  23.2 us
    all_to_all x1, blocking collectives, body(): atts = lax.all_to_all(att, 'seq', 0, 0, axis_index_groups=SAME_X)  20.8 us
    ppermute x4, waiting for transfers between devices, from_sources(): return lax.ppermute(array, ('batch', 'seq'), source_perm(dzl, dy))  11.8 us
    pallas_call x3, Pallas kernels, attend(): pl.pallas_call(functools.partial(attend_kernel, fresh=fresh, last=last, c...  10.5 us
    ppermute x4, starting transfers between devices, from_sources(): return lax.ppermute(array, ('batch', 'seq'), source_perm(dzl, dy))  3.91 us
    all_to_all x1, starting transfers between devices, body(): gates = lax.all_to_all(gate, 'seq', 0, 0, axis_index_groups=SAME_X)  3.43 us
  transfers between devices with their start and end apart: 22, of which 3 were waited for; matrix products, arithmetic and copies ran while one was open for 4% of the time, Pallas kernels for 27%

profile of v2, /device:TPU:30, one launch (start us, length us, event | category | flops | bytes accessed | tf_op | source)
XLA Modules:
  0.0 161.0 jit_solution(10732694654840200264)
XLA Ops:
  10.6 3.3 %collective-permute-start = (s32[1,160]{1,0:T(1,128)S(1)}, s32[1,160]{1,0:T(1,128)S(1)}, u32[]{:S(2)}, u32[]{:S(2)}) collective-permute-start(s32[1,160]{1,0:T(1,128)S(1)} %constant_dynamic-update-slice_fusion), channel_id=1, source_target_pairs={{0,2},{1,3},{2,4},{3,5},{4,6},{5,7},{6,0},{7,1},{8,10},{9,11},{10,... | collective-permute-start | bytes 1928 | tf_op jit(solution)/shard_map/ppermute | solution.py:43
  13.8 3.0 %collective-permute-start.1 = (s32[1,160]{1,0:T(1,128)S(1)}, s32[1,160]{1,0:T(1,128)S(1)}, u32[]{:S(2)}, u32[]{:S(2)}) collective-permute-start(s32[1,160]{1,0:T(1,128)S(1)} %constant_dynamic-update-slice_fusion), channel_id=1, source_target_pairs={{0,6},{1,7},{2,0},{3,1},{4,2},{5,3},{6,4},{7,5},{8,14},{9,15},{10,... | collective-permute-start | bytes 1928 | tf_op jit(solution)/shard_map/ppermute | solution.py:43
  16.9 5.0 %collective-permute-start.2 = (s32[1,160]{1,0:T(1,128)S(1)}, s32[1,160]{1,0:T(1,128)S(1)}, u32[]{:S(2)}, u32[]{:S(2)}) collective-permute-start(s32[1,160]{1,0:T(1,128)S(1)} %constant_dynamic-update-slice_fusion), channel_id=1, source_target_pairs={{0,4},{1,5},{2,6},{3,7},{4,0},{5,1},{6,2},{7,3},{8,12},{9,13},{10,... | collective-permute-start | bytes 1928 | tf_op jit(solution)/shard_map/ppermute | solution.py:43
  30.1 8.6 %collective-permute-done.7 = bf16[2,256,128]{2,1,0:T(8,128)(2,1)S(1)} collective-permute-done((bf16[2,256,128]{2,1,0:T(8,128)(2,1)S(1)}, bf16[2,256,128]{2,1,0:T(8,128)(2,1)S(1)}, u32[]{:S(2)}, u32[]{:S(2)}) %collective-permute-start.7) | collective-permute-done | bytes 131104 | tf_op jit(solution)/shard_map/ppermute | solution.py:58
  38.7 3.2 %collective-permute-done.8 = bf16[2,256,128]{2,1,0:T(8,128)(2,1)S(1)} collective-permute-done((bf16[2,256,128]{2,1,0:T(8,128)(2,1)S(1)}, bf16[2,256,128]{2,1,0:T(8,128)(2,1)S(1)}, u32[]{:S(2)}, u32[]{:S(2)}) %collective-permute-start.8) | collective-permute-done | bytes 131104 | tf_op jit(solution)/shard_map/ppermute | solution.py:58
  45.8 2.9 %collective-permute-done.9.w1 = bf16[4,256,128]{2,1,0:T(8,128)(2,1)S(1)} collective-permute-done((bf16[4,256,128]{2,1,0:T(8,128)(2,1)S(1)}, bf16[4,256,128]{2,1,0:T(8,128)(2,1)S(1)}, u32[]{:S(2)}, u32[]{:S(2)}) %collective-permute-start.9) | collective-permute-done | bytes 262176 | tf_op jit(solution)/shard_map/ppermute | solution.py:43
  50.9 7.1 %make_bias.4.tie_ref.rest_2_ = f32[1280,1024]{1,0:T(8,128)S(1)} custom-call(s32[2]{0:T(128)S(1)} %pad_add_fusion.3.kpos_ref, s32[40]{0:T(128)S(1)} %fusion.16.flat_ref, f32[40]{0:T(128)S(1)} %broadcast_select_fusion.20.value_ref, s32[1]{0:T(128)} %get-tuple-element.30.later_ref.flag_ref, s32[16,128]{1,0:T(8,128)S(1)} %add_add_fusion.tq_ref, ...), custom_call_target="tpu_custom_call" | custom-call | flops 2621440000 | bytes 5242880 | tf_op jit(solution)/shard_map/make_bias/pallas_call | solution.py:121
  58.0 2.3 %copy-done = f32[1280,1024]{1,0:T(8,128)} copy-done((f32[1280,1024]{1,0:T(8,128)}, f32[1280,1024]{1,0:T(8,128)S(1)}, u32[]{:S(2)}) %copy-start) | copy-done | bytes 5242904
  60.3 2.5 %copy-done.1 = f32[1280,1024]{1,0:T(8,128)S(1)} copy-done((f32[1280,1024]{1,0:T(8,128)S(1)}, f32[1280,1024]{1,0:T(8,128)}, u32[]{:S(2)}) %copy-start.1) | copy-done | bytes 5242904
  64.6 3.4 %project.1 = (bf16[1280,128]{1,0:T(8,128)(2,1)S(1)}, bf16[1024,256]{1,0:T(8,128)(2,1)S(1)}, f32[256,128]{1,0:T(8,128)S(1)}, bf16[8,160,128]{2,1,0:T(8,128)(2,1)}, bf16[128,1024]{1,0:T(8,128)(2,1)}) custom-call(s32[4]{0:T(128)S(1)} %get-tuple-element.15.x_ref, f32[1280,1024]{1,0:T(8,128)S(1)} %copy-done.1, bf16[8,160,1024]{2,1,0:T(8,128)(2,1)S(1)} %bitcast.26, ...), custom_call_target="tpu_custom_call" | custom-call | flops 1342177280 | bytes 6291456 | tf_op jit(solution)/shard_map/project/pallas_call | solution.py:167
  72.3 11.7 %make_bias.5.rest_1_ = f32[1280,1024]{1,0:T(8,128)S(1)} custom-call(s32[2]{0:T(128)S(1)} %pad_add_fusion.4.kpos_ref, s32[40]{0:T(128)S(1)} %fusion.16.flat_ref, f32[40]{0:T(128)S(1)} %broadcast_select_fusion.20.value_ref, s32[1]{0:T(128)} %get-tuple-element.29.later_ref.flag_ref, s32[16,128]{1,0:T(8,128)S(1)} %add_add_fusion.tq_ref, ...), custom_call_target="tpu_custom_call" | custom-call | flops 2621440000 | bytes 5242880 | tf_op jit(solution)/shard_map/make_bias/pallas_call | solution.py:121
  84.1 2.3 %copy-done.3 = f32[1280,1024]{1,0:T(8,128)} copy-done((f32[1280,1024]{1,0:T(8,128)}, f32[1280,1024]{1,0:T(8,128)S(1)}, u32[]{:S(2)}) %copy-start.3) | copy-done | bytes 5242904
  86.3 3.4 %all-to-all-start = ((bf16[8,160,128]{2,1,0:T(8,128)(2,1)}), bf16[8,160,128]{2,1,0:T(8,128)(2,1)S(1)}, u32[]{:S(2)}, u32[]{:S(2)}) async-start(bf16[8,160,128]{2,1,0:T(8,128)(2,1)} %get-tuple-element.9), calls=%async_computation | async-start | bytes 655360 | tf_op jit(solution)/shard_map/all_to_all | solution.py:327
  89.8 7.9 %make_bias.6.rest_2_ = f32[1280,1024]{1,0:T(8,128)S(1)} custom-call(s32[2]{0:T(128)S(1)} %pad_add_fusion.5.kpos_ref, s32[40]{0:T(128)S(1)} %fusion.16.flat_ref, f32[40]{0:T(128)S(1)} %broadcast_select_fusion.20.value_ref, s32[1]{0:T(128)} %get-tuple-element.28.later_ref, s32[16,128]{1,0:T(8,128)S(1)} %add_add_fusion.tq_ref, ...), custom_call_target="tpu_custom_call" | custom-call | flops 2621440000 | bytes 5242880 | tf_op jit(solution)/shard_map/make_bias/pallas_call | solution.py:121
  97.7 2.4 %copy-done.4 = f32[1280,1024]{1,0:T(8,128)} copy-done((f32[1280,1024]{1,0:T(8,128)}, f32[1280,1024]{1,0:T(8,128)S(1)}, u32[]{:S(2)}) %copy-start.4) | copy-done | bytes 5242904
  100.1 6.4 %make_bias.7.rest_3_ = f32[1280,1024]{1,0:T(8,128)S(1)} custom-call(s32[2]{0:T(128)S(1)} %pad_add_fusion.6.kpos_ref, s32[40]{0:T(128)S(1)} %fusion.16.flat_ref, f32[40]{0:T(128)S(1)} %broadcast_select_fusion.20.value_ref, s32[1]{0:T(128)} %get-tuple-element.27.later_ref, s32[16,128]{1,0:T(8,128)S(1)} %add_add_fusion.tq_ref, ...), custom_call_target="tpu_custom_call" | custom-call | flops 2621440000 | bytes 5242880 | tf_op jit(solution)/shard_map/make_bias/pallas_call | solution.py:121
  106.5 2.3 %copy-done.6 = f32[1280,1024]{1,0:T(8,128)} copy-done((f32[1280,1024]{1,0:T(8,128)}, f32[1280,1024]{1,0:T(8,128)S(1)}, u32[]{:S(2)}) %copy-start.6) | copy-done | bytes 5242904
  112.2 2.5 %attend.3.sums_in = f32[1280,128]{1,0:T(8,128)S(1)} custom-call(s32[1]{0:T(128)} %get-tuple-element.29.later_ref.flag_ref, bf16[1280,128]{1,0:T(8,128)(2,1)S(1)} %get-tuple-element.8.tie_ref.q_ref, bf16[1280,128]{1,0:T(8,128)(2,1)S(1)} %get-tuple-element.8.tie_ref.q_ref, f32[256,128]{1,0:T(8,128)S(1)} %get-tuple-element.10.sums_in, ...), custom_call_target="tpu_custom_call" | custom-call | flops 1342177280 | bytes 5242880 | tf_op jit(solution)/shard_map/attend/pallas_call | solution.py:220
  114.8 2.5 %copy-done.5 = f32[1280,1024]{1,0:T(8,128)S(1)} copy-done((f32[1280,1024]{1,0:T(8,128)S(1)}, f32[1280,1024]{1,0:T(8,128)}, u32[]{:S(2)}) %copy-start.5) | copy-done | bytes 5242904
  117.2 2.5 %copy-done.7 = f32[1280,1024]{1,0:T(8,128)S(1)} copy-done((f32[1280,1024]{1,0:T(8,128)S(1)}, f32[1280,1024]{1,0:T(8,128)}, u32[]{:S(2)}) %copy-start.7) | copy-done | bytes 5242904
  119.7 4.4 %attend.4.sums_in = f32[1280,128]{1,0:T(8,128)S(1)} custom-call(s32[2]{0:T(128)S(1)} %slice.77.flag_ref, bf16[8,160,128]{2,1,0:T(8,128)(2,1)S(1)} %all-to-all-done.tie_ref.gate_ref, bf16[1280,128]{1,0:T(8,128)(2,1)S(1)} %get-tuple-element.8.tie_ref.q_ref, f32[1280,128]{1,0:T(8,128)S(1)} %attend.3.sums_in, ...), custom_call_target="tpu_custom_call" | custom-call | flops 2684354560 | bytes 10485760 | tf_op jit(solution)/shard_map/attend/pallas_call | solution.py:220
  124.2 2.5 %copy-done.2 = f32[1280,1024]{1,0:T(8,128)S(1)} copy-done((f32[1280,1024]{1,0:T(8,128)S(1)}, f32[1280,1024]{1,0:T(8,128)}, u32[]{:S(2)}) %copy-start.2) | copy-done | bytes 5242904
  126.7 3.5 %attend.5 = bf16[8,160,128]{2,1,0:T(8,128)(2,1)S(1)} custom-call(s32[1]{0:T(128)} %get-tuple-element.30.later_ref.flag_ref, bf16[1280,128]{1,0:T(8,128)(2,1)S(1)} %get-tuple-element.8.tie_ref.q_ref, bf16[1280,128]{1,0:T(8,128)(2,1)S(1)} %get-tuple-element.8.tie_ref.q_ref, f32[1280,128]{1,0:T(8,128)S(1)} %attend.4.sums_in, ...), custom_call_target="tpu_custom_call" | custom-call | flops 1342177280 | bytes 5242880 | tf_op jit(solution)/shard_map/attend/pallas_call | solution.py:220
  130.2 20.8 %all_to_all.10.att_ref = bf16[8,160,128]{2,1,0:T(8,128)(2,1)S(1)} all-to-all(bf16[8,160,128]{2,1,0:T(8,128)(2,1)S(1)} %attend.5), channel_id=1, replica_groups={{0,1,2,3,4,5,6,7},{8,9,10,11,12,13,14,15},{16,17,18,19,20,21,22,23},{24..., dimensions={0} | all-to-all | bytes 655360 | tf_op jit(solution)/shard_map/all_to_all | solution.py:331
  (109 shorter events, 30.1 us)
Async XLA Ops:
  7.2 53.2 %all-gather.6.cloned.1.call-start = ((), (), s32[]{:S(2)}) async-start(), calls=%async_computation.3 | async-start | bytes 2949120 | tf_op jit(solution)/shard_map/all_gather | solution.py:287
  9.2 141.8 %all-gather.4.cloned.1.call-start = ((), (), s32[]{:S(2)}) async-start(), calls=%async_computation.2 | async-start | bytes 2359296 | tf_op jit(solution)/shard_map/all_gather | solution.py:323
  10.6 16.0 %collective-permute-start = (s32[1,160]{1,0:T(1,128)S(1)}, s32[1,160]{1,0:T(1,128)S(1)}, u32[]{:S(2)}, u32[]{:S(2)}) collective-permute-start(s32[1,160]{1,0:T(1,128)S(1)} %constant_dynamic-update-slice_fusion), channel_id=1, source_target_pairs={{0,2},{1,3},{2,4},{3,5},{4,6},{5,7},{6,0},{7,1},{8,10},{9,11},{10,... | collective-permute-start | bytes 1928 | tf_op jit(solution)/shard_map/ppermute | solution.py:43
  13.8 12.7 %collective-permute-start.1 = (s32[1,160]{1,0:T(1,128)S(1)}, s32[1,160]{1,0:T(1,128)S(1)}, u32[]{:S(2)}, u32[]{:S(2)}) collective-permute-start(s32[1,160]{1,0:T(1,128)S(1)} %constant_dynamic-update-slice_fusion), channel_id=1, source_target_pairs={{0,6},{1,7},{2,0},{3,1},{4,2},{5,3},{6,4},{7,5},{8,14},{9,15},{10,... | collective-permute-start | bytes 1928 | tf_op jit(solution)/shard_map/ppermute | solution.py:43
  16.9 9.7 %collective-permute-start.2 = (s32[1,160]{1,0:T(1,128)S(1)}, s32[1,160]{1,0:T(1,128)S(1)}, u32[]{:S(2)}, u32[]{:S(2)}) collective-permute-start(s32[1,160]{1,0:T(1,128)S(1)} %constant_dynamic-update-slice_fusion), channel_id=1, source_target_pairs={{0,4},{1,5},{2,6},{3,7},{4,0},{5,1},{6,2},{7,3},{8,12},{9,13},{10,... | collective-permute-start | bytes 1928 | tf_op jit(solution)/shard_map/ppermute | solution.py:43
  22.7 4.0 %collective-permute-start.5 = (bf16[256,128]{1,0:T(8,128)(2,1)S(1)}, bf16[256,128]{1,0:T(8,128)(2,1)S(1)}, u32[]{:S(2)}, u32[]{:S(2)}) collective-permute-start(bf16[256,128]{1,0:T(8,128)(2,1)S(1)} %dynamic_slice.7), channel_id=1, source_target_pairs={{0,128},{1,129},{2,130},{3,131},{8,136},{9,137},{10,138},{11,139},... | collective-permute-start | bytes 196616 | tf_op jit(solution)/shard_map/ppermute | solution.py:58
  26.6 3.4 %collective-permute-start.3 = (s32[4,160]{1,0:T(4,128)S(1)}, s32[4,160]{1,0:T(4,128)S(1)}, u32[]{:S(2)}, u32[]{:S(2)}) collective-permute-start(s32[4,160]{1,0:T(4,128)S(1)} %pad_add_fusion.1), channel_id=1, source_target_pairs={{0,1},{1,0},{2,3},{3,2},{4,5},{5,4},{6,7},{7,6},{8,9},{9,8},{10,11... | collective-permute-start | bytes 7688 | tf_op jit(solution)/shard_map/ppermute | solution.py:43
  26.8 3.3 %collective-permute-start.6 = (bf16[2,256,128]{2,1,0:T(8,128)(2,1)S(1)}, bf16[2,256,128]{2,1,0:T(8,128)(2,1)S(1)}, u32[]{:S(2)}, u32[]{:S(2)}) collective-permute-start(bf16[2,256,128]{2,1,0:T(8,128)(2,1)S(1)} %pad_maximum_fusion.1), channel_id=1, source_target_pairs={{0,64},{1,65},{2,66},{3,67},{8,72},{9,73},{10,74},{11,75},{16,80},... | collective-permute-start | bytes 393224 | tf_op jit(solution)/shard_map/ppermute | solution.py:58
  27.4 11.2 %collective-permute-start.7 = (bf16[2,256,128]{2,1,0:T(8,128)(2,1)S(1)}, bf16[2,256,128]{2,1,0:T(8,128)(2,1)S(1)}, u32[]{:S(2)}, u32[]{:S(2)}) collective-permute-start(bf16[2,256,128]{2,1,0:T(8,128)(2,1)S(1)} %pad_maximum_fusion.1), channel_id=1, source_target_pairs={{0,32},{1,33},{2,34},{3,35},{8,40},{9,41},{10,42},{11,43},{16,48},... | collective-permute-start | bytes 393224 | tf_op jit(solution)/shard_map/ppermute | solution.py:58
  28.7 13.1 %collective-permute-start.8 = (bf16[2,256,128]{2,1,0:T(8,128)(2,1)S(1)}, bf16[2,256,128]{2,1,0:T(8,128)(2,1)S(1)}, u32[]{:S(2)}, u32[]{:S(2)}) collective-permute-start(bf16[2,256,128]{2,1,0:T(8,128)(2,1)S(1)} %pad_maximum_fusion.1), channel_id=1, source_target_pairs={{0,96},{1,97},{2,98},{3,99},{8,104},{9,105},{10,106},{11,107},{16,... | collective-permute-start | bytes 393224 | tf_op jit(solution)/shard_map/ppermute | solution.py:58
  42.0 6.7 %collective-permute-start.9 = (bf16[4,256,128]{2,1,0:T(8,128)(2,1)S(1)}, bf16[4,256,128]{2,1,0:T(8,128)(2,1)S(1)}, u32[]{:S(2)}, u32[]{:S(2)}) collective-permute-start(bf16[4,256,128]{2,1,0:T(8,128)(2,1)S(1)} %pad_maximum_fusion.w0), channel_id=1, source_target_pairs={{0,8},{1,9},{2,10},{3,11},{4,12},{5,13},{6,14},{7,15},{8,16},{9,17... | collective-permute-start | bytes 786440 | tf_op jit(solution)/shard_map/ppermute | solution.py:43
  42.6 7.7 %collective-permute-start.10 = (bf16[4,256,128]{2,1,0:T(8,128)(2,1)S(1)}, bf16[4,256,128]{2,1,0:T(8,128)(2,1)S(1)}, u32[]{:S(2)}, u32[]{:S(2)}) collective-permute-start(bf16[4,256,128]{2,1,0:T(8,128)(2,1)S(1)} %pad_maximum_fusion.w0), channel_id=1, source_target_pairs={{0,24},{1,25},{2,26},{3,27},{4,28},{5,29},{6,30},{7,31},{8,0},{9,1... | collective-permute-start | bytes 786440 | tf_op jit(solution)/shard_map/ppermute | solution.py:43
  44.2 6.7 %collective-permute-start.4 = (s32[8,128]{1,0:T(8,128)S(1)}, s32[8,128]{1,0:T(8,128)S(1)}, u32[]{:S(2)}, u32[]{:S(2)}) collective-permute-start(s32[8,128]{1,0:T(8,128)S(1)} %slice.83.tk_ref), channel_id=1, source_target_pairs={{0,16},{1,17},{2,18},{3,19},{4,20},{5,21},{6,22},{7,23},{8,24},{9,... | collective-permute-start | bytes 12296 | tf_op jit(solution)/shard_map/ppermute | solution.py:43
  48.6 11.7 %collective-permute-start.11 = (bf16[2,256,128]{2,1,0:T(8,128)(2,1)S(1)}, bf16[2,256,128]{2,1,0:T(8,128)(2,1)S(1)}, u32[]{:S(2)}, u32[]{:S(2)}) collective-permute-start(bf16[2,256,128]{2,1,0:T(8,128)(2,1)S(1)} %slice.89), channel_id=1, source_target_pairs={{0,8},{1,9},{2,10},{3,11},{4,12},{5,13},{6,14},{7,15},{8,16},{9,17... | collective-permute-start | bytes 393224 | tf_op jit(solution)/shard_map/ppermute | solution.py:43
  50.3 10.0 %collective-permute-start.12 = (bf16[2,256,128]{2,1,0:T(8,128)(2,1)S(1)}, bf16[2,256,128]{2,1,0:T(8,128)(2,1)S(1)}, u32[]{:S(2)}, u32[]{:S(2)}) collective-permute-start(bf16[2,256,128]{2,1,0:T(8,128)(2,1)S(1)} %slice.90), channel_id=1, source_target_pairs={{0,24},{1,25},{2,26},{3,27},{4,28},{5,29},{6,30},{7,31},{8,0},{9,1... | collective-permute-start | bytes 393224 | tf_op jit(solution)/shard_map/ppermute | solution.py:43
  68.3 21.5 %collective-permute-start.15 = (s32[8,128]{1,0:T(8,128)S(1)}, s32[8,128]{1,0:T(8,128)S(1)}, u32[]{:S(2)}, u32[]{:S(2)}) collective-permute-start(s32[8,128]{1,0:T(8,128)S(1)} %slice.83.tk_ref), channel_id=1, source_target_pairs={{0,8},{1,9},{2,10},{3,11},{4,12},{5,13},{6,14},{7,15},{8,16},{9,17... | collective-permute-start | bytes 12296 | tf_op jit(solution)/shard_map/ppermute | solution.py:43
  68.3 31.8 %collective-permute-start.16 = (s32[8,128]{1,0:T(8,128)S(1)}, s32[8,128]{1,0:T(8,128)S(1)}, u32[]{:S(2)}, u32[]{:S(2)}) collective-permute-start(s32[8,128]{1,0:T(8,128)S(1)} %slice.83.tk_ref), channel_id=1, source_target_pairs={{0,24},{1,25},{2,26},{3,27},{4,28},{5,29},{6,30},{7,31},{8,0},{9,1... | collective-permute-start | bytes 12296 | tf_op jit(solution)/shard_map/ppermute | solution.py:43
  70.3 38.4 %collective-permute-start.13 = (bf16[1024,256]{1,0:T(8,128)(2,1)S(1)}, bf16[1024,256]{1,0:T(8,128)(2,1)S(1)}, u32[]{:S(2)}, u32[]{:S(2)}) collective-permute-start(bf16[1024,256]{1,0:T(8,128)(2,1)S(1)} %get-tuple-element.11.rest_0_), channel_id=1, source_target_pairs={{0,8},{1,9},{2,10},{3,11},{4,12},{5,13},{6,14},{7,15},{8,16},{9,17... | collective-permute-start | bytes 1572872 | tf_op jit(solution)/shard_map/ppermute | solution.py:43
  71.8 37.7 %collective-permute-start.14 = (bf16[1024,256]{1,0:T(8,128)(2,1)S(1)}, bf16[1024,256]{1,0:T(8,128)(2,1)S(1)}, u32[]{:S(2)}, u32[]{:S(2)}) collective-permute-start(bf16[1024,256]{1,0:T(8,128)(2,1)S(1)} %get-tuple-element.11.rest_0_), channel_id=1, source_target_pairs={{0,24},{1,25},{2,26},{3,27},{4,28},{5,29},{6,30},{7,31},{8,0},{9,1... | collective-permute-start | bytes 1572872 | tf_op jit(solution)/shard_map/ppermute | solution.py:43
  86.3 28.4 %all-to-all-start = ((bf16[8,160,128]{2,1,0:T(8,128)(2,1)}), bf16[8,160,128]{2,1,0:T(8,128)(2,1)S(1)}, u32[]{:S(2)}, u32[]{:S(2)}) async-start(bf16[8,160,128]{2,1,0:T(8,128)(2,1)} %get-tuple-element.9), calls=%async_computation | async-start | bytes 655360 | tf_op jit(solution)/shard_map/all_to_all | solution.py:327
  109.4 14.7 %collective-permute-start.17 = (bf16[512,256]{1,0:T(8,128)(2,1)}, bf16[512,256]{1,0:T(8,128)(2,1)S(1)}, u32[]{:S(2)}, u32[]{:S(2)}) collective-permute-start(bf16[512,256]{1,0:T(8,128)(2,1)} %slice.91), channel_id=1, source_target_pairs={{0,8},{1,9},{2,10},{3,11},{4,12},{5,13},{6,14},{7,15},{8,16},{9,17... | collective-permute-start | bytes 786440 | tf_op jit(solution)/shard_map/ppermute | solution.py:43
  110.2 14.0 %collective-permute-start.18 = (bf16[512,256]{1,0:T(8,128)(2,1)}, bf16[512,256]{1,0:T(8,128)(2,1)S(1)}, u32[]{:S(2)}, u32[]{:S(2)}) collective-permute-start(bf16[512,256]{1,0:T(8,128)(2,1)} %slice.92), channel_id=1, source_target_pairs={{0,24},{1,25},{2,26},{3,27},{4,28},{5,29},{6,30},{7,31},{8,0},{9,1... | collective-permute-start | bytes 786440 | tf_op jit(solution)/shard_map/ppermute | solution.py:43
  119.7 31.3 %copy-start.10 = (bf16[1,128,1024]{2,1,0:T(8,128)(2,1)S(1)}, bf16[1,128,1024]{2,1,0:T(8,128)(2,1)}, u32[]{:S(2)}) copy-start(bf16[1,128,1024]{2,1,0:T(8,128)(2,1)} %hist_ref.3) | copy-start | bytes 786436
  119.7 31.3 %copy-start.12 = (bf16[1,32,1024]{2,1,0:T(8,128)(2,1)S(1)}, bf16[1,32,1024]{2,1,0:T(8,128)(2,1)}, u32[]{:S(2)}) copy-start(bf16[1,32,1024]{2,1,0:T(8,128)(2,1)} %cand_ref.3) | copy-start | bytes 196612
  (13 other events, 75.5 us)
Sparse Core Ops, SparseCore 0:
  9.8 42.6 all-gather.5
  68.1 44.2 all-gather.3

commit v3 on v2

v3 whole, which is shorter than its diff:
```python
import functools

import jax
import jax.numpy as jnp
from jax import lax
from jax.experimental import pallas as pl
from jax.experimental.pallas import tpu as pltpu
from jax.sharding import PartitionSpec as P

F32, BF16, I32 = jnp.float32, jnp.bfloat16, jnp.int32
ZL, NY, NX, ZH, NC = 2, 4, 4, 4, 2
NB, NS = ZL * NY, NX * ZH * NC
OFF = (0, -1, 1, 2)
HEADS, HD, D = 8, 128, 1024
HIST, CAND = 128, 32
ROWS = HIST + CAND
NP = ZH * NC
QH, QC = NP * HIST, NP * CAND
QROWS = QH + QC
KEYS = NP * HIST
LENGTH = NS * HIST
LEVELS = 12
MASKED = -1e30
SAME_X = [[x * NP + p for p in range(NP)] for x in range(NX)]
VM = pl.BlockSpec(memory_space=pltpu.VMEM)
SM = pl.BlockSpec(memory_space=pltpu.SMEM)


def params(mib):
    return pltpu.CompilerParams(vmem_limit_bytes=mib << 20)


def seq_perm(dx=0, dz=0, flip=False):
    pairs = []
    for s in range(NS):
        x, z, c = s // (ZH * NC), s // NC % ZH, s % NC
        t = ((x + dx) % NX * ZH + (z + dz) % ZH) * NC + (c ^ int(flip))
        pairs.append((s, t))
    return pairs


def shift(array, dx=0, dz=0, flip=False):
    return lax.ppermute(array, "seq", seq_perm(dx, dz, flip))


def source_perm(dzl=0, dy=0):
    pairs = []
    for b in range(NB):
        zl, y = b // NY, b % NY
        t = (zl + dzl) % ZL * NY + (y + dy) % NY
        for s in range(NS):
            if y % 2 == s // NC % ZH // 2:
                pairs.append((b * NS + s, t * NS + s))
    return pairs


def from_sources(array, dzl=0, dy=0):
    return lax.ppermute(array, ("batch", "seq"), source_perm(dzl, dy))


def norm_kernel(hist_ref, cand_ref, events_ref, requests_ref, out_ref, times_ref):
    for ref, first, count in ((hist_ref, 0, HIST), (cand_ref, HIST, CAND)):
        rows = ref[0].astype(F32)
        rows = rows - jnp.mean(rows, axis=-1, keepdims=True)
        spread = jnp.mean(rows * rows, axis=-1, keepdims=True)
        out_ref[first : first + count, :] = (rows * lax.rsqrt(spread + 1e-6)).astype(BF16)
    times_ref[...] = jnp.zeros_like(times_ref)
    times_ref[:, :HIST] = events_ref[...]
    times_ref[:, HIST:ROWS] = requests_ref[...]


def norm_rows(hist, cand, events, requests):
    return pl.pallas_call(
        norm_kernel,
        out_shape=[jax.ShapeDtypeStruct((ROWS, D), BF16), jax.ShapeDtypeStruct((1, 2 * HIST), I32)],
        in_specs=[VM] * 4,
        out_specs=[VM] * 2,
        cost_estimate=pl.CostEstimate(flops=8 * ROWS * D, bytes_accessed=4 * ROWS * D, transcendentals=0),
        name="norm_rows",
    )(hist, cand, events, requests)


def prepare_kernel(tq_ref, wout_ref, col_ref, wout_out):
    for i in range(QROWS // 128):
        col_ref[i * 128 : (i + 1) * 128, :] = jnp.transpose(jnp.broadcast_to(tq_ref[i : i + 1, :], (128, 128)))
    wout_out[...] = wout_ref[...]


def prepare(tq, w_out):
    return pl.pallas_call(
        prepare_kernel,
        out_shape=[jax.ShapeDtypeStruct((QROWS, 128), I32), jax.ShapeDtypeStruct(w_out.shape, BF16)],
        in_specs=[VM] * 2,
        out_specs=[VM] * 2,
        cost_estimate=pl.CostEstimate(flops=2 << 20, bytes_accessed=1 << 20, transcendentals=0),
        name="prepare",
    )(tq, w_out)


def half_silu(half):
    return half + half * jnp.tanh(half)


def project_kernel(core_ref, *refs):
    pieces, weights = refs[:NP], refs[NP]
    q_ref, kv_ref, own_ref, gate_ref, rows = refs[NP + 1 :]
    for r in range(ZH):
        for c in range(NC):
            place = core_ref[1 + r] * NC + (core_ref[0] ^ c)
            piece = pieces[c * ZH + r]
            rows[pl.ds(pl.multiple_of(place * HIST, HIST), HIST), :] = piece[:HIST, :]
            rows[pl.ds(pl.multiple_of(QH + place * CAND, CAND), CAND), :] = piece[HIST:, :]
    mixed = jnp.dot(rows[...], weights[:, 2 * HD :], preferred_element_type=F32)
    mixed = half_silu(0.5 * mixed)
    queries, keys = mixed[:, :HD], mixed[:, HD:]
    q_ref[...] = (queries * (0.5 * HD**-0.5)).astype(BF16)
    kv_ref[:, :HD] = keys[:QH].astype(BF16)
    dots = jnp.sum(queries[QH:].astype(BF16).astype(F32) * keys[QH:].astype(BF16).astype(F32), axis=-1, keepdims=True)
    own = half_silu(dots * (0.5 * HD**-0.5)).astype(BF16).astype(F32)
    mixed = jnp.dot(rows[...], weights[:, : 2 * HD], preferred_element_type=F32)
    mixed = half_silu(0.5 * mixed).astype(BF16)
    kv_ref[:, HD:] = mixed[:QH, HD:]
    own_ref[...] = own * mixed[QH:, HD:].astype(F32)
    for place in range(NP):
        gate_ref[place, :HIST, :] = mixed[place * HIST : (place + 1) * HIST, :HD]
        gate_ref[place, HIST:, :] = mixed[QH + place * CAND : QH + (place + 1) * CAND, :HD]


def project(where, pieces, w_head):
    return pl.pallas_call(
        project_kernel,
        out_shape=[
            jax.ShapeDtypeStruct((QROWS, HD), BF16),
            jax.ShapeDtypeStruct((KEYS, 2 * HD), BF16),
            jax.ShapeDtypeStruct((QC, HD), F32),
            jax.ShapeDtypeStruct((NP, ROWS, HD), BF16),
        ],
        in_specs=[SM] + [VM] * (NP + 1),
        out_specs=[VM] * 4,
        scratch_shapes=[pltpu.VMEM((QROWS, D), BF16)],
        compiler_params=params(14),
        cost_estimate=pl.CostEstimate(flops=2 * QROWS * D * 4 * HD, bytes_accessed=6 << 20, transcendentals=QROWS * 4 * HD),
        name="project",
    )(where, *pieces, w_head)


BLOCK = 256
TILES = (QROWS // 128) * NP


def attend_kernel(flag_ref, code_ref, base_ref, apart_ref, steps_ref, tie_ref, q_ref, sums_in, col_ref, *rest, fresh, last, chunks):
    arrays = sum(len(chunk) for chunk in chunks)
    kvs, tks = list(rest[:arrays]), rest[arrays : arrays + len(chunks)]
    out_ref, sums_ref, half_ref = rest[arrays + len(chunks) :]
    if fresh:
        sums_ref[:QH, :] = jnp.zeros((QH, HD), F32)
        sums_ref[QH:, :] = sums_in[...]
    else:
        sums_ref[...] = sums_in[...]
    row = lax.broadcasted_iota(I32, (128, 128), 0)
    lane = lax.broadcasted_iota(I32, (128, 128), 1)

    def scores(n, block, slot):
        first = block * BLOCK
        begin = 0
        for kv in parts[n]:
            keys = kv.shape[0]
            half = lax.dot_general(
                q_ref[first : first + BLOCK, :], kv[:, :HD], (((1,), (1,)), ((), ())), preferred_element_type=F32
            )
            for i in range(BLOCK // 128):
                for j in range(keys // 128):
                    at = n * TILES + (block * (BLOCK // 128) + i) * NP + begin // 128 + j
                    half_ref[slot, i * 128 : (i + 1) * 128, begin + j * 128 : begin + (j + 1) * 128] = (
                        half[i * 128 : (i + 1) * 128, j * 128 : (j + 1) * 128] + base_ref[at]
                    )
            begin += keys

    def correct(n, block, slot):
        is_cand = block * BLOCK >= QH

        def tile(t, carry):
            i, j = t // NP, t % NP
            at = n * TILES + (block * (BLOCK // 128)) * NP + t
            code = code_ref[at]
            time_low, time_high, place_low, place_high = (code & 15, (code >> 4) & 15, (code >> 8) & 15, (code >> 12) & 15)

            @pl.when((time_low != time_high) | (place_low != place_high))
            def _():
                rows = pl.ds(pl.multiple_of(i * 128, 128), 128)
                columns = pl.ds(pl.multiple_of(j * 128, 128), 128)
                first = pl.multiple_of(block * BLOCK + i * 128, 128)
                value = half_ref[slot, rows, columns]
                gap = col_ref[pl.ds(first, 128), :] - tks[n][pl.ds(j, 1), :]

                def time_step(level, value):
                    return value + jnp.where(gap >= (1 << (2 * level)), steps_ref[level], 0.0)

                value = lax.fori_loop(time_low, time_high, time_step, value)
                if is_cand:
                    gap2 = (LENGTH - apart_ref[NX + n] - j * 128) - lane
                else:
                    gap2 = (apart_ref[n] + (block * (BLOCK // 128) + i - j) * 128) + row - lane

                def place_step(level, value):
                    return value + jnp.where(gap2 >= (1 << level), steps_ref[LEVELS + level], 0.0)

                value = lax.fori_loop(place_low, place_high, place_step, value)
                if not is_cand:
                    value = jnp.where(gap2 >= 0, value, MASKED)
                half_ref[slot, rows, columns] = value

            return carry

        lax.fori_loop(0, BLOCK // 128 * NP, tile, 0)

    def combine(n, block, slot):
        first = block * BLOCK
        begin = 0
        total = sums_ref[first : first + BLOCK, :]
        for kv in parts[n]:
            keys = kv.shape[0]
            weights = half_silu(half_ref[slot, :, begin : begin + keys]).astype(BF16)
            total = total + jnp.dot(weights, kv[:, HD:], preferred_element_type=F32)
            begin += keys
        sums_ref[first : first + BLOCK, :] = total

    def sweep(n, blocks):
        for k, block in enumerate(blocks):
            scores(n, block, k % 2)
            if k > 0:
                combine(n, blocks[k - 1], (k - 1) % 2)
            correct(n, block, k % 2)
        combine(n, blocks[-1], (len(blocks) - 1) % 2)

    parts = []
    for chunk in chunks:
        parts.append([kvs.pop(0) for _ in chunk])
    for n in range(len(chunks)):

        @pl.when(flag_ref[n] == 0)
        def _():
            sweep(n, list(range(QROWS // BLOCK)))

        @pl.when(flag_ref[n] != 0)
        def _():
            sweep(n, [QROWS // BLOCK - 1])

    if last:
        for place in range(NP):
            out_ref[place, :HIST, :] = sums_ref[place * HIST : (place + 1) * HIST, :].astype(BF16)
            out_ref[place, HIST:, :] = sums_ref[QH + place * CAND : QH + (place + 1) * CAND, :].astype(BF16)
    else:
        out_ref[...] = sums_ref[...]


def attend(tables, steps, tie, q, sums, col, chunks, tks, fresh=False, last=False):
    flags, codes, bases, apart = tables
    kvs = [kv for chunk in chunks for kv in chunk]
    shapes = tuple(tuple(kv.shape[0] for kv in chunk) for chunk in chunks)
    keys = sum(kv.shape[0] for kv in kvs)
    return pl.pallas_call(
        functools.partial(attend_kernel, fresh=fresh, last=last, chunks=shapes),
        in_specs=[SM] * 5 + [pl.BlockSpec(memory_space=pl.ANY)] + [VM] * (3 + len(kvs) + len(tks)),
        out_specs=VM,
        out_shape=jax.ShapeDtypeStruct((NP, ROWS, HD), BF16) if last else jax.ShapeDtypeStruct((QROWS, HD), F32),
        scratch_shapes=[pltpu.VMEM((QROWS, HD), F32), pltpu.VMEM((2, BLOCK, KEYS), F32)],
        compiler_params=params(16),
        cost_estimate=pl.CostEstimate(
            flops=16 * QROWS * keys * HD, bytes_accessed=4 * QROWS * keys, transcendentals=QROWS * keys
        ),
        name="attend",
    )(flags, codes, bases, apart, steps, tie, q, sums, col, *kvs, *tks)


def finish_kernel(hist_ref, cand_ref, w_ref, att_ref, gate_ref, hist_out, cand_out):
    parts = [att_ref[h].astype(F32) for h in range(HEADS)]
    center = sum(jnp.sum(part, axis=-1, keepdims=True) for part in parts) * (1.0 / D)
    parts = [part - center for part in parts]
    spread = sum(jnp.sum(part * part, axis=-1, keepdims=True) for part in parts) * (1.0 / D)
    scale = lax.rsqrt(spread + 1e-6)
    parts = [(part * scale * gate_ref[h].astype(F32)).astype(BF16) for h, part in enumerate(parts)]
    total = jnp.dot(jnp.concatenate(parts, axis=1), w_ref[...], preferred_element_type=F32)
    hist_out[0] = (hist_ref[0].astype(F32) + total[:HIST]).astype(BF16)
    cand_out[0] = (cand_ref[0].astype(F32) + total[HIST:]).astype(BF16)


def finish(hist, cand, w_out, att, gate):
    return pl.pallas_call(
        finish_kernel,
        out_shape=[
            jax.ShapeDtypeStruct((1, HIST, D), BF16),
            jax.ShapeDtypeStruct((1, CAND, D), BF16),
        ],
        in_specs=[VM] * 5,
        out_specs=[VM, VM],
        compiler_params=params(6),
        cost_estimate=pl.CostEstimate(flops=2 * ROWS * D * D, bytes_accessed=4 << 20, transcendentals=0),
        name="finish",
    )(hist, cand, w_out, att, gate)


def gather_weights(w_proj, z, core, batch):
    z_lo, y = batch // NY, batch % NY
    head = NC * z + core
    mine = lax.dynamic_slice(w_proj, (0, head % 4 * HD), (D, HD))
    other = from_sources(mine, dzl=1)
    pair = jnp.stack([mine, other])
    up, down, across = from_sources(pair, dy=1), from_sources(pair, dy=-1), from_sources(pair, dy=2)
    is_source = y % 2 == z // 2
    halves = []
    for f in range(2):
        source = jnp.where(y // 2 == f, pair, across)
        sink = jnp.where((y - 1) % NY // 2 == f, up, down)
        halves.append(jnp.where(is_source, source, sink))
    low = [jnp.where(z_lo == 0, half[0], half[1]) for half in halves]
    high = [jnp.where(z_lo == 0, half[1], half[0]) for half in halves]
    return jnp.concatenate(low + high, axis=1)


def body(history, candidates, event_times, request_times, w_proj, w_out, bias_steps):
    seq, batch = lax.axis_index("seq"), lax.axis_index("batch")
    x, z, core = seq // (ZH * NC), seq // NC % ZH, seq % NC
    head = NC * z + core
    zs = [(z + off) % ZH for off in OFF]
    xs = jnp.stack([(x + off) % NX for off in OFF])

    n0, t0 = norm_rows(history, candidates, event_times, request_times)
    near = [n0, shift(n0, dz=1), shift(n0, dz=-1), shift(n0, dz=2)]
    pieces = near + [shift(piece, flip=True) for piece in near]

    near = [t0, shift(t0, dz=1), shift(t0, dz=-1), shift(t0, dz=2)]
    t4 = jnp.concatenate([sum(jnp.where(zs[r] == j, near[r], 0) for r in range(ZH)) for j in range(ZH)], axis=0)
    other = shift(t4, flip=True)
    t8 = jnp.stack([jnp.where(core == 0, t4, other), jnp.where(core == 0, other, t4)], axis=1).reshape(NP, 2 * HIST)
    k0 = t8[:, :HIST]
    tks = [k0, shift(k0, dx=1), shift(k0, dx=-1), shift(k0, dx=2)]
    cand_times = t8[:, HIST:ROWS].reshape(QC // 128, 128)
    tq = jnp.concatenate([k0, cand_times, jnp.zeros((6, 128), I32)], axis=0)

    w_head = gather_weights(w_proj, z, core, batch)

    steps = 0.5 * lax.dynamic_slice(bias_steps, (0, head), (2 * LEVELS, 1))[:, 0]
    level = jnp.arange(LEVELS, dtype=I32)
    tk = jnp.stack(tks)
    first_q = jnp.concatenate([k0[:, 0], jnp.min(cand_times, axis=1)])
    last_q = jnp.concatenate([k0[:, -1], jnp.max(cand_times, axis=1)])

    def passed(gap, marks):
        return jnp.sum((gap[..., None] >= marks).astype(I32), axis=-1)

    time_low = passed(first_q[None, :, None] - tk[:, None, :, -1], 4**level)
    time_high = passed(last_q[None, :, None] - tk[:, None, :, 0], 4**level)
    blocks = jnp.arange(NP, dtype=I32)
    hist_gap = ((x - xs)[:, None, None] * NP + blocks[None, :, None] - blocks[None, None, :]) * HIST
    cand_gap = LENGTH - (xs[:, None, None] * NP + blocks[None, None, :]) * HIST
    cand_gap = jnp.broadcast_to(cand_gap, (NX, QC // 128, NP))
    place_low = passed(jnp.concatenate([hist_gap, cand_gap], axis=1) - (HIST - 1), 2**level)
    place_high = passed(jnp.concatenate([hist_gap + (HIST - 1), cand_gap], axis=1), 2**level)
    hidden = jnp.concatenate([hist_gap < 0, cand_gap < 0], axis=1)
    code = time_low | (time_high << 4) | (place_low << 8) | (place_high << 12)
    code = jnp.where(hidden, 0, code).reshape(NX, TILES)
    base = jnp.sum(jnp.where(time_low[..., None] > level, steps[:LEVELS], 0.0), axis=-1)
    base = base + jnp.sum(jnp.where(place_low[..., None] > level, steps[LEVELS:], 0.0), axis=-1)
    base = jnp.where(hidden, MASKED, base).reshape(NX, TILES)
    later = (xs > x).astype(I32)
    col, w_mine = prepare(tq, w_out)
    w_full = lax.all_gather(w_mine, "batch", axis=0, tiled=True)

    def tables(first, count):
        chosen = slice(first, first + count)
        apart = jnp.zeros((2 * NX,), I32).at[:count].set((x - xs[chosen]) * KEYS).at[NX : NX + count].set(xs[chosen] * KEYS)
        return later[chosen], code[chosen].reshape(-1), base[chosen].reshape(-1), apart

    q, kv0, own, gate = project(jnp.stack([core, *zs]), pieces, w_head)
    kv1, kv2 = shift(kv0, dx=1), shift(kv0, dx=-1)
    part = KEYS // 2
    kv3a, kv3b = shift(kv1[:part], dx=1), shift(kv2[part:], dx=-1)
    gates = lax.all_to_all(gate, "seq", 0, 0, axis_index_groups=SAME_X)
    sums = attend(tables(0, 1), steps, q, q, own, col, [[kv0]], tks[:1], fresh=True)
    sums = attend(tables(1, 2), steps, gates, q, sums, col, [[kv1], [kv2]], tks[1:3])
    att = attend(tables(3, 1), steps, q, q, sums, col, [[kv3a, kv3b]], tks[3:], last=True)
    atts = lax.all_to_all(att, "seq", 0, 0, axis_index_groups=SAME_X)
    return tuple(finish(history, candidates, w_full, atts, gates))


def solution(mesh):
    in_specs = (
        P("batch", "seq", None),
        P("batch", "seq", None),
        P("batch", "seq"),
        P("batch", "seq"),
        P(None, "batch"),
        P("batch", None),
        P(),
    )
    out_specs = (P("batch", "seq", None), P("batch", "seq", None))
    return jax.shard_map(body, mesh=mesh, in_specs=in_specs, out_specs=out_specs, check_vma=False)
```

time: 162 us -> 176 us (1.086)
  waiting for transfers between devices: 14.7 us -> 38.5 us
  local copies, waits for them, and re-layouts: 28 us -> 10.4 us
  Pallas kernels: 50.4 us -> 35.7 us
  starting transfers between devices: 30.8 us -> 44.2 us
  other arithmetic: 1.64 us -> 8.23 us
    pallas_call x5 -> x2, Pallas kernels: 35 us -> 4.15 us  [the longest x1 2.08 us: norm_rows(): pl.pallas_call(norm_kernel, out_shape=[jax.ShapeDtypeStruct((ROWS, D), BF...]
    ppermute x15 -> x18, waiting for transfers between devices: 2.9 us -> 24.1 us  [shift(): return lax.ppermute(array, 'seq', seq_perm(dx, dz, flip))]
    unnamed x31 -> x22, local copies, waits for them, and re-layouts: 23.2 us -> 5.39 us
    pallas_call x3, Pallas kernels: 10.5 us -> 26.6 us  [attend(): pl.pallas_call(functools.partial(attend_kernel, fresh=fresh, last=last, c...]
    ppermute x15 -> x18, starting transfers between devices: 23.4 us -> 36.4 us  [shift(): return lax.ppermute(array, 'seq', seq_perm(dx, dz, flip))]
    reduce_sum x2 -> x4, other arithmetic: 0.18 us -> 3.48 us  [the longest x2 3.06 us: passed(): return jnp.sum((gap[..., None] >= marks).astype(I32), axis=-1)]
    ppermute x4, waiting for transfers between devices: 11.8 us -> 14.4 us  [from_sources(): return lax.ppermute(array, ('batch', 'seq'), source_perm(dzl, dy))]
  transfers between devices with their start and end apart: 22 -> 24, of which waited for: 3 -> 5; matrix products, arithmetic and copies ran while one was open for 4% -> 8% of each run, Pallas kernels for 27% -> 18%
where the time goes in v3:
time: 176 us; the launch traced here: 174 us
  starting transfers between devices  44.2 us (25%)
  waiting for transfers between devices  38.5 us (22%)
  Pallas kernels  35.7 us (20%)
  blocking collectives  21.2 us (12%)
  between operations  15.9 us (9%)
  local copies, waits for them, and re-layouts  10.4 us (6%)
  other arithmetic  8.23 us (5%)
    ppermute x18, starting transfers between devices, shift(): return lax.ppermute(array, 'seq', seq_perm(dx, dz, flip))  36.4 us
    pallas_call x3, Pallas kernels, attend(): pl.pallas_call(functools.partial(attend_kernel, fresh=fresh, last=last, c...  26.6 us
    ppermute x18, waiting for transfers between devices, shift(): return lax.ppermute(array, 'seq', seq_perm(dx, dz, flip))  24.1 us
    all_to_all x1, blocking collectives, body(): atts = lax.all_to_all(att, 'seq', 0, 0, axis_index_groups=SAME_X)  21.2 us
    ppermute x4, waiting for transfers between devices, from_sources(): return lax.ppermute(array, ('batch', 'seq'), source_perm(dzl, dy))  14.4 us
    unnamed x22, local copies, waits for them, and re-layouts  5.39 us
    ppermute x4, starting transfers between devices, from_sources(): return lax.ppermute(array, ('batch', 'seq'), source_perm(dzl, dy))  3.95 us
    all_to_all x1, starting transfers between devices, body(): gates = lax.all_to_all(gate, 'seq', 0, 0, axis_index_groups=SAME_X)  3.82 us
  transfers between devices with their start and end apart: 24, of which 5 were waited for; matrix products, arithmetic and copies ran while one was open for 8% of the time, Pallas kernels for 18%

profile of v3, /device:TPU:30, one launch (start us, length us, event | category | flops | bytes accessed | tf_op | source)
XLA Modules:
  0.0 174.0 jit_solution(11545016340537223149)
XLA Ops:
  7.2 2.1 %norm_rows.1 = (bf16[160,1024]{1,0:T(8,128)(2,1)}, s32[1,256]{1,0:T(1,128)}) custom-call(bf16[1,128,1024]{2,1,0:T(8,128)(2,1)} %hist_ref.3, bf16[1,32,1024]{2,1,0:T(8,128)(2,1)} %cand_ref.3, s32[1,128]{1,0:T(1,128)} %events_ref.1, s32[1,32]{1,0:T(1,128)} %requests_ref.1), custom_call_target="tpu_custom_call" | custom-call | flops 1310720 | bytes 655360 | tf_op jit(solution)/shard_map/norm_rows/pallas_call | solution.py:73
  9.3 3.3 %collective-permute-start.7 = (bf16[160,1024]{1,0:T(8,128)(2,1)}, bf16[160,1024]{1,0:T(8,128)(2,1)S(1)}, u32[]{:S(2)}, u32[]{:S(2)}) collective-permute-start(bf16[160,1024]{1,0:T(8,128)(2,1)} %get-tuple-element.84.refs_0_), channel_id=1, source_target_pairs={{0,2},{1,3},{2,4},{3,5},{4,6},{5,7},{6,0},{7,1},{8,10},{9,11},{10,... | collective-permute-start | bytes 983048 | tf_op jit(solution)/shard_map/ppermute | solution.py:43
  12.6 3.1 %collective-permute-start.8 = (bf16[160,1024]{1,0:T(8,128)(2,1)}, bf16[160,1024]{1,0:T(8,128)(2,1)S(1)}, u32[]{:S(2)}, u32[]{:S(2)}) collective-permute-start(bf16[160,1024]{1,0:T(8,128)(2,1)} %get-tuple-element.84.refs_0_), channel_id=1, source_target_pairs={{0,6},{1,7},{2,0},{3,1},{4,2},{5,3},{6,4},{7,5},{8,14},{9,15},{10,... | collective-permute-start | bytes 983048 | tf_op jit(solution)/shard_map/ppermute | solution.py:43
  17.1 2.8 %collective-permute-start.1 = (s32[1,256]{1,0:T(1,128)}, s32[1,256]{1,0:T(1,128)S(1)}, u32[]{:S(2)}, u32[]{:S(2)}) collective-permute-start(s32[1,256]{1,0:T(1,128)} %get-tuple-element.82), channel_id=1, source_target_pairs={{0,6},{1,7},{2,0},{3,1},{4,2},{5,3},{6,4},{7,5},{8,14},{9,15},{10,... | collective-permute-start | bytes 3080 | tf_op jit(solution)/shard_map/ppermute | solution.py:43
  19.8 4.9 %collective-permute-start.2 = (s32[1,256]{1,0:T(1,128)}, s32[1,256]{1,0:T(1,128)S(1)}, u32[]{:S(2)}, u32[]{:S(2)}) collective-permute-start(s32[1,256]{1,0:T(1,128)} %get-tuple-element.82), channel_id=1, source_target_pairs={{0,4},{1,5},{2,6},{3,7},{4,0},{5,1},{6,2},{7,3},{8,12},{9,13},{10,... | collective-permute-start | bytes 3080 | tf_op jit(solution)/shard_map/ppermute | solution.py:43
  27.8 1.5 convert_reduce_fusion.1
  29.7 2.2 %collective-permute-done.1 = s32[1,256]{1,0:T(1,128)S(1)} collective-permute-done((s32[1,256]{1,0:T(1,128)}, s32[1,256]{1,0:T(1,128)S(1)}, u32[]{:S(2)}, u32[]{:S(2)}) %collective-permute-start.1) | collective-permute-done | bytes 1056 | tf_op jit(solution)/shard_map/ppermute | solution.py:43
  37.1 1.5 collective-permute-start.5
  38.6 1.4 collective-permute-start.6
  41.3 2.1 %prepare.1 = (s32[1280,128]{1,0:T(8,128)}, bf16[128,1024]{1,0:T(8,128)(2,1)}) custom-call(s32[16,128]{1,0:T(8,128)} %add_add_fusion.tq_ref, bf16[128,1024]{1,0:T(8,128)(2,1)} %wout_ref.1), custom_call_target="tpu_custom_call" | custom-call | flops 2097152 | bytes 1048576 | tf_op jit(solution)/shard_map/prepare/pallas_call | solution.py:90
  44.8 1.5 convert_reduce_fusion.2
  50.0 12.5 %collective-permute-start.9 = (bf16[160,1024]{1,0:T(8,128)(2,1)S(1)}, bf16[160,1024]{1,0:T(8,128)(2,1)S(1)}, u32[]{:S(2)}, u32[]{:S(2)}) collective-permute-start(bf16[160,1024]{1,0:T(8,128)(2,1)S(1)} %copy-done.5), channel_id=1, source_target_pairs={{0,4},{1,5},{2,6},{3,7},{4,0},{5,1},{6,2},{7,3},{8,12},{9,13},{10,... | collective-permute-start | bytes 983048 | tf_op jit(solution)/shard_map/ppermute | solution.py:43
  62.8 19.8 %collective-permute-done.9.refs_3_ = bf16[160,1024]{1,0:T(8,128)(2,1)S(1)} collective-permute-done((bf16[160,1024]{1,0:T(8,128)(2,1)S(1)}, bf16[160,1024]{1,0:T(8,128)(2,1)S(1)}, u32[]{:S(2)}, u32[]{:S(2)}) %collective-permute-start.9) | collective-permute-done | bytes 327712 | tf_op jit(solution)/shard_map/ppermute | solution.py:43
  83.1 14.3 %collective-permute-done.16 = bf16[2,1024,128]{2,1,0:T(8,128)(2,1)S(1)} collective-permute-done((bf16[2,1024,128]{2,1,0:T(8,128)(2,1)S(1)}, bf16[2,1024,128]{2,1,0:T(8,128)(2,1)S(1)}, u32[]{:S(2)}, u32[]{:S(2)}) %collective-permute-start.16) | collective-permute-done | bytes 524320 | tf_op jit(solution)/shard_map/ppermute | solution.py:58
  99.1 3.3 %project.1 = (bf16[1280,128]{1,0:T(8,128)(2,1)S(1)}, bf16[1024,256]{1,0:T(8,128)(2,1)}, f32[256,128]{1,0:T(8,128)S(1)}, bf16[8,160,128]{2,1,0:T(8,128)(2,1)}) custom-call(s32[5]{0:T(128)S(1)} %stack.86.core_ref, bf16[160,1024]{1,0:T(8,128)(2,1)S(1)} %copy-done.5, bf16[160,1024]{1,0:T(8,128)(2,1)S(1)} %collective-permute-done.7.refs_1_, ...), custom_call_target="tpu_custom_call" | custom-call | flops 1342177280 | bytes 6291456 | tf_op jit(solution)/shard_map/project/pallas_call | solution.py:130
  103.7 1.5 collective-permute-start.19
  105.2 3.8 %all-to-all-start = ((bf16[8,160,128]{2,1,0:T(8,128)(2,1)}), bf16[8,160,128]{2,1,0:T(8,128)(2,1)S(1)}, u32[]{:S(2)}, u32[]{:S(2)}) async-start(bf16[8,160,128]{2,1,0:T(8,128)(2,1)} %get-tuple-element.86), calls=%async_computation | async-start | bytes 655360 | tf_op jit(solution)/shard_map/all_to_all | solution.py:379
  110.5 9.7 %attend.3.sums_in = f32[1280,128]{1,0:T(8,128)S(1)} custom-call(s32[1]{0:T(128)} %get-tuple-element.124.flag_ref, s32[80]{0:T(128)S(1)} %reshape.360.code_ref, f32[80]{0:T(128)S(1)} %reshape.361.base_ref, s32[8]{0:T(128)S(1)} %constant_dynamic-update-slice_fusion.apart_ref, f32[24]{0:T(128)S(1)} %fusion.23.steps_ref, bf16[1280,128]{1,0:T(8,128)(2,1)S(1)} %copy-done.7, ...), custom_call_target="tpu_custom_call" | custom-call | flops 2684354560 | bytes 5242880 | tf_op jit(solution)/shard_map/attend/pallas_call | solution.py:262
  121.0 1.7 collective-permute-start.20
  125.8 10.7 %attend.4.sums_in = f32[1280,128]{1,0:T(8,128)S(1)} custom-call(s32[2]{0:T(128)S(1)} %slice.176.flag_ref, s32[160]{0:T(256)S(1)} %reshape.358.code_ref, f32[160]{0:T(256)S(1)} %reshape.359.base_ref, s32[8]{0:T(128)S(1)} %constant_dynamic-update-slice_fusion.1.apart_ref, f32[24]{0:T(128)S(1)} %fusion.23.steps_ref, ...), custom_call_target="tpu_custom_call" | custom-call | flops 5368709120 | bytes 10485760 | tf_op jit(solution)/shard_map/attend/pallas_call | solution.py:262
  136.5 6.3 %attend.5 = bf16[8,160,128]{2,1,0:T(8,128)(2,1)S(1)} custom-call(s32[1]{0:T(128)} %get-tuple-element.125.flag_ref, s32[80]{0:T(128)S(1)} %reshape.356.code_ref, f32[80]{0:T(128)S(1)} %reshape.357.base_ref, s32[8]{0:T(128)S(1)} %constant_dynamic-update-slice_fusion.2.apart_ref, f32[24]{0:T(128)S(1)} %fusion.23.steps_ref, bf16[1280,128]{1,0:T(8,128)(2,1)S(1)} %copy-done.8, ...), custom_call_target="tpu_custom_call" | custom-call | flops 2684354560 | bytes 5242880 | tf_op jit(solution)/shard_map/attend/pallas_call | solution.py:262
  142.8 21.2 %all_to_all.10.att_ref = bf16[8,160,128]{2,1,0:T(8,128)(2,1)S(1)} all-to-all(bf16[8,160,128]{2,1,0:T(8,128)(2,1)S(1)} %attend.5), channel_id=1, replica_groups={{0,1,2,3,4,5,6,7},{8,9,10,11,12,13,14,15},{16,17,18,19,20,21,22,23},{24..., dimensions={0} | all-to-all | bytes 655360 | tf_op jit(solution)/shard_map/all_to_all | solution.py:383
  164.0 1.6 copy-done.1
  165.6 1.6 finish.1
  (127 shorter events, 23.8 us)
Async XLA Ops:
  7.2 156.8 %all-gather.2.cloned.1.call-start = ((), (), s32[]{:S(2)}) async-start(), calls=%async_computation.2 | async-start | bytes 2359296 | tf_op jit(solution)/shard_map/all_gather | solution.py:368
  9.3 40.6 %collective-permute-start.7 = (bf16[160,1024]{1,0:T(8,128)(2,1)}, bf16[160,1024]{1,0:T(8,128)(2,1)S(1)}, u32[]{:S(2)}, u32[]{:S(2)}) collective-permute-start(bf16[160,1024]{1,0:T(8,128)(2,1)} %get-tuple-element.84.refs_0_), channel_id=1, source_target_pairs={{0,2},{1,3},{2,4},{3,5},{4,6},{5,7},{6,0},{7,1},{8,10},{9,11},{10,... | collective-permute-start | bytes 983048 | tf_op jit(solution)/shard_map/ppermute | solution.py:43
  12.6 49.9 %collective-permute-start.8 = (bf16[160,1024]{1,0:T(8,128)(2,1)}, bf16[160,1024]{1,0:T(8,128)(2,1)S(1)}, u32[]{:S(2)}, u32[]{:S(2)}) collective-permute-start(bf16[160,1024]{1,0:T(8,128)(2,1)} %get-tuple-element.84.refs_0_), channel_id=1, source_target_pairs={{0,6},{1,7},{2,0},{3,1},{4,2},{5,3},{6,4},{7,5},{8,14},{9,15},{10,... | collective-permute-start | bytes 983048 | tf_op jit(solution)/shard_map/ppermute | solution.py:43
  15.7 14.0 %collective-permute-start = (s32[1,256]{1,0:T(1,128)}, s32[1,256]{1,0:T(1,128)S(1)}, u32[]{:S(2)}, u32[]{:S(2)}) collective-permute-start(s32[1,256]{1,0:T(1,128)} %get-tuple-element.82), channel_id=1, source_target_pairs={{0,2},{1,3},{2,4},{3,5},{4,6},{5,7},{6,0},{7,1},{8,10},{9,11},{10,... | collective-permute-start | bytes 3080 | tf_op jit(solution)/shard_map/ppermute | solution.py:43
  17.1 14.8 %collective-permute-start.1 = (s32[1,256]{1,0:T(1,128)}, s32[1,256]{1,0:T(1,128)S(1)}, u32[]{:S(2)}, u32[]{:S(2)}) collective-permute-start(s32[1,256]{1,0:T(1,128)} %get-tuple-element.82), channel_id=1, source_target_pairs={{0,6},{1,7},{2,0},{3,1},{4,2},{5,3},{6,4},{7,5},{8,14},{9,15},{10,... | collective-permute-start | bytes 3080 | tf_op jit(solution)/shard_map/ppermute | solution.py:43
  19.8 12.9 %collective-permute-start.2 = (s32[1,256]{1,0:T(1,128)}, s32[1,256]{1,0:T(1,128)S(1)}, u32[]{:S(2)}, u32[]{:S(2)}) collective-permute-start(s32[1,256]{1,0:T(1,128)} %get-tuple-element.82), channel_id=1, source_target_pairs={{0,4},{1,5},{2,6},{3,7},{4,0},{5,1},{6,2},{7,3},{8,12},{9,13},{10,... | collective-permute-start | bytes 3080 | tf_op jit(solution)/shard_map/ppermute | solution.py:43
  33.5 3.0 %collective-permute-start.3 = (s32[4,256]{1,0:T(4,128)S(1)}, s32[4,256]{1,0:T(4,128)S(1)}, u32[]{:S(2)}, u32[]{:S(2)}) collective-permute-start(s32[4,256]{1,0:T(4,128)S(1)} %pad_add_fusion.5), channel_id=1, source_target_pairs={{0,1},{1,0},{2,3},{3,2},{4,5},{5,4},{6,7},{7,6},{8,9},{9,8},{10,11... | collective-permute-start | bytes 12296 | tf_op jit(solution)/shard_map/ppermute | solution.py:43
  36.5 7.3 %collective-permute-start.4 = (s32[8,128]{1,0:T(8,128)S(1)}, s32[8,128]{1,0:T(8,128)S(1)}, u32[]{:S(2)}, u32[]{:S(2)}) collective-permute-start(s32[8,128]{1,0:T(8,128)S(1)} %get-tuple-element.114.rest_1_), channel_id=1, source_target_pairs={{0,8},{1,9},{2,10},{3,11},{4,12},{5,13},{6,14},{7,15},{8,16},{9,17... | collective-permute-start | bytes 12296 | tf_op jit(solution)/shard_map/ppermute | solution.py:43
  37.1 7.4 %collective-permute-start.5 = (s32[8,128]{1,0:T(8,128)S(1)}, s32[8,128]{1,0:T(8,128)S(1)}, u32[]{:S(2)}, u32[]{:S(2)}) collective-permute-start(s32[8,128]{1,0:T(8,128)S(1)} %get-tuple-element.114.rest_1_), channel_id=1, source_target_pairs={{0,24},{1,25},{2,26},{3,27},{4,28},{5,29},{6,30},{7,31},{8,0},{9,1... | collective-permute-start | bytes 12296 | tf_op jit(solution)/shard_map/ppermute | solution.py:43
  38.6 5.8 %collective-permute-start.6 = (s32[8,128]{1,0:T(8,128)S(1)}, s32[8,128]{1,0:T(8,128)S(1)}, u32[]{:S(2)}, u32[]{:S(2)}) collective-permute-start(s32[8,128]{1,0:T(8,128)S(1)} %get-tuple-element.114.rest_1_), channel_id=1, source_target_pairs={{0,16},{1,17},{2,18},{3,19},{4,20},{5,21},{6,22},{7,23},{8,24},{9,... | collective-permute-start | bytes 12296 | tf_op jit(solution)/shard_map/ppermute | solution.py:43
  43.8 2.6 %collective-permute-start.14 = (bf16[1024,128]{1,0:T(8,128)(2,1)S(1)}, bf16[1024,128]{1,0:T(8,128)(2,1)S(1)}, u32[]{:S(2)}, u32[]{:S(2)}) collective-permute-start(bf16[1024,128]{1,0:T(8,128)(2,1)S(1)} %constant_dynamic-slice_fusion), channel_id=1, source_target_pairs={{0,128},{1,129},{2,130},{3,131},{8,136},{9,137},{10,138},{11,139},... | collective-permute-start | bytes 786440 | tf_op jit(solution)/shard_map/ppermute | solution.py:58
  46.4 36.2 %collective-permute-start.15 = (bf16[2,1024,128]{2,1,0:T(8,128)(2,1)S(1)}, bf16[2,1024,128]{2,1,0:T(8,128)(2,1)S(1)}, u32[]{:S(2)}, u32[]{:S(2)}) collective-permute-start(bf16[2,1024,128]{2,1,0:T(8,128)(2,1)S(1)} %pad_maximum_fusion.1), channel_id=1, source_target_pairs={{0,64},{1,65},{2,66},{3,67},{8,72},{9,73},{10,74},{11,75},{16,80},... | collective-permute-start | bytes 1572872 | tf_op jit(solution)/shard_map/ppermute | solution.py:58
  47.1 50.3 %collective-permute-start.16 = (bf16[2,1024,128]{2,1,0:T(8,128)(2,1)S(1)}, bf16[2,1024,128]{2,1,0:T(8,128)(2,1)S(1)}, u32[]{:S(2)}, u32[]{:S(2)}) collective-permute-start(bf16[2,1024,128]{2,1,0:T(8,128)(2,1)S(1)} %pad_maximum_fusion.1), channel_id=1, source_target_pairs={{0,32},{1,33},{2,34},{3,35},{8,40},{9,41},{10,42},{11,43},{16,48},... | collective-permute-start | bytes 1572872 | tf_op jit(solution)/shard_map/ppermute | solution.py:58
  48.4 49.0 %collective-permute-start.17 = (bf16[2,1024,128]{2,1,0:T(8,128)(2,1)S(1)}, bf16[2,1024,128]{2,1,0:T(8,128)(2,1)S(1)}, u32[]{:S(2)}, u32[]{:S(2)}) collective-permute-start(bf16[2,1024,128]{2,1,0:T(8,128)(2,1)S(1)} %pad_maximum_fusion.1), channel_id=1, source_target_pairs={{0,96},{1,97},{2,98},{3,99},{8,104},{9,105},{10,106},{11,107},{16,... | collective-permute-start | bytes 1572872 | tf_op jit(solution)/shard_map/ppermute | solution.py:58
  50.0 32.6 %collective-permute-start.9 = (bf16[160,1024]{1,0:T(8,128)(2,1)S(1)}, bf16[160,1024]{1,0:T(8,128)(2,1)S(1)}, u32[]{:S(2)}, u32[]{:S(2)}) collective-permute-start(bf16[160,1024]{1,0:T(8,128)(2,1)S(1)} %copy-done.5), channel_id=1, source_target_pairs={{0,4},{1,5},{2,6},{3,7},{4,0},{5,1},{6,2},{7,3},{8,12},{9,13},{10,... | collective-permute-start | bytes 983048 | tf_op jit(solution)/shard_map/ppermute | solution.py:43
  62.5 35.3 %collective-permute-start.10 = (bf16[160,1024]{1,0:T(8,128)(2,1)S(1)}, bf16[160,1024]{1,0:T(8,128)(2,1)S(1)}, u32[]{:S(2)}, u32[]{:S(2)}) collective-permute-start(bf16[160,1024]{1,0:T(8,128)(2,1)S(1)} %copy-done.5), channel_id=1, source_target_pairs={{0,1},{1,0},{2,3},{3,2},{4,5},{5,4},{6,7},{7,6},{8,9},{9,8},{10,11... | collective-permute-start | bytes 983048 | tf_op jit(solution)/shard_map/ppermute | solution.py:43
  82.6 15.3 %collective-permute-start.11 = (bf16[160,1024]{1,0:T(8,128)(2,1)S(1)}, bf16[160,1024]{1,0:T(8,128)(2,1)S(1)}, u32[]{:S(2)}, u32[]{:S(2)}) collective-permute-start(bf16[160,1024]{1,0:T(8,128)(2,1)S(1)} %collective-permute-done.7.refs_1_), channel_id=1, source_target_pairs={{0,1},{1,0},{2,3},{3,2},{4,5},{5,4},{6,7},{7,6},{8,9},{9,8},{10,11... | collective-permute-start | bytes 983048 | tf_op jit(solution)/shard_map/ppermute | solution.py:43
  82.6 15.3 %collective-permute-start.12 = (bf16[160,1024]{1,0:T(8,128)(2,1)S(1)}, bf16[160,1024]{1,0:T(8,128)(2,1)S(1)}, u32[]{:S(2)}, u32[]{:S(2)}) collective-permute-start(bf16[160,1024]{1,0:T(8,128)(2,1)S(1)} %collective-permute-done.8.refs_2_), channel_id=1, source_target_pairs={{0,1},{1,0},{2,3},{3,2},{4,5},{5,4},{6,7},{7,6},{8,9},{9,8},{10,11... | collective-permute-start | bytes 983048 | tf_op jit(solution)/shard_map/ppermute | solution.py:43
  97.4 1.6 collective-permute-start.13
  103.1 17.0 %collective-permute-start.18 = (bf16[1024,256]{1,0:T(8,128)(2,1)}, bf16[1024,256]{1,0:T(8,128)(2,1)S(1)}, u32[]{:S(2)}, u32[]{:S(2)}) collective-permute-start(bf16[1024,256]{1,0:T(8,128)(2,1)} %get-tuple-element.89.rest_0_), channel_id=1, source_target_pairs={{0,8},{1,9},{2,10},{3,11},{4,12},{5,13},{6,14},{7,15},{8,16},{9,17... | collective-permute-start | bytes 1572872 | tf_op jit(solution)/shard_map/ppermute | solution.py:43
  103.7 19.0 %collective-permute-start.19 = (bf16[1024,256]{1,0:T(8,128)(2,1)}, bf16[1024,256]{1,0:T(8,128)(2,1)S(1)}, u32[]{:S(2)}, u32[]{:S(2)}) collective-permute-start(bf16[1024,256]{1,0:T(8,128)(2,1)} %get-tuple-element.89.rest_0_), channel_id=1, source_target_pairs={{0,24},{1,25},{2,26},{3,27},{4,28},{5,29},{6,30},{7,31},{8,0},{9,1... | collective-permute-start | bytes 1572872 | tf_op jit(solution)/shard_map/ppermute | solution.py:43
  105.2 18.6 %all-to-all-start = ((bf16[8,160,128]{2,1,0:T(8,128)(2,1)}), bf16[8,160,128]{2,1,0:T(8,128)(2,1)S(1)}, u32[]{:S(2)}, u32[]{:S(2)}) async-start(bf16[8,160,128]{2,1,0:T(8,128)(2,1)} %get-tuple-element.86), calls=%async_computation | async-start | bytes 655360 | tf_op jit(solution)/shard_map/all_to_all | solution.py:379
  121.0 15.5 %collective-permute-start.20 = (bf16[512,256]{1,0:T(8,128)(2,1)}, bf16[512,256]{1,0:T(8,128)(2,1)S(1)}, u32[]{:S(2)}, u32[]{:S(2)}) collective-permute-start(bf16[512,256]{1,0:T(8,128)(2,1)} %slice.200), channel_id=1, source_target_pairs={{0,8},{1,9},{2,10},{3,11},{4,12},{5,13},{6,14},{7,15},{8,16},{9,17... | collective-permute-start | bytes 786440 | tf_op jit(solution)/shard_map/ppermute | solution.py:43
  123.4 13.1 %collective-permute-start.21 = (bf16[512,256]{1,0:T(8,128)(2,1)}, bf16[512,256]{1,0:T(8,128)(2,1)}, u32[]{:S(2)}, u32[]{:S(2)}) collective-permute-start(bf16[512,256]{1,0:T(8,128)(2,1)} %slice.201), channel_id=1, source_target_pairs={{0,24},{1,25},{2,26},{3,27},{4,28},{5,29},{6,30},{7,31},{8,0},{9,1... | collective-permute-start | bytes 786440 | tf_op jit(solution)/shard_map/ppermute | solution.py:43
  (11 other events, 133.5 us)
Sparse Core Ops, SparseCore 0:
  43.5 52.1 all-gather.1

commit v4 on v3

--- a/solution.py
+++ b/solution.py
@@ -80,36 +80,39 @@
     )(hist, cand, events, requests)
 
 
-def prepare_kernel(tq_ref, wout_ref, col_ref, wout_out):
+def prepare_kernel(tq_ref, col_ref):
     for i in range(QROWS // 128):
         col_ref[i * 128 : (i + 1) * 128, :] = jnp.transpose(jnp.broadcast_to(tq_ref[i : i + 1, :], (128, 128)))
-    wout_out[...] = wout_ref[...]
-
-
-def prepare(tq, w_out):
+
+
+def prepare(tq):
     return pl.pallas_call(
         prepare_kernel,
-        out_shape=[jax.ShapeDtypeStruct((QROWS, 128), I32), jax.ShapeDtypeStruct(w_out.shape, BF16)],
-        in_specs=[VM] * 2,
-        out_specs=[VM] * 2,
+        out_shape=jax.ShapeDtypeStruct((QROWS, 128), I32),
+        in_specs=[VM],
+        out_specs=VM,
         cost_estimate=pl.CostEstimate(flops=2 << 20, bytes_accessed=1 << 20, transcendentals=0),
         name="prepare",
-    )(tq, w_out)
+    )(tq)
 
 
 def half_silu(half):
     return half + half * jnp.tanh(half)
 
 
-def project_kernel(core_ref, *refs):
-    pieces, weights = refs[:NP], refs[NP]
-    q_ref, kv_ref, own_ref, gate_ref, rows = refs[NP + 1 :]
-    for r in range(ZH):
-        for c in range(NC):
-            place = core_ref[1 + r] * NC + (core_ref[0] ^ c)
-            piece = pieces[c * ZH + r]
-            rows[pl.ds(pl.multiple_of(place * HIST, HIST), HIST), :] = piece[:HIST, :]
-            rows[pl.ds(pl.multiple_of(QH + place * CAND, CAND), CAND), :] = piece[HIST:, :]
+def project_kernel(where_ref, *refs):
+    rows_ref, (w0, w1, w2, w3a, w3b), wout_ref = refs[0], refs[1:6], refs[6]
+    q_ref, kv_ref, own_ref, gate_ref, wout_out, rows, weights = refs[7:]
+    wout_out[...] = wout_ref[...]
+    for place in range(NP):
+        rows[place * HIST : (place + 1) * HIST, :] = rows_ref[place, :HIST, :]
+        rows[QH + place * CAND : QH + (place + 1) * CAND, :] = rows_ref[place, HIST:, :]
+    depth = D // NX
+    for m in range(NX):
+        at = pl.multiple_of(where_ref[m] * depth, depth)
+        for kind in range(4):
+            part = (w0, w1, w2)[m][kind] if m < 3 else (w3a, w3b)[kind // 2][kind % 2]
+            weights[pl.ds(at, depth), kind * HD : (kind + 1) * HD] = part
     mixed = jnp.dot(rows[...], weights[:, 2 * HD :], preferred_element_type=F32)
     mixed = half_silu(0.5 * mixed)
     queries, keys = mixed[:, :HD], mixed[:, HD:]
@@ -126,7 +129,7 @@
         gate_ref[place, HIST:, :] = mixed[QH + place * CAND : QH + (place + 1) * CAND, :HD]
 
 
-def project(where, pieces, w_head):
+def project(where, rows, parts, w_out):
     return pl.pallas_call(
         project_kernel,
         out_shape=[
@@ -134,21 +137,24 @@
             jax.ShapeDtypeStruct((KEYS, 2 * HD), BF16),
             jax.ShapeDtypeStruct((QC, HD), F32),
             jax.ShapeDtypeStruct((NP, ROWS, HD), BF16),
+            jax.ShapeDtypeStruct(w_out.shape, BF16),
         ],
-        in_specs=[SM] + [VM] * (NP + 1),
-        out_specs=[VM] * 4,
-        scratch_shapes=[pltpu.VMEM((QROWS, D), BF16)],
-        compiler_params=params(14),
+        in_specs=[SM] + [VM] * 7,
+        out_specs=[VM] * 5,
+        scratch_shapes=[pltpu.VMEM((QROWS, D), BF16), pltpu.VMEM((D, 4 * HD), BF16)],
+        compiler_params=params(16),
         cost_estimate=pl.CostEstimate(flops=2 * QROWS * D * 4 * HD, bytes_accessed=6 << 20, transcendentals=QROWS * 4 * HD),
         name="project",
-    )(where, *pieces, w_head)
+    )(where, rows, *parts, w_out)
 
 
 BLOCK = 256
 TILES = (QROWS // 128) * NP
-
-
-def attend_kernel(flag_ref, code_ref, base_ref, apart_ref, steps_ref, tie_ref, q_ref, sums_in, col_ref, *rest, fresh, last, chunks):
+STEPS = QROWS // BLOCK
+STEP_TILES = TILES // STEPS
+
+
+def attend_kernel(flag_ref, count_ref, work_ref, base_ref, apart_ref, steps_ref, tie_ref, q_ref, sums_in, col_ref, *rest, fresh, last, chunks):
     arrays = sum(len(chunk) for chunk in chunks)
     kvs, tks = list(rest[:arrays]), rest[arrays : arrays + len(chunks)]
     out_ref, sums_ref, half_ref = rest[arrays + len(chunks) :]
@@ -179,14 +185,11 @@
     def correct(n, block, slot):
         is_cand = block * BLOCK >= QH
 
-        def tile(t, carry):
-            i, j = t // NP, t % NP
-            at = n * TILES + (block * (BLOCK // 128)) * NP + t
-            code = code_ref[at]
-            time_low, time_high, place_low, place_high = (code & 15, (code >> 4) & 15, (code >> 8) & 15, (code >> 12) & 15)
-
-            @pl.when((time_low != time_high) | (place_low != place_high))
-            def _():
+        def tile(k, carry):
+            code = work_ref[n * TILES + block * STEP_TILES + k]
+            i, j = (code >> 3) & 1, code & 7
+            time_low, time_high, place_low, place_high = [(code >> bit) & 15 for bit in (4, 8, 12, 16)]
+            if True:
                 rows = pl.ds(pl.multiple_of(i * 128, 128), 128)
                 columns = pl.ds(pl.multiple_of(j * 128, 128), 128)
                 first = pl.multiple_of(block * BLOCK + i * 128, 128)
@@ -212,7 +215,7 @@
 
             return carry
 
-        lax.fori_loop(0, BLOCK // 128 * NP, tile, 0)
+        lax.fori_loop(0, count_ref[n * STEPS + block], tile, 0)
 
     def combine(n, block, slot):
         first = block * BLOCK
@@ -255,13 +258,13 @@
 
 
 def attend(tables, steps, tie, q, sums, col, chunks, tks, fresh=False, last=False):
-    flags, codes, bases, apart = tables
+    flags, counts, works, bases, apart = tables
     kvs = [kv for chunk in chunks for kv in chunk]
     shapes = tuple(tuple(kv.shape[0] for kv in chunk) for chunk in chunks)
     keys = sum(kv.shape[0] for kv in kvs)
     return pl.pallas_call(
         functools.partial(attend_kernel, fresh=fresh, last=last, chunks=shapes),
-        in_specs=[SM] * 5 + [pl.BlockSpec(memory_space=pl.ANY)] + [VM] * (3 + len(kvs) + len(tks)),
+        in_specs=[SM] * 6 + [pl.BlockSpec(memory_space=pl.ANY)] + [VM] * (3 + len(kvs) + len(tks)),
         out_specs=VM,
         out_shape=jax.ShapeDtypeStruct((NP, ROWS, HD), BF16) if last else jax.ShapeDtypeStruct((QROWS, HD), F32),
         scratch_shapes=[pltpu.VMEM((QROWS, HD), F32), pltpu.VMEM((2, BLOCK, KEYS), F32)],
@@ -270,7 +273,7 @@
             flops=16 * QROWS * keys * HD, bytes_accessed=4 * QROWS * keys, transcendentals=QROWS * keys
         ),
         name="attend",
-    )(flags, codes, bases, apart, steps, tie, q, sums, col, *kvs, *tks)
+    )(flags, counts, works, bases, apart, steps, tie, q, sums, col, *kvs, *tks)
 
 
 def finish_kernel(hist_ref, cand_ref, w_ref, att_ref, gate_ref, hist_out, cand_out):
@@ -300,10 +303,11 @@
     )(hist, cand, w_out, att, gate)
 
 
-def gather_weights(w_proj, z, core, batch):
+def gather_weights(w_proj, x, z, core, batch):
+    depth = D // NX
     z_lo, y = batch // NY, batch % NY
     head = NC * z + core
-    mine = lax.dynamic_slice(w_proj, (0, head % 4 * HD), (D, HD))
+    mine = lax.dynamic_slice(w_proj, (x * depth, head % 4 * HD), (depth, HD))
     other = from_sources(mine, dzl=1)
     pair = jnp.stack([mine, other])
     up, down, across = from_sources(pair, dy=1), from_sources(pair, dy=-1), from_sources(pair, dy=2)
@@ -315,30 +319,35 @@
         halves.append(jnp.where(is_source, source, sink))
     low = [jnp.where(z_lo == 0, half[0], half[1]) for half in halves]
     high = [jnp.where(z_lo == 0, half[1], half[0]) for half in halves]
-    return jnp.concatenate(low + high, axis=1)
+    return jnp.stack(low + high)
 
 
 def body(history, candidates, event_times, request_times, w_proj, w_out, bias_steps):
     seq, batch = lax.axis_index("seq"), lax.axis_index("batch")
     x, z, core = seq // (ZH * NC), seq // NC % ZH, seq % NC
     head = NC * z + core
-    zs = [(z + off) % ZH for off in OFF]
     xs = jnp.stack([(x + off) % NX for off in OFF])
 
     n0, t0 = norm_rows(history, candidates, event_times, request_times)
-    near = [n0, shift(n0, dz=1), shift(n0, dz=-1), shift(n0, dz=2)]
-    pieces = near + [shift(piece, flip=True) for piece in near]
-
-    near = [t0, shift(t0, dz=1), shift(t0, dz=-1), shift(t0, dz=2)]
-    t4 = jnp.concatenate([sum(jnp.where(zs[r] == j, near[r], 0) for r in range(ZH)) for j in range(ZH)], axis=0)
-    other = shift(t4, flip=True)
-    t8 = jnp.stack([jnp.where(core == 0, t4, other), jnp.where(core == 0, other, t4)], axis=1).reshape(NP, 2 * HIST)
+    rows = lax.all_gather(n0, "seq", axis_index_groups=SAME_X)
+
+    bits = [seq >> bit & 1 for bit in range(5)]
+    times = t0
+    for bit in range(5):
+        if bit == 3:
+            t8, times = times, times[:, :HIST]
+        other = lax.ppermute(times, "seq", [(s, s ^ (1 << bit)) for s in range(NS)])
+        first = bits[bit] == 0
+        times = jnp.concatenate([jnp.where(first, times, other), jnp.where(first, other, times)], axis=0)
     k0 = t8[:, :HIST]
-    tks = [k0, shift(k0, dx=1), shift(k0, dx=-1), shift(k0, dx=2)]
+    by_x = times.reshape(NX, NP, HIST)
+    tks = [sum(jnp.where(xs[m] == j, by_x[j], 0) for j in range(NX)) for m in range(NX)]
     cand_times = t8[:, HIST:ROWS].reshape(QC // 128, 128)
     tq = jnp.concatenate([k0, cand_times, jnp.zeros((6, 128), I32)], axis=0)
 
-    w_head = gather_weights(w_proj, z, core, batch)
+    w0 = gather_weights(w_proj, x, z, core, batch)
+    w1, w2 = shift(w0, dx=1), shift(w0, dx=-1)
+    w_parts = [w0, w1, w2, shift(w1[:2], dx=1), shift(w2[2:], dx=-1)]
 
     steps = 0.5 * lax.dynamic_slice(bias_steps, (0, head), (2 * LEVELS, 1))[:, 0]
     level = jnp.arange(LEVELS, dtype=I32)
@@ -359,20 +368,27 @@
     place_high = passed(jnp.concatenate([hist_gap + (HIST - 1), cand_gap], axis=1), 2**level)
     hidden = jnp.concatenate([hist_gap < 0, cand_gap < 0], axis=1)
     code = time_low | (time_high << 4) | (place_low << 8) | (place_high << 12)
-    code = jnp.where(hidden, 0, code).reshape(NX, TILES)
+    mixed = ~hidden & ((time_low != time_high) | (place_low != place_high))
+    number = jnp.arange(STEP_TILES, dtype=I32)
+    code = (code << 4 | number.reshape(BLOCK // 128, NP)[jnp.arange(QROWS // 128) % (BLOCK // 128)]).reshape(NX, STEPS, STEP_TILES)
+    mixed = mixed.reshape(NX, STEPS, STEP_TILES)
+    rank = jnp.sum(jnp.where(number[None, :] < number[:, None], mixed[..., None, :].astype(I32), 0), axis=-1)
+    spot = mixed[..., None] & (rank[..., None] == number)
+    works = jnp.sum(jnp.where(spot, code[..., None], 0), axis=-2).reshape(NX, TILES)
+    counts = jnp.sum(mixed.astype(I32), axis=-1)
     base = jnp.sum(jnp.where(time_low[..., None] > level, steps[:LEVELS], 0.0), axis=-1)
     base = base + jnp.sum(jnp.where(place_low[..., None] > level, steps[LEVELS:], 0.0), axis=-1)
     base = jnp.where(hidden, MASKED, base).reshape(NX, TILES)
     later = (xs > x).astype(I32)
-    col, w_mine = prepare(tq, w_out)
-    w_full = lax.all_gather(w_mine, "batch", axis=0, tiled=True)
+    col = prepare(tq)
 
     def tables(first, count):
         chosen = slice(first, first + count)
-        apart = jnp.zeros((2 * NX,), I32).at[:count].set((x - xs[chosen]) * KEYS).at[NX : NX + count].set(xs[chosen] * KEYS)
-        return later[chosen], code[chosen].reshape(-1), base[chosen].reshape(-1), apart
-
-    q, kv0, own, gate = project(jnp.stack([core, *zs]), pieces, w_head)
+        apart = jnp.concatenate([jnp.roll((x - xs) * KEYS, -first), jnp.roll(xs * KEYS, -first)])
+        return later[chosen], counts[chosen].reshape(-1), works[chosen].reshape(-1), base[chosen].reshape(-1), apart
+
+    q, kv0, own, gate, w_mine = project(xs, rows, w_parts, w_out)
+    w_full = lax.all_gather(w_mine, "batch", axis=0, tiled=True)
     kv1, kv2 = shift(kv0, dx=1), shift(kv0, dx=-1)
     part = KEYS // 2
     kv3a, kv3b = shift(kv1[:part], dx=1), shift(kv2[part:], dx=-1)

time: 176 us -> 147 us (0.84)
  waiting for transfers between devices: 38.5 us -> 26.7 us
  starting transfers between devices: 44.2 us -> 36.9 us
  Pallas kernels: 35.7 us -> 29.3 us
  blocking collectives: 21.2 us -> 15.9 us
  other arithmetic: 8.23 us -> 11.2 us
    ppermute x18 -> x8, starting transfers between devices: 36.4 us -> 9.9 us  [shift(): return lax.ppermute(array, 'seq', seq_perm(dx, dz, flip))]
    ppermute x0 -> x5, starting transfers between devices: none -> 15.1 us  [body(): other = lax.ppermute(times, 'seq', [(s, s ^ 1 << bit) for s in range(NS)])]
    ppermute x18 -> x8, waiting for transfers between devices: 24.1 us -> 11 us  [shift(): return lax.ppermute(array, 'seq', seq_perm(dx, dz, flip))]
    ppermute x4, waiting for transfers between devices: 14.4 us -> 5.52 us  [from_sources(): return lax.ppermute(array, ('batch', 'seq'), source_perm(dzl, dy))]
    all_to_all x1, waiting for transfers between devices: 0.01 us -> 6.42 us  [body(): gates = lax.all_to_all(gate, 'seq', 0, 0, axis_index_groups=SAME_X)]
    pallas_call x3, Pallas kernels: 26.6 us -> 20.6 us  [attend(): pl.pallas_call(functools.partial(attend_kernel, fresh=fresh, last=last, c...]
    all_to_all x1, blocking collectives: 21.2 us -> 15.9 us  [body(): atts = lax.all_to_all(att, 'seq', 0, 0, axis_index_groups=SAME_X)]
    all_to_all x1, starting transfers between devices: 3.82 us -> 8 us  [body(): gates = lax.all_to_all(gate, 'seq', 0, 0, axis_index_groups=SAME_X)]
  transfers between devices with their start and end apart: 24 -> 20, of which waited for: 5 -> 9; matrix products, arithmetic and copies ran while one was open for 8% -> 12% of each run, Pallas kernels for 18% -> 15%
where the time goes in v4:
time: 147 us; the launch traced here: 146 us
  starting transfers between devices  36.9 us (25%)
  Pallas kernels  29.3 us (20%)
  waiting for transfers between devices  26.7 us (18%)
  blocking collectives  15.9 us (11%)
  between operations  14.6 us (10%)
  local copies, waits for them, and re-layouts  11.2 us (8%)
  other arithmetic  11.2 us (8%)
    pallas_call x3, Pallas kernels, attend(): pl.pallas_call(functools.partial(attend_kernel, fresh=fresh, last=last, c...  20.6 us
    all_to_all x1, blocking collectives, body(): atts = lax.all_to_all(att, 'seq', 0, 0, axis_index_groups=SAME_X)  15.9 us
    ppermute x5, starting transfers between devices, body(): other = lax.ppermute(times, 'seq', [(s, s ^ 1 << bit) for s in range(NS)])  15.1 us
    ppermute x8, waiting for transfers between devices, shift(): return lax.ppermute(array, 'seq', seq_perm(dx, dz, flip))  11 us
    ppermute x8, starting transfers between devices, shift(): return lax.ppermute(array, 'seq', seq_perm(dx, dz, flip))  9.9 us
    all_to_all x1, starting transfers between devices, body(): gates = lax.all_to_all(gate, 'seq', 0, 0, axis_index_groups=SAME_X)  8 us
    all_to_all x1, waiting for transfers between devices, body(): gates = lax.all_to_all(gate, 'seq', 0, 0, axis_index_groups=SAME_X)  6.42 us
    ppermute x4, waiting for transfers between devices, from_sources(): return lax.ppermute(array, ('batch', 'seq'), source_perm(dzl, dy))  5.52 us
  transfers between devices with their start and end apart: 20, of which 9 were waited for; matrix products, arithmetic and copies ran while one was open for 12% of the time, Pallas kernels for 15%

profile of v4, /device:TPU:30, one launch (start us, length us, event | category | flops | bytes accessed | tf_op | source)
XLA Modules:
  0.0 145.9 jit_solution(1396142533463217215)
XLA Ops:
  7.2 2.0 %norm_rows.1 = (bf16[160,1024]{1,0:T(8,128)(2,1)}, s32[1,256]{1,0:T(1,128)}) custom-call(bf16[1,128,1024]{2,1,0:T(8,128)(2,1)} %hist_ref.3, bf16[1,32,1024]{2,1,0:T(8,128)(2,1)} %cand_ref.3, s32[1,128]{1,0:T(1,128)} %events_ref.1, s32[1,32]{1,0:T(1,128)} %requests_ref.1), custom_call_target="tpu_custom_call" | custom-call | flops 1310720 | bytes 655360 | tf_op jit(solution)/shard_map/norm_rows/pallas_call | solution.py:73
  20.9 3.4 %collective-permute-start.9 = (s32[2,256]{1,0:T(2,128)S(1)}, s32[2,256]{1,0:T(2,128)S(1)}, u32[]{:S(2)}, u32[]{:S(2)}) collective-permute-start(s32[2,256]{1,0:T(2,128)S(1)} %pad_add_fusion.7), channel_id=1, source_target_pairs={{0,2},{1,3},{2,0},{3,1},{4,6},{5,7},{6,4},{7,5},{8,10},{9,11},{10,... | collective-permute-start | bytes 6152 | tf_op jit(solution)/shard_map/ppermute | solution.py:339
  24.3 1.6 %collective-permute-done.9 = s32[2,256]{1,0:T(2,128)S(1)} collective-permute-done((s32[2,256]{1,0:T(2,128)S(1)}, s32[2,256]{1,0:T(2,128)S(1)}, u32[]{:S(2)}, u32[]{:S(2)}) %collective-permute-start.9) | collective-permute-done | bytes 2080 | tf_op jit(solution)/shard_map/ppermute | solution.py:339
  25.9 9.3 %collective-permute-start.10 = (s32[4,256]{1,0:T(4,128)S(1)}, s32[4,256]{1,0:T(4,128)S(1)}, u32[]{:S(2)}, u32[]{:S(2)}) collective-permute-start(s32[4,256]{1,0:T(4,128)S(1)} %pad_add_fusion.6), channel_id=1, source_target_pairs={{0,4},{1,5},{2,6},{3,7},{4,0},{5,1},{6,2},{7,3},{8,12},{9,13},{10,... | collective-permute-start | bytes 12296 | tf_op jit(solution)/shard_map/ppermute | solution.py:339
  36.1 1.6 %collective-permute-done.10 = s32[4,256]{1,0:T(4,128)S(1)} collective-permute-done((s32[4,256]{1,0:T(4,128)S(1)}, s32[4,256]{1,0:T(4,128)S(1)}, u32[]{:S(2)}, u32[]{:S(2)}) %collective-permute-start.10) | collective-permute-done | bytes 4128 | tf_op jit(solution)/shard_map/ppermute | solution.py:339
  40.3 1.8 %prepare.1.col_ref = s32[1280,128]{1,0:T(8,128)} custom-call(s32[16,128]{1,0:T(8,128)} %add_add_fusion.tq_ref), custom_call_target="tpu_custom_call" | custom-call | flops 2097152 | bytes 1048576 | tf_op jit(solution)/shard_map/prepare/pallas_call | solution.py:89
  47.3 3.0 %collective-permute-done.2 = bf16[2,256,128]{2,1,0:T(8,128)(2,1)S(1)} collective-permute-done((bf16[2,256,128]{2,1,0:T(8,128)(2,1)S(1)}, bf16[2,256,128]{2,1,0:T(8,128)(2,1)S(1)}, u32[]{:S(2)}, u32[]{:S(2)}) %collective-permute-start.2) | collective-permute-done | bytes 131104 | tf_op jit(solution)/shard_map/ppermute | solution.py:58
  50.3 2.5 %collective-permute-done.3 = bf16[2,256,128]{2,1,0:T(8,128)(2,1)S(1)} collective-permute-done((bf16[2,256,128]{2,1,0:T(8,128)(2,1)S(1)}, bf16[2,256,128]{2,1,0:T(8,128)(2,1)S(1)}, u32[]{:S(2)}, u32[]{:S(2)}) %collective-permute-start.3) | collective-permute-done | bytes 131104 | tf_op jit(solution)/shard_map/ppermute | solution.py:58
  52.9 2.6 %collective-permute-start.4 = (bf16[4,256,128]{2,1,0:T(8,128)(2,1)S(1)}, bf16[4,256,128]{2,1,0:T(8,128)(2,1)S(1)}, u32[]{:S(2)}, u32[]{:S(2)}) collective-permute-start(bf16[4,256,128]{2,1,0:T(8,128)(2,1)S(1)} %pad_maximum_fusion.refs_1_), channel_id=1, source_target_pairs={{0,8},{1,9},{2,10},{3,11},{4,12},{5,13},{6,14},{7,15},{8,16},{9,17... | collective-permute-start | bytes 786440 | tf_op jit(solution)/shard_map/ppermute | solution.py:43
  55.6 5.1 %collective-permute-done.4.refs_2_ = bf16[4,256,128]{2,1,0:T(8,128)(2,1)S(1)} collective-permute-done((bf16[4,256,128]{2,1,0:T(8,128)(2,1)S(1)}, bf16[4,256,128]{2,1,0:T(8,128)(2,1)S(1)}, u32[]{:S(2)}, u32[]{:S(2)}) %collective-permute-start.4) | collective-permute-done | bytes 262176 | tf_op jit(solution)/shard_map/ppermute | solution.py:43
  60.7 3.0 %collective-permute-start.6 = (bf16[2,256,128]{2,1,0:T(8,128)(2,1)S(1)}, bf16[2,256,128]{2,1,0:T(8,128)(2,1)S(1)}, u32[]{:S(2)}, u32[]{:S(2)}) collective-permute-start(bf16[2,256,128]{2,1,0:T(8,128)(2,1)S(1)} %slice.211), channel_id=1, source_target_pairs={{0,8},{1,9},{2,10},{3,11},{4,12},{5,13},{6,14},{7,15},{8,16},{9,17... | collective-permute-start | bytes 393224 | tf_op jit(solution)/shard_map/ppermute | solution.py:43
  64.2 2.0 %collective-permute-done.6.refs_4_ = bf16[2,256,128]{2,1,0:T(8,128)(2,1)S(1)} collective-permute-done((bf16[2,256,128]{2,1,0:T(8,128)(2,1)S(1)}, bf16[2,256,128]{2,1,0:T(8,128)(2,1)S(1)}, u32[]{:S(2)}, u32[]{:S(2)}) %collective-permute-start.6) | collective-permute-done | bytes 131104 | tf_op jit(solution)/shard_map/ppermute | solution.py:43
  66.2 3.9 %collective-permute-done.7.refs_5_ = bf16[2,256,128]{2,1,0:T(8,128)(2,1)S(1)} collective-permute-done((bf16[2,256,128]{2,1,0:T(8,128)(2,1)S(1)}, bf16[2,256,128]{2,1,0:T(8,128)(2,1)S(1)}, u32[]{:S(2)}, u32[]{:S(2)}) %collective-permute-start.7) | collective-permute-done | bytes 131104 | tf_op jit(solution)/shard_map/ppermute | solution.py:43
  70.2 1.7 %copy-done.4 = bf16[1280,1024]{1,0:T(8,128)(2,1)S(1)} copy-done((bf16[1280,1024]{1,0:T(8,128)(2,1)S(1)}, bf16[1280,1024]{1,0:T(8,128)(2,1)}, u32[]{:S(2)}) %copy-start.4) | copy-done | bytes 2621464
  71.9 3.4 %project.1 = (bf16[1280,128]{1,0:T(8,128)(2,1)S(1)}, bf16[1024,256]{1,0:T(8,128)(2,1)S(1)}, f32[256,128]{1,0:T(8,128)S(1)}, bf16[8,160,128]{2,1,0:T(8,128)(2,1)}, bf16[128,1024]{1,0:T(8,128)(2,1)}) custom-call(s32[4]{0:T(128)S(1)} %get-tuple-element.29.where_ref, bf16[8,160,1024]{2,1,0:T(8,128)(2,1)S(1)} %bitcast.26, ...), custom_call_target="tpu_custom_call" | custom-call | flops 1342177280 | bytes 6291456 | tf_op jit(solution)/shard_map/project/pallas_call | solution.py:133
  78.7 2.0 %collective-permute-start.14 = (bf16[1024,256]{1,0:T(8,128)(2,1)S(1)}, bf16[1024,256]{1,0:T(8,128)(2,1)S(1)}, u32[]{:S(2)}, u32[]{:S(2)}) collective-permute-start(bf16[1024,256]{1,0:T(8,128)(2,1)S(1)} %get-tuple-element.15.rest_0_), channel_id=1, source_target_pairs={{0,24},{1,25},{2,26},{3,27},{4,28},{5,29},{6,30},{7,31},{8,0},{9,1... | collective-permute-start | bytes 1572872 | tf_op jit(solution)/shard_map/ppermute | solution.py:43
  80.7 8.0 %all-to-all-start = ((bf16[8,160,128]{2,1,0:T(8,128)(2,1)}), bf16[8,160,128]{2,1,0:T(8,128)(2,1)S(1)}, u32[]{:S(2)}, u32[]{:S(2)}) async-start(bf16[8,160,128]{2,1,0:T(8,128)(2,1)} %get-tuple-element.13), calls=%async_computation | async-start | bytes 655360 | tf_op jit(solution)/shard_map/all_to_all | solution.py:395
  89.6 8.1 %attend.3.sums_in = f32[1280,128]{1,0:T(8,128)S(1)} custom-call(s32[1]{0:T(128)} %get-tuple-element.65.flag_ref, s32[5]{0:T(128)S(1)} %get-tuple-element.20.count_ref, s32[80]{0:T(128)S(1)} %reshape.388.work_ref, f32[80]{0:T(128)S(1)} %reshape.389.base_ref, s32[8]{0:T(128)S(1)} %pad_add_fusion.13.apart_ref, f32[24]{0:T(128)S(1)} %fusion.25.steps_ref, ...), custom_call_target="tpu_custom_call" | custom-call | flops 2684354560 | bytes 5242880 | tf_op jit(solution)/shard_map/attend/pallas_call | solution.py:265
  100.0 6.4 %all-to-all-done.tie_ref.gate_ref = bf16[8,160,128]{2,1,0:T(8,128)(2,1)S(1)} async-done(((bf16[8,160,128]{2,1,0:T(8,128)(2,1)}), bf16[8,160,128]{2,1,0:T(8,128)(2,1)S(1)}, u32[]{:S(2)}, u32[]{:S(2)}) %all-to-all-start) | async-done | bytes 327712 | tf_op jit(solution)/shard_map/all_to_all | solution.py:395
  107.5 7.9 %attend.4.sums_in = f32[1280,128]{1,0:T(8,128)S(1)} custom-call(s32[2]{0:T(128)S(1)} %slice.191.flag_ref, s32[10]{0:T(128)S(1)} %reshape.384.count_ref, s32[160]{0:T(256)S(1)} %reshape.385.work_ref, f32[160]{0:T(256)S(1)} %reshape.386.base_ref, s32[8]{0:T(128)S(1)} %pad_add_fusion.12.apart_ref, f32[24]{0:T(128)S(1)} %fusion.25.steps_ref, ...), custom_call_target="tpu_custom_call" | custom-call | flops 5368709120 | bytes 10485760 | tf_op jit(solution)/shard_map/attend/pallas_call | solution.py:265
  115.5 4.5 %attend.5 = bf16[8,160,128]{2,1,0:T(8,128)(2,1)S(1)} custom-call(s32[1]{0:T(128)} %get-tuple-element.66.flag_ref, s32[5]{0:T(128)S(1)} %get-tuple-element.21.count_ref, s32[80]{0:T(128)S(1)} %reshape.382.work_ref, f32[80]{0:T(128)S(1)} %reshape.383.base_ref, s32[8]{0:T(128)S(1)} %pad_add_fusion.11.apart_ref, f32[24]{0:T(128)S(1)} %fusion.25.steps_ref, ...), custom_call_target="tpu_custom_call" | custom-call | flops 2684354560 | bytes 5242880 | tf_op jit(solution)/shard_map/attend/pallas_call | solution.py:265
  120.0 15.9 %all_to_all.10.att_ref = bf16[8,160,128]{2,1,0:T(8,128)(2,1)S(1)} all-to-all(bf16[8,160,128]{2,1,0:T(8,128)(2,1)S(1)} %attend.5), channel_id=1, replica_groups={{0,1,2,3,4,5,6,7},{8,9,10,11,12,13,14,15},{16,17,18,19,20,21,22,23},{24..., dimensions={0} | all-to-all | bytes 655360 | tf_op jit(solution)/shard_map/all_to_all | solution.py:399
  135.9 1.6 %copy-done = bf16[1024,1024]{1,0:T(8,128)(2,1)S(1)} copy-done((bf16[1024,1024]{1,0:T(8,128)(2,1)S(1)}, bf16[1024,1024]{1,0:T(8,128)(2,1)}, u32[]{:S(2)}) %copy-start) | copy-done | bytes 2097176
  137.5 1.6 %finish.1 = (bf16[1,128,1024]{2,1,0:T(8,128)(2,1)}, bf16[1,32,1024]{2,1,0:T(8,128)(2,1)}) custom-call(bf16[1,128,1024]{2,1,0:T(8,128)(2,1)S(1)} %copy-done.1, bf16[1,32,1024]{2,1,0:T(8,128)(2,1)S(1)} %copy-done.3, bf16[1024,1024]{1,0:T(8,128)(2,1)S(1)} %copy-done, bf16[8,160,128]{2,1,0:T(8,128)(2,1)S(1)} %all_to_all.10.att_ref, ...), custom_call_target="tpu_custom_call" | custom-call | flops 335544320 | bytes 4194304 | tf_op jit(solution)/shard_map/finish/pallas_call | solution.py:292
  (142 shorter events, 28.4 us)
Async XLA Ops:
  7.2 63.0 %all-gather.6.cloned.1.call-start = ((), (), s32[]{:S(2)}) async-start(), calls=%async_computation.3 | async-start | bytes 2949120 | tf_op jit(solution)/shard_map/all_gather | solution.py:332
  9.2 60.9 %copy-start.5 = (bf16[128,1024]{1,0:T(8,128)(2,1)S(1)}, bf16[128,1024]{1,0:T(8,128)(2,1)}, u32[]{:S(2)}) copy-start(bf16[128,1024]{1,0:T(8,128)(2,1)} %refs_6_.1) | copy-start | bytes 786436
  9.2 126.6 %all-gather.4.cloned.1.call-start = ((), (), s32[]{:S(2)}) async-start(), calls=%async_computation.2 | async-start | bytes 2359296 | tf_op jit(solution)/shard_map/all_gather | solution.py:391
  10.2 33.2 %collective-permute-start = (bf16[256,128]{1,0:T(8,128)(2,1)S(1)}, bf16[256,128]{1,0:T(8,128)(2,1)S(1)}, u32[]{:S(2)}, u32[]{:S(2)}) collective-permute-start(bf16[256,128]{1,0:T(8,128)(2,1)S(1)} %dynamic_slice.6), channel_id=1, source_target_pairs={{0,128},{1,129},{2,130},{3,131},{8,136},{9,137},{10,138},{11,139},... | collective-permute-start | bytes 196616 | tf_op jit(solution)/shard_map/ppermute | solution.py:58
  10.9 9.4 %collective-permute-start.8 = (s32[1,256]{1,0:T(1,128)}, s32[1,256]{1,0:T(1,128)S(1)}, u32[]{:S(2)}, u32[]{:S(2)}) collective-permute-start(s32[1,256]{1,0:T(1,128)} %get-tuple-element.11), channel_id=1, source_target_pairs={{0,1},{1,0},{2,3},{3,2},{4,5},{5,4},{6,7},{7,6},{8,9},{9,8},{10,11... | collective-permute-start | bytes 3080 | tf_op jit(solution)/shard_map/ppermute | solution.py:339
  20.9 4.9 %collective-permute-start.9 = (s32[2,256]{1,0:T(2,128)S(1)}, s32[2,256]{1,0:T(2,128)S(1)}, u32[]{:S(2)}, u32[]{:S(2)}) collective-permute-start(s32[2,256]{1,0:T(2,128)S(1)} %pad_add_fusion.7), channel_id=1, source_target_pairs={{0,2},{1,3},{2,0},{3,1},{4,6},{5,7},{6,4},{7,5},{8,10},{9,11},{10,... | collective-permute-start | bytes 6152 | tf_op jit(solution)/shard_map/ppermute | solution.py:339
  25.9 11.7 %collective-permute-start.10 = (s32[4,256]{1,0:T(4,128)S(1)}, s32[4,256]{1,0:T(4,128)S(1)}, u32[]{:S(2)}, u32[]{:S(2)}) collective-permute-start(s32[4,256]{1,0:T(4,128)S(1)} %pad_add_fusion.6), channel_id=1, source_target_pairs={{0,4},{1,5},{2,6},{3,7},{4,0},{5,1},{6,2},{7,3},{8,12},{9,13},{10,... | collective-permute-start | bytes 12296 | tf_op jit(solution)/shard_map/ppermute | solution.py:339
  37.6 4.4 %collective-permute-start.11 = (s32[8,128]{1,0:T(8,128)S(1)}, s32[8,128]{1,0:T(8,128)S(1)}, u32[]{:S(2)}, u32[]{:S(2)}) collective-permute-start(s32[8,128]{1,0:T(8,128)S(1)} %fusion.5), channel_id=1, source_target_pairs={{0,8},{1,9},{2,10},{3,11},{4,12},{5,13},{6,14},{7,15},{8,0},{9,1},... | collective-permute-start | bytes 12296 | tf_op jit(solution)/shard_map/ppermute | solution.py:339
  42.1 5.2 %collective-permute-start.12 = (s32[16,128]{1,0:T(8,128)S(1)}, s32[16,128]{1,0:T(8,128)S(1)}, u32[]{:S(2)}, u32[]{:S(2)}) collective-permute-start(s32[16,128]{1,0:T(8,128)S(1)} %pad_add_fusion.4), channel_id=1, source_target_pairs={{0,16},{1,17},{2,18},{3,19},{4,20},{5,21},{6,22},{7,23},{8,24},{9,... | collective-permute-start | bytes 24584 | tf_op jit(solution)/shard_map/ppermute | solution.py:339
  43.4 6.9 %collective-permute-start.2 = (bf16[2,256,128]{2,1,0:T(8,128)(2,1)S(1)}, bf16[2,256,128]{2,1,0:T(8,128)(2,1)S(1)}, u32[]{:S(2)}, u32[]{:S(2)}) collective-permute-start(bf16[2,256,128]{2,1,0:T(8,128)(2,1)S(1)} %pad_maximum_fusion.1), channel_id=1, source_target_pairs={{0,32},{1,33},{2,34},{3,35},{8,40},{9,41},{10,42},{11,43},{16,48},... | collective-permute-start | bytes 393224 | tf_op jit(solution)/shard_map/ppermute | solution.py:58
  44.7 8.1 %collective-permute-start.3 = (bf16[2,256,128]{2,1,0:T(8,128)(2,1)S(1)}, bf16[2,256,128]{2,1,0:T(8,128)(2,1)S(1)}, u32[]{:S(2)}, u32[]{:S(2)}) collective-permute-start(bf16[2,256,128]{2,1,0:T(8,128)(2,1)S(1)} %pad_maximum_fusion.1), channel_id=1, source_target_pairs={{0,96},{1,97},{2,98},{3,99},{8,104},{9,105},{10,106},{11,107},{16,... | collective-permute-start | bytes 393224 | tf_op jit(solution)/shard_map/ppermute | solution.py:58
  46.0 6.8 %collective-permute-start.1 = (bf16[2,256,128]{2,1,0:T(8,128)(2,1)S(1)}, bf16[2,256,128]{2,1,0:T(8,128)(2,1)S(1)}, u32[]{:S(2)}, u32[]{:S(2)}) collective-permute-start(bf16[2,256,128]{2,1,0:T(8,128)(2,1)S(1)} %pad_maximum_fusion.1), channel_id=1, source_target_pairs={{0,64},{1,65},{2,66},{3,67},{8,72},{9,73},{10,74},{11,75},{16,80},... | collective-permute-start | bytes 393224 | tf_op jit(solution)/shard_map/ppermute | solution.py:58
  52.9 7.7 %collective-permute-start.4 = (bf16[4,256,128]{2,1,0:T(8,128)(2,1)S(1)}, bf16[4,256,128]{2,1,0:T(8,128)(2,1)S(1)}, u32[]{:S(2)}, u32[]{:S(2)}) collective-permute-start(bf16[4,256,128]{2,1,0:T(8,128)(2,1)S(1)} %pad_maximum_fusion.refs_1_), channel_id=1, source_target_pairs={{0,8},{1,9},{2,10},{3,11},{4,12},{5,13},{6,14},{7,15},{8,16},{9,17... | collective-permute-start | bytes 786440 | tf_op jit(solution)/shard_map/ppermute | solution.py:43
  55.6 8.1 %collective-permute-start.5 = (bf16[4,256,128]{2,1,0:T(8,128)(2,1)S(1)}, bf16[4,256,128]{2,1,0:T(8,128)(2,1)S(1)}, u32[]{:S(2)}, u32[]{:S(2)}) collective-permute-start(bf16[4,256,128]{2,1,0:T(8,128)(2,1)S(1)} %pad_maximum_fusion.refs_1_), channel_id=1, source_target_pairs={{0,24},{1,25},{2,26},{3,27},{4,28},{5,29},{6,30},{7,31},{8,0},{9,1... | collective-permute-start | bytes 786440 | tf_op jit(solution)/shard_map/ppermute | solution.py:43
  60.7 5.5 %collective-permute-start.6 = (bf16[2,256,128]{2,1,0:T(8,128)(2,1)S(1)}, bf16[2,256,128]{2,1,0:T(8,128)(2,1)S(1)}, u32[]{:S(2)}, u32[]{:S(2)}) collective-permute-start(bf16[2,256,128]{2,1,0:T(8,128)(2,1)S(1)} %slice.211), channel_id=1, source_target_pairs={{0,8},{1,9},{2,10},{3,11},{4,12},{5,13},{6,14},{7,15},{8,16},{9,17... | collective-permute-start | bytes 393224 | tf_op jit(solution)/shard_map/ppermute | solution.py:43
  63.7 6.4 %collective-permute-start.7 = (bf16[2,256,128]{2,1,0:T(8,128)(2,1)S(1)}, bf16[2,256,128]{2,1,0:T(8,128)(2,1)S(1)}, u32[]{:S(2)}, u32[]{:S(2)}) collective-permute-start(bf16[2,256,128]{2,1,0:T(8,128)(2,1)S(1)} %slice.212), channel_id=1, source_target_pairs={{0,24},{1,25},{2,26},{3,27},{4,28},{5,29},{6,30},{7,31},{8,0},{9,1... | collective-permute-start | bytes 393224 | tf_op jit(solution)/shard_map/ppermute | solution.py:43
  71.9 17.6 %copy-start.2 = (s32[1280,128]{1,0:T(8,128)S(1)}, s32[1280,128]{1,0:T(8,128)}, u32[]{:S(2)}) copy-start(s32[1280,128]{1,0:T(8,128)} %prepare.1.col_ref) | copy-start | bytes 1966084
  78.6 19.1 %collective-permute-start.13 = (bf16[1024,256]{1,0:T(8,128)(2,1)S(1)}, bf16[1024,256]{1,0:T(8,128)(2,1)S(1)}, u32[]{:S(2)}, u32[]{:S(2)}) collective-permute-start(bf16[1024,256]{1,0:T(8,128)(2,1)S(1)} %get-tuple-element.15.rest_0_), channel_id=1, source_target_pairs={{0,8},{1,9},{2,10},{3,11},{4,12},{5,13},{6,14},{7,15},{8,16},{9,17... | collective-permute-start | bytes 1572872 | tf_op jit(solution)/shard_map/ppermute | solution.py:43
  78.7 19.6 %collective-permute-start.14 = (bf16[1024,256]{1,0:T(8,128)(2,1)S(1)}, bf16[1024,256]{1,0:T(8,128)(2,1)S(1)}, u32[]{:S(2)}, u32[]{:S(2)}) collective-permute-start(bf16[1024,256]{1,0:T(8,128)(2,1)S(1)} %get-tuple-element.15.rest_0_), channel_id=1, source_target_pairs={{0,24},{1,25},{2,26},{3,27},{4,28},{5,29},{6,30},{7,31},{8,0},{9,1... | collective-permute-start | bytes 1572872 | tf_op jit(solution)/shard_map/ppermute | solution.py:43
  80.7 25.7 %all-to-all-start = ((bf16[8,160,128]{2,1,0:T(8,128)(2,1)}), bf16[8,160,128]{2,1,0:T(8,128)(2,1)S(1)}, u32[]{:S(2)}, u32[]{:S(2)}) async-start(bf16[8,160,128]{2,1,0:T(8,128)(2,1)} %get-tuple-element.13), calls=%async_computation | async-start | bytes 655360 | tf_op jit(solution)/shard_map/all_to_all | solution.py:395
  97.8 17.7 %collective-permute-start.15 = (bf16[512,256]{1,0:T(8,128)(2,1)S(1)}, bf16[512,256]{1,0:T(8,128)(2,1)S(1)}, u32[]{:S(2)}, u32[]{:S(2)}) collective-permute-start(bf16[512,256]{1,0:T(8,128)(2,1)S(1)} %slice.231), channel_id=1, source_target_pairs={{0,8},{1,9},{2,10},{3,11},{4,12},{5,13},{6,14},{7,15},{8,16},{9,17... | collective-permute-start | bytes 786440 | tf_op jit(solution)/shard_map/ppermute | solution.py:43
  98.6 16.9 %collective-permute-start.16 = (bf16[512,256]{1,0:T(8,128)(2,1)S(1)}, bf16[512,256]{1,0:T(8,128)(2,1)S(1)}, u32[]{:S(2)}, u32[]{:S(2)}) collective-permute-start(bf16[512,256]{1,0:T(8,128)(2,1)S(1)} %slice.232), channel_id=1, source_target_pairs={{0,24},{1,25},{2,26},{3,27},{4,28},{5,29},{6,30},{7,31},{8,0},{9,1... | collective-permute-start | bytes 786440 | tf_op jit(solution)/shard_map/ppermute | solution.py:43
  115.5 20.4 %copy-start.1 = (bf16[1,128,1024]{2,1,0:T(8,128)(2,1)S(1)}, bf16[1,128,1024]{2,1,0:T(8,128)(2,1)}, u32[]{:S(2)}) copy-start(bf16[1,128,1024]{2,1,0:T(8,128)(2,1)} %hist_ref.3) | copy-start | bytes 786436
  115.5 20.4 %copy-start.3 = (bf16[1,32,1024]{2,1,0:T(8,128)(2,1)S(1)}, bf16[1,32,1024]{2,1,0:T(8,128)(2,1)}, u32[]{:S(2)}) copy-start(bf16[1,32,1024]{2,1,0:T(8,128)(2,1)} %cand_ref.3) | copy-start | bytes 196612
  (4 other events, 5.3 us)
Sparse Core Ops, SparseCore 0:
  9.8 42.9 all-gather.5
  75.4 48.6 all-gather.3

commit v5 on v4

v5 whole, which is shorter than its diff:
```python
import functools

import jax
import jax.numpy as jnp
from jax import lax
from jax.experimental import pallas as pl
from jax.experimental.pallas import tpu as pltpu
from jax.sharding import PartitionSpec as P

F32, BF16, I32 = jnp.float32, jnp.bfloat16, jnp.int32
ZL, NY, NX, ZH, NC = 2, 4, 4, 4, 2
NB, NS = ZL * NY, NX * ZH * NC
OFF = (0, -1, 1, 2)
HEADS, HD, D = 8, 128, 1024
HIST, CAND = 128, 32
ROWS = HIST + CAND
NP = ZH * NC
QH, QC = NP * HIST, NP * CAND
QROWS = QH + QC
KEYS = NP * HIST
LENGTH = NS * HIST
LEVELS = 12
MASKED = -1e30
SAME_X = [[x * NP + p for p in range(NP)] for x in range(NX)]
VM = pl.BlockSpec(memory_space=pltpu.VMEM)
SM = pl.BlockSpec(memory_space=pltpu.SMEM)
HBM = pl.BlockSpec(memory_space=pl.ANY)
DEPTH = D // NX


def params(mib):
    return pltpu.CompilerParams(vmem_limit_bytes=mib << 20)


def position():
    seq = lax.axis_index("seq")
    return seq // (ZH * NC), seq // NC % ZH, seq % NC


def seq_perm(dx=0, dz=0, flip=False):
    pairs = []
    for s in range(NS):
        x, z, c = s // (ZH * NC), s // NC % ZH, s % NC
        t = ((x + dx) % NX * ZH + (z + dz) % ZH) * NC + (c ^ int(flip))
        pairs.append((s, t))
    return pairs


def shift(array, dx=0, dz=0, flip=False):
    return lax.ppermute(array, "seq", seq_perm(dx, dz, flip))


def norm_kernel(hist_ref, cand_ref, events_ref, requests_ref, proj_ref, out_ref, times_ref, shards_ref, part_ref, sem):
    x, z, core = position()
    column = pl.multiple_of((NC * z + core) % 4 * HD, HD)
    copy = pltpu.make_async_copy(
        proj_ref.at[pl.ds(pl.multiple_of(x * DEPTH, DEPTH), DEPTH), pl.ds(column, HD)], part_ref, sem
    )
    copy.start()
    for ref, first, count in ((hist_ref, 0, HIST), (cand_ref, HIST, CAND)):
        rows = ref[0].astype(F32)
        rows = rows - jnp.mean(rows, axis=-1, keepdims=True)
        spread = jnp.mean(rows * rows, axis=-1, keepdims=True)
        out_ref[first : first + count, :] = (rows * lax.rsqrt(spread + 1e-6)).astype(BF16)
    times_ref[...] = jnp.zeros_like(times_ref)
    times_ref[:, :HIST] = events_ref[...]
    times_ref[:, HIST:ROWS] = requests_ref[...]
    copy.wait()
    for b in range(NB):
        shards_ref[b] = part_ref[...]


def norm_rows(hist, cand, events, requests, w_proj):
    return pl.pallas_call(
        norm_kernel,
        out_shape=[
            jax.ShapeDtypeStruct((ROWS, D), BF16),
            jax.ShapeDtypeStruct((1, 2 * HIST), I32),
            jax.ShapeDtypeStruct((NB, DEPTH, HD), BF16),
        ],
        in_specs=[VM] * 4 + [HBM],
        out_specs=[VM] * 3,
        scratch_shapes=[pltpu.VMEM((DEPTH, HD), BF16), pltpu.SemaphoreType.DMA(())],
        cost_estimate=pl.CostEstimate(flops=8 * ROWS * D, bytes_accessed=4 * ROWS * D, transcendentals=0),
        name="norm_rows",
    )(hist, cand, events, requests, w_proj)


def merge_kernel(mine_ref, other_ref, wout_ref, *rest, bit):
    out_ref, wout_out = rest[-2:]
    count = mine_ref.shape[0]
    first = lax.axis_index("seq") >> bit & 1 == 0
    out_ref[:count] = jnp.where(first, mine_ref[...], other_ref[...])
    out_ref[count:] = jnp.where(first, other_ref[...], mine_ref[...])
    wout_out[...] = wout_ref[...]


def merge(mine, other, bit, w_out, ties):
    return pl.pallas_call(
        functools.partial(merge_kernel, bit=bit),
        out_shape=[
            jax.ShapeDtypeStruct((2 * mine.shape[0], mine.shape[1]), mine.dtype),
            jax.ShapeDtypeStruct(w_out.shape, w_out.dtype),
        ],
        in_specs=[VM] * 3 + [HBM] * len(ties),
        out_specs=[VM] * 2,
        cost_estimate=pl.CostEstimate(flops=1 << 12, bytes_accessed=1 << 16, transcendentals=0),
        name="merge",
    )(mine, other, w_out, *ties)


def prepare_kernel(tq_ref, col_ref):
    for i in range(QROWS // 128):
        col_ref[i * 128 : (i + 1) * 128, :] = jnp.transpose(jnp.broadcast_to(tq_ref[i : i + 1, :], (128, 128)))


def prepare(tq):
    return pl.pallas_call(
        prepare_kernel,
        out_shape=jax.ShapeDtypeStruct((QROWS, 128), I32),
        in_specs=[VM],
        out_specs=VM,
        cost_estimate=pl.CostEstimate(flops=2 << 20, bytes_accessed=1 << 20, transcendentals=0),
        name="prepare",
    )(tq)


def half_silu(half):
    return half + half * jnp.tanh(half)


HALF = NP // 2


HALF = NP // 2


def project_kernel(rows_ref, *refs):
    parts, (qh_ref, qc_ref, kv_ref, own_ref, gate_ref, rows, weights, sems) = refs[:NX], refs[NX:]
    x = position()[0]
    hist, cand = HALF * HIST, HALF * CAND
    copies, fetches = [], []
    for m in range(NX):
        at = pl.multiple_of((x + OFF[m]) % NX * DEPTH, DEPTH)
        for kind in range(4):
            block = weights.at[pl.ds(at, DEPTH), kind * HD : (kind + 1) * HD]
            fetches.append(pltpu.make_async_copy(parts[m].at[kind], block, sems.at[2 + m, kind]))
            fetches[-1].start()
    for place in range(NP):
        step, at = place // HALF, place % HALF
        copies.append(
            (
                pltpu.make_async_copy(
                    rows_ref.at[place, :HIST, :], rows.at[step, at * HIST : (at + 1) * HIST, :], sems.at[0, place]
                ),
                pltpu.make_async_copy(
                    rows_ref.at[place, HIST:, :],
                    rows.at[step, hist + at * CAND : hist + (at + 1) * CAND, :],
                    sems.at[1, place],
                ),
            )
        )
        for copy in copies[-1]:
            copy.start()
    for fetch in fetches:
        fetch.wait()
    for step in range(NP // HALF):
        for pair in copies[step * HALF : (step + 1) * HALF]:
            for copy in pair:
                copy.wait()
        mixed = jnp.dot(rows[step], weights[:, 2 * HD :], preferred_element_type=F32)
        mixed = half_silu(0.5 * mixed)
        queries, keys = mixed[:, :HD], mixed[:, HD:]
        scaled = (queries * (0.5 * HD**-0.5)).astype(BF16)
        hists, cands = slice(step * hist, (step + 1) * hist), slice(step * cand, (step + 1) * cand)
        qh_ref[hists, :] = scaled[:hist]
        qc_ref[cands, :] = scaled[hist:]
        kv_ref[hists, :HD] = keys[:hist].astype(BF16)
        dots = queries[hist:].astype(BF16).astype(F32) * keys[hist:].astype(BF16).astype(F32)
        dots = jnp.sum(dots, axis=-1, keepdims=True)
        own = half_silu(dots * (0.5 * HD**-0.5)).astype(BF16).astype(F32)
        mixed = jnp.dot(rows[step], weights[:, : 2 * HD], preferred_element_type=F32)
        mixed = half_silu(0.5 * mixed).astype(BF16)
        kv_ref[hists, HD:] = mixed[:hist, HD:]
        own_ref[cands, :] = own * mixed[hist:, HD:].astype(F32)
        for at in range(HALF):
            place = step * HALF + at
            gate_ref[place, :HIST, :] = mixed[at * HIST : (at + 1) * HIST, :HD]
            gate_ref[place, HIST:, :] = mixed[hist + at * CAND : hist + (at + 1) * CAND, :HD]


def project(rows, parts):
    return pl.pallas_call(
        project_kernel,
        in_specs=[HBM] * (1 + NX),
        out_specs=[VM] * 5,
        scratch_shapes=[
            pltpu.VMEM((NP // HALF, HALF * ROWS, D), BF16),
            pltpu.VMEM((D, 4 * HD), BF16),
            pltpu.SemaphoreType.DMA((2 + NX, NP)),
        ],
        out_shape=[
            jax.ShapeDtypeStruct((QH, HD), BF16),
            jax.ShapeDtypeStruct((QC, HD), BF16),
            jax.ShapeDtypeStruct((KEYS, 2 * HD), BF16),
            jax.ShapeDtypeStruct((QC, HD), F32),
            jax.ShapeDtypeStruct((NP, ROWS, HD), BF16),
        ],
        compiler_params=params(56),
        cost_estimate=pl.CostEstimate(flops=2 * QROWS * D * 4 * HD, bytes_accessed=6 << 20, transcendentals=QROWS * 4 * HD),
        name="project",
    )(rows, *parts)


BLOCK = 256
TILES = (QROWS // 128) * NP
STEPS = QROWS // BLOCK
STEP_TILES = TILES // STEPS


def attend_kernel(count_ref, work_ref, base_ref, steps_ref, qh_ref, qc_ref, sums_in, col_ref, *rest, fresh, last, chunks, start):
    arrays = sum(len(chunk) for chunk in chunks)
    gate_ref = rest[-4]
    kvs, tks = list(rest[:arrays]), rest[arrays : arrays + len(chunks)]
    out_ref, sums_ref, half_ref = rest[-3:]
    if fresh:
        sums_ref[:QH, :] = jnp.zeros((QH, HD), F32)
        sums_ref[QH:, :] = sums_in[...]
    else:
        sums_ref[...] = sums_in[...]
    row = lax.broadcasted_iota(I32, (128, 128), 0)
    lane = lax.broadcasted_iota(I32, (128, 128), 1)
    x = position()[0]
    froms = [(x + OFF[start + n]) % NX for n in range(len(chunks))]

    def scores(n, block, slot):
        first = block * BLOCK
        begin = 0
        for kv in parts[n]:
            keys = kv.shape[0]
            queries = qc_ref[first - QH : first - QH + BLOCK, :] if first >= QH else qh_ref[first : first + BLOCK, :]
            half = lax.dot_general(
                queries, kv[:, :HD], (((1,), (1,)), ((), ())), preferred_element_type=F32
            )
            for i in range(BLOCK // 128):
                for j in range(keys // 128):
                    at = (start + n) * TILES + (block * (BLOCK // 128) + i) * NP + begin // 128 + j
                    half_ref[slot, i * 128 : (i + 1) * 128, begin + j * 128 : begin + (j + 1) * 128] = (
                        half[i * 128 : (i + 1) * 128, j * 128 : (j + 1) * 128] + base_ref[at]
                    )
            begin += keys

    def correct(n, block, slot):
        is_cand = block * BLOCK >= QH

        def tile(k, carry):
            code = work_ref[(start + n) * TILES + block * STEP_TILES + k]
            i, j = (code >> 3) & 1, code & 7
            time_low, time_high, place_low, place_high = [(code >> bit) & 15 for bit in (4, 8, 12, 16)]
            if True:
                rows = pl.ds(pl.multiple_of(i * 128, 128), 128)
                columns = pl.ds(pl.multiple_of(j * 128, 128), 128)
                first = pl.multiple_of(block * BLOCK + i * 128, 128)
                value = half_ref[slot, rows, columns]
                gap = col_ref[pl.ds(first, 128), :] - tks[n][pl.ds(j, 1), :]

                def time_step(level, value):
                    return value + jnp.where(gap >= (1 << (2 * level)), steps_ref[level], 0.0)

                value = lax.fori_loop(time_low, time_high, time_step, value)
                if is_cand:
                    gap2 = (LENGTH - froms[n] * KEYS - j * 128) - lane
                else:
                    gap2 = ((x - froms[n]) * KEYS + (block * (BLOCK // 128) + i - j) * 128) + row - lane

                def place_step(level, value):
                    return value + jnp.where(gap2 >= (1 << level), steps_ref[LEVELS + level], 0.0)

                value = lax.fori_loop(place_low, place_high, place_step, value)
                if not is_cand:
                    value = jnp.where(gap2 >= 0, value, MASKED)
                half_ref[slot, rows, columns] = value

            return carry

        lax.fori_loop(0, count_ref[(start + n) * STEPS + block], tile, 0)

    def combine(n, block, slot):
        first = block * BLOCK
        begin = 0
        total = sums_ref[first : first + BLOCK, :]
        for kv in parts[n]:
            keys = kv.shape[0]
            weights = half_silu(half_ref[slot, :, begin : begin + keys]).astype(BF16)
            total = total + jnp.dot(weights, kv[:, HD:], preferred_element_type=F32)
            begin += keys
        sums_ref[first : first + BLOCK, :] = total

    def sweep(n, blocks):
        for k, block in enumerate(blocks):
            scores(n, block, k % 2)
            if k > 0:
                combine(n, blocks[k - 1], (k - 1) % 2)
            correct(n, block, k % 2)
        combine(n, blocks[-1], (len(blocks) - 1) % 2)

    parts = []
    for chunk in chunks:
        parts.append([kvs.pop(0) for _ in chunk])
    for n in range(len(chunks)):

        @pl.when(froms[n] <= x)
        def _():
            sweep(n, list(range(QROWS // BLOCK)))

        @pl.when(froms[n] > x)
        def _():
            sweep(n, [QROWS // BLOCK - 1])

    if last:
        for place in range(NP):
            out_ref[place, :HIST, :HD] = sums_ref[place * HIST : (place + 1) * HIST, :].astype(BF16)
            out_ref[place, HIST:, :HD] = sums_ref[QH + place * CAND : QH + (place + 1) * CAND, :].astype(BF16)
            out_ref[place, :, HD:] = gate_ref[place]
    else:
        out_ref[...] = sums_ref[...]


def attend(tables, queries, sums, col, chunks, tks, start, gates=None):
    fresh, last = start == 0, gates is not None
    gates = [gates] if last else []
    kvs = [kv for chunk in chunks for kv in chunk]
    shapes = tuple(tuple(kv.shape[0] for kv in chunk) for chunk in chunks)
    keys = sum(kv.shape[0] for kv in kvs)
    return pl.pallas_call(
        functools.partial(attend_kernel, fresh=fresh, last=last, chunks=shapes, start=start),
        in_specs=[SM] * 4 + [VM] * (4 + len(kvs) + len(tks) + len(gates)),
        out_specs=VM,
        out_shape=jax.ShapeDtypeStruct((NP, ROWS, 2 * HD), BF16) if last else jax.ShapeDtypeStruct((QROWS, HD), F32),
        scratch_shapes=[pltpu.VMEM((QROWS, HD), F32), pltpu.VMEM((2, BLOCK, KEYS), F32)],
        compiler_params=params(16),
        cost_estimate=pl.CostEstimate(
            flops=16 * QROWS * keys * HD, bytes_accessed=4 * QROWS * keys, transcendentals=QROWS * keys
        ),
        name="attend",
    )(*tables, *queries, sums, col, *kvs, *tks, *gates)


def finish_kernel(hist_ref, cand_ref, pair_ref, w_hbm, hist_out, cand_out, w_ref, sem):
    copy = pltpu.make_async_copy(w_hbm, w_ref, sem)
    copy.start()
    parts = [pair_ref[h, :, :HD].astype(F32) for h in range(HEADS)]
    center = sum(jnp.sum(part, axis=-1, keepdims=True) for part in parts) * (1.0 / D)
    parts = [part - center for part in parts]
    spread = sum(jnp.sum(part * part, axis=-1, keepdims=True) for part in parts) * (1.0 / D)
    scale = lax.rsqrt(spread + 1e-6)
    parts = [(part * scale * pair_ref[h, :, HD:].astype(F32)).astype(BF16) for h, part in enumerate(parts)]
    copy.wait()
    total = jnp.dot(jnp.concatenate(parts, axis=1), w_ref[...], preferred_element_type=F32)
    hist_out[0] = (hist_ref[0].astype(F32) + total[:HIST]).astype(BF16)
    cand_out[0] = (cand_ref[0].astype(F32) + total[HIST:]).astype(BF16)


def finish(hist, cand, w_out, pairs):
    return pl.pallas_call(
        finish_kernel,
        out_shape=[
            jax.ShapeDtypeStruct((1, HIST, D), BF16),
            jax.ShapeDtypeStruct((1, CAND, D), BF16),
        ],
        in_specs=[VM] * 3 + [HBM],
        out_specs=[VM, VM],
        scratch_shapes=[pltpu.VMEM((D, D), BF16), pltpu.SemaphoreType.DMA(())],
        compiler_params=params(56),
        cost_estimate=pl.CostEstimate(flops=2 * ROWS * D * D, bytes_accessed=4 << 20, transcendentals=0),
        name="finish",
    )(hist, cand, pairs, w_out)


def gather_weights(shards, z):
    shards = lax.all_to_all(shards, "batch", 0, 0)
    return lax.dynamic_index_in_dim(shards.reshape(4, 2, DEPTH, HD), z // 2, axis=1, keepdims=False)


def body(history, candidates, event_times, request_times, w_proj, w_out, bias_steps):
    seq = lax.axis_index("seq")
    x, z, core = position()
    head = NC * z + core
    xs = jnp.stack([(x + off) % NX for off in OFF])

    n0, t0, shards = norm_rows(history, candidates, event_times, request_times, w_proj)
    rows = lax.all_gather(n0, "seq", axis_index_groups=SAME_X)

    w0 = gather_weights(shards, z)
    w_parts = [w0, shift(w0, dx=1), shift(w0, dx=-1), shift(w0, dx=2)]

    times = t0
    order = (3, 4, 0, 1, 2)
    for bit in order:
        other = lax.ppermute(times, "seq", [(s, s ^ (1 << bit)) for s in range(NS)])
        if bit == order[-2]:
            times, w_mine = merge(times, other, bit, w_out, w_parts[1:])
            w_full = lax.all_gather(w_mine, "batch", axis=0, tiled=True)
        else:
            first = seq >> bit & 1 == 0
            times = jnp.concatenate([jnp.where(first, times, other), jnp.where(first, other, times)], axis=0)
    times = times.reshape(ZH, NC, NX, 2 * HIST).transpose(2, 0, 1, 3).reshape(NX, NP, 2 * HIST)
    t8 = jnp.sum(jnp.where((x == jnp.arange(NX))[:, None, None], times, 0), axis=0)
    k0 = t8[:, :HIST]
    tks = [jnp.sum(jnp.where((xs[m] == jnp.arange(NX))[:, None, None], times[..., :HIST], 0), axis=0) for m in range(NX)]
    cand_times = t8[:, HIST:ROWS].reshape(QC // 128, 128)

    qh, qc, kv0, own, gates = project(rows, w_parts)

    steps = 0.5 * lax.dynamic_slice(bias_steps, (0, head), (2 * LEVELS, 1))[:, 0]
    level = jnp.arange(LEVELS, dtype=I32)
    tie = (kv0[0, 0] * 0).astype(I32)
    tk = jnp.stack(tks) + tie
    tq = jnp.concatenate([k0, cand_times, jnp.zeros((6, 128), I32)], axis=0) + tie
    first_q = jnp.concatenate([k0[:, 0], jnp.min(cand_times, axis=1)]) + tie
    last_q = jnp.concatenate([k0[:, -1], jnp.max(cand_times, axis=1)]) + tie

    def passed(gap, marks):
        return jnp.sum((gap[..., None] >= marks).astype(I32), axis=-1)

    time_low = passed(first_q[None, :, None] - tk[:, None, :, -1], 4**level)
    time_high = passed(last_q[None, :, None] - tk[:, None, :, 0], 4**level)
    blocks = jnp.arange(NP, dtype=I32)
    hist_gap = ((x - xs)[:, None, None] * NP + blocks[None, :, None] - blocks[None, None, :]) * HIST
    cand_gap = LENGTH - (xs[:, None, None] * NP + blocks[None, None, :]) * HIST
    cand_gap = jnp.broadcast_to(cand_gap, (NX, QC // 128, NP))
    place_low = passed(jnp.concatenate([hist_gap, cand_gap], axis=1) - (HIST - 1), 2**level)
    place_high = passed(jnp.concatenate([hist_gap + (HIST - 1), cand_gap], axis=1), 2**level)
    hidden = jnp.concatenate([hist_gap < 0, cand_gap < 0], axis=1)
    code = time_low | (time_high << 4) | (place_low << 8) | (place_high << 12)
    mixed = ~hidden & ((time_low != time_high) | (place_low != place_high))
    number = jnp.arange(STEP_TILES, dtype=I32)
    code = (code << 4 | number.reshape(BLOCK // 128, NP)[jnp.arange(QROWS // 128) % (BLOCK // 128)]).reshape(NX, STEPS, STEP_TILES)
    mixed = mixed.reshape(NX, STEPS, STEP_TILES)
    rank = jnp.sum(jnp.where(number[None, :] < number[:, None], mixed[..., None, :].astype(I32), 0), axis=-1)
    spot = mixed[..., None] & (rank[..., None] == number)
    works = jnp.sum(jnp.where(spot, code[..., None], 0), axis=-2).reshape(NX, TILES)
    counts = jnp.sum(mixed.astype(I32), axis=-1)
    base = jnp.sum(jnp.where(time_low[..., None] > level, steps[:LEVELS], 0.0), axis=-1)
    base = base + jnp.sum(jnp.where(place_low[..., None] > level, steps[LEVELS:], 0.0), axis=-1)
    base = jnp.where(hidden, MASKED, base).reshape(NX, TILES)
    col = prepare(tq)
    tables = (counts.reshape(-1), works.reshape(-1), base.reshape(-1), steps)

    queries = (qh, qc)
    kv1, kv2 = shift(kv0, dx=1), shift(kv0, dx=-1)
    part = KEYS // 2
    kv3a, kv3b = shift(kv1[:part], dx=1), shift(kv2[part:], dx=-1)
    sums = attend(tables, queries, own, col, [[kv0]], tks[:1], 0)
    sums = attend(tables, queries, sums, col, [[kv1], [kv2]], tks[1:3], 1)
    att = attend(tables, queries, sums, col, [[kv3a, kv3b]], tks[3:], 3, gates)
    atts = lax.all_to_all(att, "seq", 0, 0, axis_index_groups=SAME_X)
    return tuple(finish(history, candidates, w_full, atts))


def solution(mesh):
    in_specs = (
        P("batch", "seq", None),
        P("batch", "seq", None),
        P("batch", "seq"),
        P("batch", "seq"),
        P(None, "batch"),
        P("batch", None),
        P(),
    )
    out_specs = (P("batch", "seq", None), P("batch", "seq", None))
    return jax.shard_map(body, mesh=mesh, in_specs=in_specs, out_specs=out_specs, check_vma=False)
```

time: 147 us -> 140 us (0.952)
  blocking collectives: 15.9 us -> 0 us
  waiting for transfers between devices: 26.7 us -> 35.2 us
  Pallas kernels: 29.3 us -> 35.4 us
  starting transfers between devices: 36.9 us -> 32.9 us
  other arithmetic: 11.2 us -> 9.19 us
    all_to_all x1 -> x0, blocking collectives: 15.9 us -> none  [body(): atts = lax.all_to_all(att, 'seq', 0, 0, axis_index_groups=SAME_X)]
    all_to_all x1 -> x2, waiting for transfers between devices: 6.42 us -> 21.2 us  [the longest x1 21.2 us: body(): atts = lax.all_to_all(att, 'seq', 0, 0, axis_index_groups=SAME_X)]
    ppermute x4 -> x0, waiting for transfers between devices: 5.52 us -> none  [from_sources(): return lax.ppermute(array, ('batch', 'seq'), source_perm(dzl, dy))]
    all_to_all x1 -> x2, starting transfers between devices: 8 us -> 13.4 us  [the longest x1 7.38 us: body(): atts = lax.all_to_all(att, 'seq', 0, 0, axis_index_groups=SAME_X)]
    ppermute x4 -> x0, starting transfers between devices: 3.91 us -> none  [from_sources(): return lax.ppermute(array, ('batch', 'seq'), source_perm(dzl, dy))]
    concatenate x6 -> x0, other arithmetic: 3.51 us -> none  [the longest x3 2.68 us: tables(): jnp.concatenate([jnp.roll((x - xs) * KEYS, -first), jnp.roll(xs * KEYS, -...]
    pallas_call x1 -> x2, Pallas kernels: 3.38 us -> 6.87 us  [the longest x1 5.14 us: project(): pl.pallas_call(project_kernel, in_specs=[HBM] * (1 + NX), out_specs=[VM]...]
    ppermute x5, starting transfers between devices: 15.1 us -> 11.9 us  [body(): other = lax.ppermute(times, 'seq', [(s, s ^ 1 << bit) for s in range(NS)])]
  transfers between devices with their start and end apart: 20 -> 16, of which waited for: 9 -> 6; matrix products, arithmetic and copies ran while one was open for 12% -> 9% of each run, Pallas kernels for 15% -> 21%
where the time goes in v5:
time: 140 us; the launch traced here: 139 us
  Pallas kernels  35.4 us (25%)
  waiting for transfers between devices  35.2 us (25%)
  starting transfers between devices  32.9 us (24%)
  between operations  15.1 us (11%)
  local copies, waits for them, and re-layouts  10.7 us (8%)
  other arithmetic  9.19 us (7%)
    all_to_all x1, waiting for transfers between devices, body(): atts = lax.all_to_all(att, 'seq', 0, 0, axis_index_groups=SAME_X)  21.2 us
    pallas_call x3, Pallas kernels, attend(): pl.pallas_call(functools.partial(attend_kernel, fresh=fresh, last=last, c...  20 us
    ppermute x5, starting transfers between devices, body(): other = lax.ppermute(times, 'seq', [(s, s ^ 1 << bit) for s in range(NS)])  11.9 us
    ppermute x7, waiting for transfers between devices, shift(): return lax.ppermute(array, 'seq', seq_perm(dx, dz, flip))  7.94 us
    ppermute x7, starting transfers between devices, shift(): return lax.ppermute(array, 'seq', seq_perm(dx, dz, flip))  7.56 us
    all_to_all x1, starting transfers between devices, body(): atts = lax.all_to_all(att, 'seq', 0, 0, axis_index_groups=SAME_X)  7.38 us
    unnamed x28, local copies, waits for them, and re-layouts  7.06 us
    all_to_all x1, starting transfers between devices, gather_weights(): shards = lax.all_to_all(shards, 'batch', 0, 0)  6.05 us
  transfers between devices with their start and end apart: 16, of which 6 were waited for; matrix products, arithmetic and copies ran while one was open for 9% of the time, Pallas kernels for 21%

profile of v5, /device:TPU:30, one launch (start us, length us, event | category | flops | bytes accessed | tf_op | source)
XLA Modules:
  0.0 138.5 jit_solution(6411281681110758102)
XLA Ops:
  7.2 2.8 %norm_rows.1 = (bf16[160,1024]{1,0:T(8,128)(2,1)}, s32[1,256]{1,0:T(1,128)}, bf16[8,256,128]{2,1,0:T(8,128)(2,1)}) custom-call(bf16[1,128,1024]{2,1,0:T(8,128)(2,1)} %hist_ref.3, bf16[1,32,1024]{2,1,0:T(8,128)(2,1)} %cand_ref.3, s32[1,128]{1,0:T(1,128)} %events_ref.1, s32[1,32]{1,0:T(1,128)} %requests_ref.1, bf16[1024,512]{1,0:T(8,128)(2,1)} %proj_ref.1), custom_call_target="tpu_custom_call" | custom-call | flops 1310720 | bytes 655360 | tf_op jit(solution)/shard_map/norm_rows/pallas_call | solution.py:74
  10.0 6.1 %all-to-all-start = ((bf16[8,256,128]{2,1,0:T(8,128)(2,1)}), bf16[8,256,128]{2,1,0:T(8,128)(2,1)S(1)}, u32[]{:S(2)}, u32[]{:S(2)}) async-start(bf16[8,256,128]{2,1,0:T(8,128)(2,1)} %get-tuple-element.13), calls=%async_computation | async-start | bytes 1048576 | tf_op jit(solution)/shard_map/all_to_all | solution.py:381
  18.2 1.5 %convert_reduce_fusion = (s32[4,10,8]{2,1,0:T(8,128)S(1)}, s32[4,10,8]{2,1,0:T(8,128)S(1)}) fusion(s32[4,10,8]{2,1,0:T(8,128)S(1)} %get-tuple-element.50, s32[12]{0:T(128)S(1)} %get-tuple-element.59, s32[4,10,8]{2,1,0:T(8,128)S(1)} %get-tuple-element.49), kind=kLoop, calls=%fused_computation.9 | loop fusion | flops 22400 | bytes 5168 | tf_op jit(solution)/shard_map/reduce_sum | solution.py:424
  20.7 1.3 collective-permute-start.1
  22.1 3.8 %collective-permute-done.1 = s32[2,256]{1,0:T(2,128)S(1)} collective-permute-done((s32[2,256]{1,0:T(2,128)S(1)}, s32[2,256]{1,0:T(2,128)S(1)}, u32[]{:S(2)}, u32[]{:S(2)}) %collective-permute-start.1) | collective-permute-done | bytes 2080 | tf_op jit(solution)/shard_map/ppermute | solution.py:400
  26.1 1.2 collective-permute-start.4
  28.2 1.2 collective-permute-start.6
  29.5 3.4 %collective-permute-start.3 = (s32[8,256]{1,0:T(8,128)S(1)}, s32[8,256]{1,0:T(8,128)S(1)}, u32[]{:S(2)}, u32[]{:S(2)}) collective-permute-start(s32[8,256]{1,0:T(8,128)S(1)} %pad_add_fusion.4.mine_ref), channel_id=1, source_target_pairs={{0,2},{1,3},{2,0},{3,1},{4,6},{5,7},{6,4},{7,5},{8,10},{9,11},{10,... | collective-permute-start | bytes 24584 | tf_op jit(solution)/shard_map/ppermute | solution.py:400
  32.8 1.8 %collective-permute-done.3.other_ref = s32[8,256]{1,0:T(8,128)S(1)} collective-permute-done((s32[8,256]{1,0:T(8,128)S(1)}, s32[8,256]{1,0:T(8,128)S(1)}, u32[]{:S(2)}, u32[]{:S(2)}) %collective-permute-start.3) | collective-permute-done | bytes 8224 | tf_op jit(solution)/shard_map/ppermute | solution.py:400
  35.3 7.3 %collective-permute-done.5.rest_1_.refs_2_ = bf16[4,256,128]{2,1,0:T(8,128)(2,1)S(1)} collective-permute-done((bf16[4,256,128]{2,1,0:T(8,128)(2,1)S(1)}, bf16[4,256,128]{2,1,0:T(8,128)(2,1)S(1)}, u32[]{:S(2)}, u32[]{:S(2)}) %collective-permute-start.5) | collective-permute-done | bytes 262176 | tf_op jit(solution)/shard_map/ppermute | solution.py:50
  43.9 1.7 %merge.1 = (s32[16,256]{1,0:T(8,128)}, bf16[128,1024]{1,0:T(8,128)(2,1)}) custom-call(s32[8,256]{1,0:T(8,128)} %copy-done.12, s32[8,256]{1,0:T(8,128)} %copy-done.13, bf16[128,1024]{1,0:T(8,128)(2,1)} %wout_ref.1, bf16[4,256,128]{2,1,0:T(8,128)(2,1)} %copy-done.9, bf16[4,256,128]{2,1,0:T(8,128)(2,1)} %copy-done.10, bf16[4,256,128]{2,1,0:T(8,128)(2,1)} %copy-done.11), custom_call_target="tpu_custom_call" | custom-call | flops 4096 | bytes 65536 | tf_op jit(solution)/shard_map/merge/pallas_call | solution.py:99
  45.7 6.3 %collective-permute-start.7 = (s32[16,256]{1,0:T(8,128)}, s32[16,256]{1,0:T(8,128)S(1)}, u32[]{:S(2)}, u32[]{:S(2)}) collective-permute-start(s32[16,256]{1,0:T(8,128)} %get-tuple-element.14), channel_id=1, source_target_pairs={{0,4},{1,5},{2,6},{3,7},{4,0},{5,1},{6,2},{7,3},{8,12},{9,13},{10,... | collective-permute-start | bytes 49160 | tf_op jit(solution)/shard_map/ppermute | solution.py:400
  55.7 5.1 %project.1 = (bf16[1024,128]{1,0:T(8,128)(2,1)}, bf16[256,128]{1,0:T(8,128)(2,1)}, bf16[1024,256]{1,0:T(8,128)(2,1)}, f32[256,128]{1,0:T(8,128)}, bf16[8,160,128]{2,1,0:T(8,128)(2,1)}) custom-call(bf16[8,160,1024]{2,1,0:T(8,128)(2,1)} %bitcast.38, bf16[4,256,128]{2,1,0:T(8,128)(2,1)} %copy-done.8, bf16[4,256,128]{2,1,0:T(8,128)(2,1)} %copy-done.9, ...), custom_call_target="tpu_custom_call" | custom-call | flops 1342177280 | bytes 6291456 | tf_op jit(solution)/shard_map/project/pallas_call | solution.py:193
  60.9 1.2 slice.49
  62.1 1.9 %collective-permute-start.9 = (bf16[1024,256]{1,0:T(8,128)(2,1)}, bf16[1024,256]{1,0:T(8,128)(2,1)S(1)}, u32[]{:S(2)}, u32[]{:S(2)}) collective-permute-start(bf16[1024,256]{1,0:T(8,128)(2,1)} %get-tuple-element.16.rest_0_), channel_id=1, source_target_pairs={{0,24},{1,25},{2,26},{3,27},{4,28},{5,29},{6,30},{7,31},{8,0},{9,1... | collective-permute-start | bytes 1572872 | tf_op jit(solution)/shard_map/ppermute | solution.py:50
  65.2 1.5 %convert_reduce_fusion.2 = (s32[4,10,8]{2,1,0:T(8,128)S(1)}, s32[4,10,8]{2,1,0:T(8,128)S(1)}) fusion(s32[4,10,8]{2,1,0:T(8,128)S(1)} %broadcast_subtract_fusion, s32[12]{0:T(128)S(1)} %get-tuple-element.60, s32[4,10,8]{2,1,0:T(8,128)S(1)} %broadcast_subtract_fusion.1), kind=kLoop, calls=%fused_computation.11 | loop fusion | flops 22400 | bytes 5168 | tf_op jit(solution)/shard_map/reduce_sum | solution.py:424
  69.4 1.8 %prepare.1.col_ref = s32[1280,128]{1,0:T(8,128)} custom-call(s32[16,128]{1,0:T(8,128)} %add_add_fusion.1.tq_ref), custom_call_target="tpu_custom_call" | custom-call | flops 2097152 | bytes 1048576 | tf_op jit(solution)/shard_map/prepare/pallas_call | solution.py:118
  76.0 7.4 %attend.3.sums_in = f32[1280,128]{1,0:T(8,128)S(1)} custom-call(s32[20]{0:T(128)S(1)} %reshape.404.count_ref, s32[320]{0:T(512)S(1)} %reshape_reshape.4.work_ref, f32[320]{0:T(512)S(1)} %select_n.330.base_ref, f32[24]{0:T(128)S(1)} %fusion.12.steps_ref, bf16[1024,128]{1,0:T(8,128)(2,1)S(1)} %copy-done.4, bf16[256,128]{1,0:T(8,128)(2,1)S(1)} %copy-done.6, ...), custom_call_target="tpu_custom_call" | custom-call | flops 2684354560 | bytes 5242880 | tf_op jit(solution)/shard_map/attend/pallas_call | solution.py:335
  84.0 1.6 %collective-permute-start.11 = (bf16[512,256]{1,0:T(8,128)(2,1)S(1)}, bf16[512,256]{1,0:T(8,128)(2,1)S(1)}, u32[]{:S(2)}, u32[]{:S(2)}) collective-permute-start(bf16[512,256]{1,0:T(8,128)(2,1)S(1)} %slice.71), channel_id=1, source_target_pairs={{0,24},{1,25},{2,26},{3,27},{4,28},{5,29},{6,30},{7,31},{8,0},{9,1... | collective-permute-start | bytes 786440 | tf_op jit(solution)/shard_map/ppermute | solution.py:50
  85.7 7.8 %attend.4.sums_in = f32[1280,128]{1,0:T(8,128)S(1)} custom-call(s32[20]{0:T(128)S(1)} %reshape.404.count_ref, s32[320]{0:T(512)S(1)} %reshape_reshape.4.work_ref, f32[320]{0:T(512)S(1)} %select_n.330.base_ref, f32[24]{0:T(128)S(1)} %fusion.12.steps_ref, bf16[1024,128]{1,0:T(8,128)(2,1)S(1)} %copy-done.4, bf16[256,128]{1,0:T(8,128)(2,1)S(1)} %copy-done.6, ...), custom_call_target="tpu_custom_call" | custom-call | flops 5368709120 | bytes 10485760 | tf_op jit(solution)/shard_map/attend/pallas_call | solution.py:335
  93.5 4.7 %attend.5 = bf16[8,160,256]{2,1,0:T(8,128)(2,1)} custom-call(s32[20]{0:T(128)S(1)} %reshape.404.count_ref, s32[320]{0:T(512)S(1)} %reshape_reshape.4.work_ref, f32[320]{0:T(512)S(1)} %select_n.330.base_ref, f32[24]{0:T(128)S(1)} %fusion.12.steps_ref, bf16[1024,128]{1,0:T(8,128)(2,1)S(1)} %copy-done.4, bf16[256,128]{1,0:T(8,128)(2,1)S(1)} %copy-done.6, ...), custom_call_target="tpu_custom_call" | custom-call | flops 2684354560 | bytes 5242880 | tf_op jit(solution)/shard_map/attend/pallas_call | solution.py:335
  98.2 7.4 %all-to-all-start.1 = ((bf16[8,160,256]{2,1,0:T(8,128)(2,1)}), bf16[8,160,256]{2,1,0:T(8,128)(2,1)S(1)}, u32[]{:S(2)}, u32[]{:S(2)}) async-start(bf16[8,160,256]{2,1,0:T(8,128)(2,1)} %attend.5), calls=%async_computation.1 | async-start | bytes 1310720 | tf_op jit(solution)/shard_map/all_to_all | solution.py:457
  105.6 21.2 %all-to-all-done.1.pair_ref = bf16[8,160,256]{2,1,0:T(8,128)(2,1)S(1)} async-done(((bf16[8,160,256]{2,1,0:T(8,128)(2,1)}), bf16[8,160,256]{2,1,0:T(8,128)(2,1)S(1)}, u32[]{:S(2)}, u32[]{:S(2)}) %all-to-all-start.1) | async-done | bytes 655392 | tf_op jit(solution)/shard_map/all_to_all | solution.py:457
  127.6 4.0 %finish.1 = (bf16[1,128,1024]{2,1,0:T(8,128)(2,1)}, bf16[1,32,1024]{2,1,0:T(8,128)(2,1)}) custom-call(bf16[1,128,1024]{2,1,0:T(8,128)(2,1)} %hist_ref.3, bf16[1,32,1024]{2,1,0:T(8,128)(2,1)} %cand_ref.3, bf16[8,160,256]{2,1,0:T(8,128)(2,1)} %copy-done.7, bf16[1024,1024]{1,0:T(8,128)(2,1)} %all-gather.4.cloned.1.call-done.w_hbm), custom_call_target="tpu_custom_call" | custom-call | flops 335544320 | bytes 4194304 | tf_op jit(solution)/shard_map/finish/pallas_call | solution.py:365
  (125 shorter events, 19.3 us)
Async XLA Ops:
  7.2 48.6 %all-gather.6.cloned.1.call-start = ((), (), s32[]{:S(2)}) async-start(), calls=%async_computation.3 | async-start | bytes 2949120 | tf_op jit(solution)/shard_map/all_gather | solution.py:392
  10.0 16.0 %all-to-all-start = ((bf16[8,256,128]{2,1,0:T(8,128)(2,1)}), bf16[8,256,128]{2,1,0:T(8,128)(2,1)S(1)}, u32[]{:S(2)}, u32[]{:S(2)}) async-start(bf16[8,256,128]{2,1,0:T(8,128)(2,1)} %get-tuple-element.13), calls=%async_computation | async-start | bytes 1048576 | tf_op jit(solution)/shard_map/all_to_all | solution.py:381
  16.1 89.5 %all-gather.4.cloned.1.call-start = ((), (), s32[]{:S(2)}) async-start(), calls=%async_computation.2 | async-start | bytes 2359296 | tf_op jit(solution)/shard_map/all_gather | solution.py:403
  16.1 3.9 %collective-permute-start = (s32[1,256]{1,0:T(1,128)}, s32[1,256]{1,0:T(1,128)S(1)}, u32[]{:S(2)}, u32[]{:S(2)}) collective-permute-start(s32[1,256]{1,0:T(1,128)} %get-tuple-element.12), channel_id=1, source_target_pairs={{0,8},{1,9},{2,10},{3,11},{4,12},{5,13},{6,14},{7,15},{8,0},{9,1},... | collective-permute-start | bytes 3080 | tf_op jit(solution)/shard_map/ppermute | solution.py:400
  20.7 5.2 %collective-permute-start.1 = (s32[2,256]{1,0:T(2,128)S(1)}, s32[2,256]{1,0:T(2,128)S(1)}, u32[]{:S(2)}, u32[]{:S(2)}) collective-permute-start(s32[2,256]{1,0:T(2,128)S(1)} %pad_add_fusion.6), channel_id=1, source_target_pairs={{0,16},{1,17},{2,18},{3,19},{4,20},{5,21},{6,22},{7,23},{8,24},{9,... | collective-permute-start | bytes 6152 | tf_op jit(solution)/shard_map/ppermute | solution.py:400
  25.9 3.5 %collective-permute-start.2 = (s32[4,256]{1,0:T(4,128)S(1)}, s32[4,256]{1,0:T(4,128)S(1)}, u32[]{:S(2)}, u32[]{:S(2)}) collective-permute-start(s32[4,256]{1,0:T(4,128)S(1)} %pad_add_fusion.5), channel_id=1, source_target_pairs={{0,1},{1,0},{2,3},{3,2},{4,5},{5,4},{6,7},{7,6},{8,9},{9,8},{10,11... | collective-permute-start | bytes 12296 | tf_op jit(solution)/shard_map/ppermute | solution.py:400
  26.1 29.7 %copy-start.8 = (bf16[4,256,128]{2,1,0:T(8,128)(2,1)}, bf16[4,256,128]{2,1,0:T(8,128)(2,1)S(1)}, u32[]{:S(2)}) copy-start(bf16[4,256,128]{2,1,0:T(8,128)(2,1)S(1)} %dynamic-slice_bitcast_fusion.refs_0_) | copy-start | bytes 786436
  26.1 9.2 %collective-permute-start.4 = (bf16[4,256,128]{2,1,0:T(8,128)(2,1)S(1)}, bf16[4,256,128]{2,1,0:T(8,128)(2,1)S(1)}, u32[]{:S(2)}, u32[]{:S(2)}) collective-permute-start(bf16[4,256,128]{2,1,0:T(8,128)(2,1)S(1)} %dynamic-slice_bitcast_fusion.refs_0_), channel_id=1, source_target_pairs={{0,8},{1,9},{2,10},{3,11},{4,12},{5,13},{6,14},{7,15},{8,16},{9,17... | collective-permute-start | bytes 786440 | tf_op jit(solution)/shard_map/ppermute | solution.py:50
  27.3 15.2 %collective-permute-start.5 = (bf16[4,256,128]{2,1,0:T(8,128)(2,1)S(1)}, bf16[4,256,128]{2,1,0:T(8,128)(2,1)S(1)}, u32[]{:S(2)}, u32[]{:S(2)}) collective-permute-start(bf16[4,256,128]{2,1,0:T(8,128)(2,1)S(1)} %dynamic-slice_bitcast_fusion.refs_0_), channel_id=1, source_target_pairs={{0,24},{1,25},{2,26},{3,27},{4,28},{5,29},{6,30},{7,31},{8,0},{9,1... | collective-permute-start | bytes 786440 | tf_op jit(solution)/shard_map/ppermute | solution.py:50
  28.2 14.4 %collective-permute-start.6 = (bf16[4,256,128]{2,1,0:T(8,128)(2,1)S(1)}, bf16[4,256,128]{2,1,0:T(8,128)(2,1)S(1)}, u32[]{:S(2)}, u32[]{:S(2)}) collective-permute-start(bf16[4,256,128]{2,1,0:T(8,128)(2,1)S(1)} %dynamic-slice_bitcast_fusion.refs_0_), channel_id=1, source_target_pairs={{0,16},{1,17},{2,18},{3,19},{4,20},{5,21},{6,22},{7,23},{8,24},{9,... | collective-permute-start | bytes 786440 | tf_op jit(solution)/shard_map/ppermute | solution.py:50
  29.5 13.1 %copy-start.12 = (s32[8,256]{1,0:T(8,128)}, s32[8,256]{1,0:T(8,128)S(1)}, u32[]{:S(2)}) copy-start(s32[8,256]{1,0:T(8,128)S(1)} %pad_add_fusion.4.mine_ref) | copy-start | bytes 24580
  29.5 5.1 %collective-permute-start.3 = (s32[8,256]{1,0:T(8,128)S(1)}, s32[8,256]{1,0:T(8,128)S(1)}, u32[]{:S(2)}, u32[]{:S(2)}) collective-permute-start(s32[8,256]{1,0:T(8,128)S(1)} %pad_add_fusion.4.mine_ref), channel_id=1, source_target_pairs={{0,2},{1,3},{2,0},{3,1},{4,6},{5,7},{6,4},{7,5},{8,10},{9,11},{10,... | collective-permute-start | bytes 24584 | tf_op jit(solution)/shard_map/ppermute | solution.py:400
  34.6 7.9 %copy-start.13 = (s32[8,256]{1,0:T(8,128)}, s32[8,256]{1,0:T(8,128)S(1)}, u32[]{:S(2)}) copy-start(s32[8,256]{1,0:T(8,128)S(1)} %collective-permute-done.3.other_ref) | copy-start | bytes 24580
  35.3 7.3 %copy-start.9 = (bf16[4,256,128]{2,1,0:T(8,128)(2,1)}, bf16[4,256,128]{2,1,0:T(8,128)(2,1)S(1)}, u32[]{:S(2)}) copy-start(bf16[4,256,128]{2,1,0:T(8,128)(2,1)S(1)} %collective-permute-done.4.rest_0_.refs_1_) | copy-start | bytes 786436
  45.7 8.2 %collective-permute-start.7 = (s32[16,256]{1,0:T(8,128)}, s32[16,256]{1,0:T(8,128)S(1)}, u32[]{:S(2)}, u32[]{:S(2)}) collective-permute-start(s32[16,256]{1,0:T(8,128)} %get-tuple-element.14), channel_id=1, source_target_pairs={{0,4},{1,5},{2,6},{3,7},{4,0},{5,1},{6,2},{7,3},{8,12},{9,13},{10,... | collective-permute-start | bytes 49160 | tf_op jit(solution)/shard_map/ppermute | solution.py:400
  62.0 21.4 %collective-permute-start.8 = (bf16[1024,256]{1,0:T(8,128)(2,1)}, bf16[1024,256]{1,0:T(8,128)(2,1)S(1)}, u32[]{:S(2)}, u32[]{:S(2)}) collective-permute-start(bf16[1024,256]{1,0:T(8,128)(2,1)} %get-tuple-element.16.rest_0_), channel_id=1, source_target_pairs={{0,8},{1,9},{2,10},{3,11},{4,12},{5,13},{6,14},{7,15},{8,16},{9,17... | collective-permute-start | bytes 1572872 | tf_op jit(solution)/shard_map/ppermute | solution.py:50
  62.1 21.9 %collective-permute-start.9 = (bf16[1024,256]{1,0:T(8,128)(2,1)}, bf16[1024,256]{1,0:T(8,128)(2,1)S(1)}, u32[]{:S(2)}, u32[]{:S(2)}) collective-permute-start(bf16[1024,256]{1,0:T(8,128)(2,1)} %get-tuple-element.16.rest_0_), channel_id=1, source_target_pairs={{0,24},{1,25},{2,26},{3,27},{4,28},{5,29},{6,30},{7,31},{8,0},{9,1... | collective-permute-start | bytes 1572872 | tf_op jit(solution)/shard_map/ppermute | solution.py:50
  71.1 1.1 copy-start
  72.2 1.0 copy-start.2
  76.0 9.7 %copy-start.1 = (s32[1280,128]{1,0:T(8,128)S(1)}, s32[1280,128]{1,0:T(8,128)}, u32[]{:S(2)}) copy-start(s32[1280,128]{1,0:T(8,128)} %prepare.1.col_ref) | copy-start | bytes 1966084
  83.4 10.1 %collective-permute-start.10 = (bf16[512,256]{1,0:T(8,128)(2,1)S(1)}, bf16[512,256]{1,0:T(8,128)(2,1)S(1)}, u32[]{:S(2)}, u32[]{:S(2)}) collective-permute-start(bf16[512,256]{1,0:T(8,128)(2,1)S(1)} %slice.70), channel_id=1, source_target_pairs={{0,8},{1,9},{2,10},{3,11},{4,12},{5,13},{6,14},{7,15},{8,16},{9,17... | collective-permute-start | bytes 786440 | tf_op jit(solution)/shard_map/ppermute | solution.py:50
  84.0 9.5 %copy-start.3 = (bf16[8,160,128]{2,1,0:T(8,128)(2,1)S(1)}, bf16[8,160,128]{2,1,0:T(8,128)(2,1)}, u32[]{:S(2)}) copy-start(bf16[8,160,128]{2,1,0:T(8,128)(2,1)} %get-tuple-element.20.rest_3_) | copy-start | bytes 983044
  84.0 9.5 %collective-permute-start.11 = (bf16[512,256]{1,0:T(8,128)(2,1)S(1)}, bf16[512,256]{1,0:T(8,128)(2,1)S(1)}, u32[]{:S(2)}, u32[]{:S(2)}) collective-permute-start(bf16[512,256]{1,0:T(8,128)(2,1)S(1)} %slice.71), channel_id=1, source_target_pairs={{0,24},{1,25},{2,26},{3,27},{4,28},{5,29},{6,30},{7,31},{8,0},{9,1... | collective-permute-start | bytes 786440 | tf_op jit(solution)/shard_map/ppermute | solution.py:50
  98.2 28.6 %all-to-all-start.1 = ((bf16[8,160,256]{2,1,0:T(8,128)(2,1)}), bf16[8,160,256]{2,1,0:T(8,128)(2,1)S(1)}, u32[]{:S(2)}, u32[]{:S(2)}) async-start(bf16[8,160,256]{2,1,0:T(8,128)(2,1)} %attend.5), calls=%async_computation.1 | async-start | bytes 1310720 | tf_op jit(solution)/shard_map/all_to_all | solution.py:457
  (6 other events, 4.9 us)
Sparse Core Ops, SparseCore 0:
  10.2 42.8 all-gather.5
  54.9 39.9 all-gather.3

commit v6 on v5

--- a/solution.py
+++ b/solution.py
@@ -81,6 +81,7 @@
         in_specs=[VM] * 4 + [HBM],
         out_specs=[VM] * 3,
         scratch_shapes=[pltpu.VMEM((DEPTH, HD), BF16), pltpu.SemaphoreType.DMA(())],
+        compiler_params=params(6),
         cost_estimate=pl.CostEstimate(flops=8 * ROWS * D, bytes_accessed=4 * ROWS * D, transcendentals=0),
         name="norm_rows",
     )(hist, cand, events, requests, w_proj)
@@ -102,8 +103,9 @@
             jax.ShapeDtypeStruct((2 * mine.shape[0], mine.shape[1]), mine.dtype),
             jax.ShapeDtypeStruct(w_out.shape, w_out.dtype),
         ],
-        in_specs=[VM] * 3 + [HBM] * len(ties),
+        in_specs=[VM] * (3 + len(ties)),
         out_specs=[VM] * 2,
+        compiler_params=params(6),
         cost_estimate=pl.CostEstimate(flops=1 << 12, bytes_accessed=1 << 16, transcendentals=0),
         name="merge",
     )(mine, other, w_out, *ties)
@@ -120,6 +122,7 @@
         out_shape=jax.ShapeDtypeStruct((QROWS, 128), I32),
         in_specs=[VM],
         out_specs=VM,
+        compiler_params=params(4),
         cost_estimate=pl.CostEstimate(flops=2 << 20, bytes_accessed=1 << 20, transcendentals=0),
         name="prepare",
     )(tq)
@@ -139,13 +142,7 @@
     parts, (qh_ref, qc_ref, kv_ref, own_ref, gate_ref, rows, weights, sems) = refs[:NX], refs[NX:]
     x = position()[0]
     hist, cand = HALF * HIST, HALF * CAND
-    copies, fetches = [], []
-    for m in range(NX):
-        at = pl.multiple_of((x + OFF[m]) % NX * DEPTH, DEPTH)
-        for kind in range(4):
-            block = weights.at[pl.ds(at, DEPTH), kind * HD : (kind + 1) * HD]
-            fetches.append(pltpu.make_async_copy(parts[m].at[kind], block, sems.at[2 + m, kind]))
-            fetches[-1].start()
+    copies = []
     for place in range(NP):
         step, at = place // HALF, place % HALF
         copies.append(
@@ -162,8 +159,10 @@
         )
         for copy in copies[-1]:
             copy.start()
-    for fetch in fetches:
-        fetch.wait()
+    for m in range(NX):
+        at = pl.multiple_of((x + OFF[m]) % NX * DEPTH, DEPTH)
+        for kind in range(4):
+            weights[pl.ds(at, DEPTH), kind * HD : (kind + 1) * HD] = parts[m][kind]
     for step in range(NP // HALF):
         for pair in copies[step * HALF : (step + 1) * HALF]:
             for copy in pair:
@@ -192,12 +191,12 @@
 def project(rows, parts):
     return pl.pallas_call(
         project_kernel,
-        in_specs=[HBM] * (1 + NX),
+        in_specs=[HBM] + [VM] * NX,
         out_specs=[VM] * 5,
         scratch_shapes=[
             pltpu.VMEM((NP // HALF, HALF * ROWS, D), BF16),
             pltpu.VMEM((D, 4 * HD), BF16),
-            pltpu.SemaphoreType.DMA((2 + NX, NP)),
+            pltpu.SemaphoreType.DMA((2, NP)),
         ],
         out_shape=[
             jax.ShapeDtypeStruct((QH, HD), BF16),
@@ -206,7 +205,7 @@
             jax.ShapeDtypeStruct((QC, HD), F32),
             jax.ShapeDtypeStruct((NP, ROWS, HD), BF16),
         ],
-        compiler_params=params(56),
+        compiler_params=params(50),
         cost_estimate=pl.CostEstimate(flops=2 * QROWS * D * 4 * HD, bytes_accessed=6 << 20, transcendentals=QROWS * 4 * HD),
         name="project",
     )(rows, *parts)
@@ -371,7 +370,7 @@
         in_specs=[VM] * 3 + [HBM],
         out_specs=[VM, VM],
         scratch_shapes=[pltpu.VMEM((D, D), BF16), pltpu.SemaphoreType.DMA(())],
-        compiler_params=params(56),
+        compiler_params=params(12),
         cost_estimate=pl.CostEstimate(flops=2 * ROWS * D * D, bytes_accessed=4 << 20, transcendentals=0),
         name="finish",
     )(hist, cand, pairs, w_out)

time: 140 us -> 128 us (0.914)
  Pallas kernels: 35.4 us -> 27.6 us
  starting transfers between devices: 32.9 us -> 30.5 us
  waiting for transfers between devices: 35.2 us -> 37.5 us
  other arithmetic: 9.19 us -> 7.2 us
  local copies, waits for them, and re-layouts: 10.7 us -> 8.9 us
    all_gather x1, waiting for transfers between devices: 0.01 us -> 4.07 us  [body(): w_full = lax.all_gather(w_mine, 'batch', axis=0, tiled=True)]
    all_to_all x1, waiting for transfers between devices: 21.2 us -> 17.3 us  [body(): atts = lax.all_to_all(att, 'seq', 0, 0, axis_index_groups=SAME_X)]
    all_to_all x1, starting transfers between devices: 7.38 us -> 5.13 us  [body(): atts = lax.all_to_all(att, 'seq', 0, 0, axis_index_groups=SAME_X)]
    pallas_call x1, Pallas kernels: 4.03 us -> 1.92 us  [finish(): pl.pallas_call(finish_kernel, out_shape=[jax.ShapeDtypeStruct((1, HIST, D...]
    pallas_call x1, Pallas kernels: 5.14 us -> 3.51 us  [project(): pl.pallas_call(project_kernel, in_specs=[HBM] + [VM] * NX, out_specs=[VM]...]
    pallas_call x1, Pallas kernels: 2.79 us -> 1.22 us  [norm_rows(): pl.pallas_call(norm_kernel, out_shape=[jax.ShapeDtypeStruct((ROWS, D), BF...]
    pallas_call x1, Pallas kernels: 1.76 us -> 0.23 us  [prepare(): pl.pallas_call(prepare_kernel, out_shape=jax.ShapeDtypeStruct((QROWS, 128...]
    all_gather x1, waiting for transfers between devices: 0.02 us -> 1.5 us  [body(): rows = lax.all_gather(n0, 'seq', axis_index_groups=SAME_X)]
  transfers between devices with their start and end apart: 16 -> 16, of which waited for: 6 -> 9; matrix products, arithmetic and copies ran while one was open for 9% -> 8% of each run, Pallas kernels for 21% -> 19%
where the time goes in v6:
time: 128 us; the launch traced here: 127 us
  waiting for transfers between devices  37.5 us (29%)
  starting transfers between devices  30.5 us (24%)
  Pallas kernels  27.6 us (22%)
  between operations  15 us (12%)
  local copies, waits for them, and re-layouts  8.9 us (7%)
  other arithmetic  7.2 us (6%)
    pallas_call x3, Pallas kernels, attend(): pl.pallas_call(functools.partial(attend_kernel, fresh=fresh, last=last, c...  20 us
    all_to_all x1, waiting for transfers between devices, body(): atts = lax.all_to_all(att, 'seq', 0, 0, axis_index_groups=SAME_X)  17.3 us
    ppermute x5, starting transfers between devices, body(): other = lax.ppermute(times, 'seq', [(s, s ^ 1 << bit) for s in range(NS)])  11.8 us
    ppermute x7, waiting for transfers between devices, shift(): return lax.ppermute(array, 'seq', seq_perm(dx, dz, flip))  7.58 us
    ppermute x7, starting transfers between devices, shift(): return lax.ppermute(array, 'seq', seq_perm(dx, dz, flip))  7.55 us
    ppermute x5, waiting for transfers between devices, body(): other = lax.ppermute(times, 'seq', [(s, s ^ 1 << bit) for s in range(NS)])  6.99 us
    all_to_all x1, starting transfers between devices, gather_weights(): shards = lax.all_to_all(shards, 'batch', 0, 0)  6.05 us
    unnamed x18, local copies, waits for them, and re-layouts  5.92 us
  transfers between devices with their start and end apart: 16, of which 9 were waited for; matrix products, arithmetic and copies ran while one was open for 8% of the time, Pallas kernels for 19%

profile of v6, /device:TPU:30, one launch (start us, length us, event | category | flops | bytes accessed | tf_op | source)
XLA Modules:
  0.0 126.8 jit_solution(13400083685197556986)
XLA Ops:
  7.2 1.2 copy-done.1
  11.5 1.2 norm_rows.1
  12.8 6.1 %all-to-all-start = ((bf16[8,256,128]{2,1,0:T(8,128)(2,1)}), bf16[8,256,128]{2,1,0:T(8,128)(2,1)S(1)}, u32[]{:S(2)}, u32[]{:S(2)}) async-start(bf16[8,256,128]{2,1,0:T(8,128)(2,1)} %get-tuple-element.13), calls=%async_computation | async-start | bytes 1048576 | tf_op jit(solution)/shard_map/all_to_all | solution.py:380
  20.9 1.5 %convert_reduce_fusion = (s32[4,10,8]{2,1,0:T(8,128)S(1)}, s32[4,10,8]{2,1,0:T(8,128)S(1)}) fusion(s32[4,10,8]{2,1,0:T(8,128)S(1)} %get-tuple-element.50, s32[12]{0:T(128)S(1)} %get-tuple-element.59, s32[4,10,8]{2,1,0:T(8,128)S(1)} %get-tuple-element.49), kind=kLoop, calls=%fused_computation.9 | loop fusion | flops 22400 | bytes 5168 | tf_op jit(solution)/shard_map/reduce_sum | solution.py:423
  24.0 4.0 %collective-permute-done.1 = s32[2,256]{1,0:T(2,128)S(1)} collective-permute-done((s32[2,256]{1,0:T(2,128)S(1)}, s32[2,256]{1,0:T(2,128)S(1)}, u32[]{:S(2)}, u32[]{:S(2)}) %collective-permute-start.1) | collective-permute-done | bytes 2080 | tf_op jit(solution)/shard_map/ppermute | solution.py:399
  28.2 1.2 collective-permute-start.4
  30.3 1.2 collective-permute-start.6
  31.5 3.4 %collective-permute-start.3 = (s32[8,256]{1,0:T(8,128)S(1)}, s32[8,256]{1,0:T(8,128)S(1)}, u32[]{:S(2)}, u32[]{:S(2)}) collective-permute-start(s32[8,256]{1,0:T(8,128)S(1)} %pad_add_fusion.4.mine_ref), channel_id=1, source_target_pairs={{0,2},{1,3},{2,0},{3,1},{4,6},{5,7},{6,4},{7,5},{8,10},{9,11},{10,... | collective-permute-start | bytes 24584 | tf_op jit(solution)/shard_map/ppermute | solution.py:399
  34.9 2.2 %collective-permute-done.3.other_ref = s32[8,256]{1,0:T(8,128)S(1)} collective-permute-done((s32[8,256]{1,0:T(8,128)S(1)}, s32[8,256]{1,0:T(8,128)S(1)}, u32[]{:S(2)}, u32[]{:S(2)}) %collective-permute-start.3) | collective-permute-done | bytes 8224 | tf_op jit(solution)/shard_map/ppermute | solution.py:399
  37.3 7.3 %collective-permute-done.5.rest_1_.refs_2_ = bf16[4,256,128]{2,1,0:T(8,128)(2,1)S(1)} collective-permute-done((bf16[4,256,128]{2,1,0:T(8,128)(2,1)S(1)}, bf16[4,256,128]{2,1,0:T(8,128)(2,1)S(1)}, u32[]{:S(2)}, u32[]{:S(2)}) %collective-permute-start.5) | collective-permute-done | bytes 262176 | tf_op jit(solution)/shard_map/ppermute | solution.py:50
  45.3 6.3 %collective-permute-start.7 = (s32[16,256]{1,0:T(8,128)S(1)}, s32[16,256]{1,0:T(8,128)S(1)}, u32[]{:S(2)}, u32[]{:S(2)}) collective-permute-start(s32[16,256]{1,0:T(8,128)S(1)} %get-tuple-element.14), channel_id=1, source_target_pairs={{0,4},{1,5},{2,6},{3,7},{4,0},{5,1},{6,2},{7,3},{8,12},{9,13},{10,... | collective-permute-start | bytes 49160 | tf_op jit(solution)/shard_map/ppermute | solution.py:399
  55.0 1.5 %all-gather.6.cloned.1.call-done = bf16[1280,1024]{1,0:T(8,128)(2,1)} async-done(((bf16[160,1024]{1,0:T(8,128)(2,1)}), bf16[1280,1024]{1,0:T(8,128)(2,1)}) %all-gather.6.cloned.1.call-update) | async-done | bytes 2621456 | tf_op jit(solution)/shard_map/all_gather | solution.py:391
  56.5 3.5 %project.1 = (bf16[1024,128]{1,0:T(8,128)(2,1)S(1)}, bf16[256,128]{1,0:T(8,128)(2,1)S(1)}, bf16[1024,256]{1,0:T(8,128)(2,1)S(1)}, f32[256,128]{1,0:T(8,128)S(1)}, bf16[8,160,128]{2,1,0:T(8,128)(2,1)S(1)}) custom-call(bf16[8,160,1024]{2,1,0:T(8,128)(2,1)} %bitcast.38, bf16[4,256,128]{2,1,0:T(8,128)(2,1)S(1)} %dynamic-slice_bitcast_fusion.refs_0_, ...), custom_call_target="tpu_custom_call" | custom-call | flops 1342177280 | bytes 6291456 | tf_op jit(solution)/shard_map/project/pallas_call | solution.py:192
  61.1 1.5 %collective-permute-start.9 = (bf16[1024,256]{1,0:T(8,128)(2,1)S(1)}, bf16[1024,256]{1,0:T(8,128)(2,1)S(1)}, u32[]{:S(2)}, u32[]{:S(2)}) collective-permute-start(bf16[1024,256]{1,0:T(8,128)(2,1)S(1)} %get-tuple-element.16.rest_0_), channel_id=1, source_target_pairs={{0,24},{1,25},{2,26},{3,27},{4,28},{5,29},{6,30},{7,31},{8,0},{9,1... | collective-permute-start | bytes 1572872 | tf_op jit(solution)/shard_map/ppermute | solution.py:50
  63.7 1.5 %convert_reduce_fusion.2 = (s32[4,10,8]{2,1,0:T(8,128)S(1)}, s32[4,10,8]{2,1,0:T(8,128)S(1)}) fusion(s32[4,10,8]{2,1,0:T(8,128)S(1)} %broadcast_subtract_fusion, s32[12]{0:T(128)S(1)} %get-tuple-element.60, s32[4,10,8]{2,1,0:T(8,128)S(1)} %broadcast_subtract_fusion.1), kind=kLoop, calls=%fused_computation.11 | loop fusion | flops 22400 | bytes 5168 | tf_op jit(solution)/shard_map/reduce_sum | solution.py:423
  67.5 7.4 %attend.3.sums_in = f32[1280,128]{1,0:T(8,128)S(1)} custom-call(s32[20]{0:T(128)S(1)} %reshape.404.count_ref, s32[320]{0:T(512)S(1)} %reshape_reshape.4.work_ref, f32[320]{0:T(512)S(1)} %select_n.330.base_ref, f32[24]{0:T(128)S(1)} %fusion.12.steps_ref, bf16[1024,128]{1,0:T(8,128)(2,1)S(1)} %get-tuple-element.17.qh_ref, ...), custom_call_target="tpu_custom_call" | custom-call | flops 2684354560 | bytes 5242880 | tf_op jit(solution)/shard_map/attend/pallas_call | solution.py:334
  74.9 1.6 %collective-permute-start.10 = (bf16[512,256]{1,0:T(8,128)(2,1)S(1)}, bf16[512,256]{1,0:T(8,128)(2,1)S(1)}, u32[]{:S(2)}, u32[]{:S(2)}) collective-permute-start(bf16[512,256]{1,0:T(8,128)(2,1)S(1)} %slice.70), channel_id=1, source_target_pairs={{0,8},{1,9},{2,10},{3,11},{4,12},{5,13},{6,14},{7,15},{8,16},{9,17... | collective-permute-start | bytes 786440 | tf_op jit(solution)/shard_map/ppermute | solution.py:50
  77.1 8.0 %attend.4.sums_in = f32[1280,128]{1,0:T(8,128)S(1)} custom-call(s32[20]{0:T(128)S(1)} %reshape.404.count_ref, s32[320]{0:T(512)S(1)} %reshape_reshape.4.work_ref, f32[320]{0:T(512)S(1)} %select_n.330.base_ref, f32[24]{0:T(128)S(1)} %fusion.12.steps_ref, bf16[1024,128]{1,0:T(8,128)(2,1)S(1)} %get-tuple-element.17.qh_ref, ...), custom_call_target="tpu_custom_call" | custom-call | flops 5368709120 | bytes 10485760 | tf_op jit(solution)/shard_map/attend/pallas_call | solution.py:334
  85.2 4.7 %attend.5 = bf16[8,160,256]{2,1,0:T(8,128)(2,1)} custom-call(s32[20]{0:T(128)S(1)} %reshape.404.count_ref, s32[320]{0:T(512)S(1)} %reshape_reshape.4.work_ref, f32[320]{0:T(512)S(1)} %select_n.330.base_ref, f32[24]{0:T(128)S(1)} %fusion.12.steps_ref, bf16[1024,128]{1,0:T(8,128)(2,1)S(1)} %get-tuple-element.17.qh_ref, ...), custom_call_target="tpu_custom_call" | custom-call | flops 2684354560 | bytes 5242880 | tf_op jit(solution)/shard_map/attend/pallas_call | solution.py:334
  89.9 5.1 %all-to-all-start.1 = ((bf16[8,160,256]{2,1,0:T(8,128)(2,1)}), bf16[8,160,256]{2,1,0:T(8,128)(2,1)S(1)}, u32[]{:S(2)}, u32[]{:S(2)}) async-start(bf16[8,160,256]{2,1,0:T(8,128)(2,1)} %attend.5), calls=%async_computation.1 | async-start | bytes 1310720 | tf_op jit(solution)/shard_map/all_to_all | solution.py:456
  95.0 4.1 %all-gather.4.cloned.1.call-done.w_hbm = bf16[1024,1024]{1,0:T(8,128)(2,1)} async-done(((bf16[128,1024]{1,0:T(8,128)(2,1)}), bf16[1024,1024]{1,0:T(8,128)(2,1)}) %all-gather.4.cloned.1.call-update) | async-done | bytes 2097168 | tf_op jit(solution)/shard_map/all_gather | solution.py:402
  99.1 17.3 %all-to-all-done.1.pair_ref = bf16[8,160,256]{2,1,0:T(8,128)(2,1)S(1)} async-done(((bf16[8,160,256]{2,1,0:T(8,128)(2,1)}), bf16[8,160,256]{2,1,0:T(8,128)(2,1)S(1)}, u32[]{:S(2)}, u32[]{:S(2)}) %all-to-all-start.1) | async-done | bytes 655392 | tf_op jit(solution)/shard_map/all_to_all | solution.py:456
  116.4 1.6 %copy-done = bf16[1024,1024]{1,0:T(8,128)(2,1)S(1)} copy-done((bf16[1024,1024]{1,0:T(8,128)(2,1)S(1)}, bf16[1024,1024]{1,0:T(8,128)(2,1)}, u32[]{:S(2)}) %copy-start) | copy-done | bytes 2097176
  118.0 1.9 %finish.1 = (bf16[1,128,1024]{2,1,0:T(8,128)(2,1)}, bf16[1,32,1024]{2,1,0:T(8,128)(2,1)}) custom-call(bf16[1,128,1024]{2,1,0:T(8,128)(2,1)S(1)} %copy-done.3, bf16[1,32,1024]{2,1,0:T(8,128)(2,1)S(1)} %copy-done.5, bf16[8,160,256]{2,1,0:T(8,128)(2,1)S(1)} %all-to-all-done.1.pair_ref, bf16[1024,1024]{1,0:T(8,128)(2,1)S(1)} %copy-done), custom_call_target="tpu_custom_call" | custom-call | flops 335544320 | bytes 4194304 | tf_op jit(solution)/shard_map/finish/pallas_call | solution.py:364
  (115 shorter events, 16.5 us)
Async XLA Ops:
  7.2 49.4 %all-gather.6.cloned.1.call-start = ((), (), s32[]{:S(2)}) async-start(), calls=%async_computation.3 | async-start | bytes 2949120 | tf_op jit(solution)/shard_map/all_gather | solution.py:391
  7.2 1.2 copy-start.1
  8.4 0.9 copy-start.2
  9.4 0.8 copy-start.4
  10.9 0.7 copy-start.8
  11.5 33.1 %copy-start.6 = (bf16[128,1024]{1,0:T(8,128)(2,1)S(1)}, bf16[128,1024]{1,0:T(8,128)(2,1)}, u32[]{:S(2)}) copy-start(bf16[128,1024]{1,0:T(8,128)(2,1)} %wout_ref.1) | copy-start | bytes 786436
  12.8 15.3 %all-to-all-start = ((bf16[8,256,128]{2,1,0:T(8,128)(2,1)}), bf16[8,256,128]{2,1,0:T(8,128)(2,1)S(1)}, u32[]{:S(2)}, u32[]{:S(2)}) async-start(bf16[8,256,128]{2,1,0:T(8,128)(2,1)} %get-tuple-element.13), calls=%async_computation | async-start | bytes 1048576 | tf_op jit(solution)/shard_map/all_to_all | solution.py:380
  18.8 80.3 %all-gather.4.cloned.1.call-start = ((), (), s32[]{:S(2)}) async-start(), calls=%async_computation.2 | async-start | bytes 2359296 | tf_op jit(solution)/shard_map/all_gather | solution.py:402
  18.8 3.9 %collective-permute-start = (s32[1,256]{1,0:T(1,128)S(1)}, s32[1,256]{1,0:T(1,128)S(1)}, u32[]{:S(2)}, u32[]{:S(2)}) collective-permute-start(s32[1,256]{1,0:T(1,128)S(1)} %get-tuple-element.12), channel_id=1, source_target_pairs={{0,8},{1,9},{2,10},{3,11},{4,12},{5,13},{6,14},{7,15},{8,0},{9,1},... | collective-permute-start | bytes 3080 | tf_op jit(solution)/shard_map/ppermute | solution.py:399
  22.8 5.2 %collective-permute-start.1 = (s32[2,256]{1,0:T(2,128)S(1)}, s32[2,256]{1,0:T(2,128)S(1)}, u32[]{:S(2)}, u32[]{:S(2)}) collective-permute-start(s32[2,256]{1,0:T(2,128)S(1)} %pad_add_fusion.6), channel_id=1, source_target_pairs={{0,16},{1,17},{2,18},{3,19},{4,20},{5,21},{6,22},{7,23},{8,24},{9,... | collective-permute-start | bytes 6152 | tf_op jit(solution)/shard_map/ppermute | solution.py:399
  28.0 3.5 %collective-permute-start.2 = (s32[4,256]{1,0:T(4,128)S(1)}, s32[4,256]{1,0:T(4,128)S(1)}, u32[]{:S(2)}, u32[]{:S(2)}) collective-permute-start(s32[4,256]{1,0:T(4,128)S(1)} %pad_add_fusion.5), channel_id=1, source_target_pairs={{0,1},{1,0},{2,3},{3,2},{4,5},{5,4},{6,7},{7,6},{8,9},{9,8},{10,11... | collective-permute-start | bytes 12296 | tf_op jit(solution)/shard_map/ppermute | solution.py:399
  28.2 9.2 %collective-permute-start.4 = (bf16[4,256,128]{2,1,0:T(8,128)(2,1)S(1)}, bf16[4,256,128]{2,1,0:T(8,128)(2,1)S(1)}, u32[]{:S(2)}, u32[]{:S(2)}) collective-permute-start(bf16[4,256,128]{2,1,0:T(8,128)(2,1)S(1)} %dynamic-slice_bitcast_fusion.refs_0_), channel_id=1, source_target_pairs={{0,8},{1,9},{2,10},{3,11},{4,12},{5,13},{6,14},{7,15},{8,16},{9,17... | collective-permute-start | bytes 786440 | tf_op jit(solution)/shard_map/ppermute | solution.py:50
  29.4 15.2 %collective-permute-start.5 = (bf16[4,256,128]{2,1,0:T(8,128)(2,1)S(1)}, bf16[4,256,128]{2,1,0:T(8,128)(2,1)S(1)}, u32[]{:S(2)}, u32[]{:S(2)}) collective-permute-start(bf16[4,256,128]{2,1,0:T(8,128)(2,1)S(1)} %dynamic-slice_bitcast_fusion.refs_0_), channel_id=1, source_target_pairs={{0,24},{1,25},{2,26},{3,27},{4,28},{5,29},{6,30},{7,31},{8,0},{9,1... | collective-permute-start | bytes 786440 | tf_op jit(solution)/shard_map/ppermute | solution.py:50
  30.3 14.4 %collective-permute-start.6 = (bf16[4,256,128]{2,1,0:T(8,128)(2,1)S(1)}, bf16[4,256,128]{2,1,0:T(8,128)(2,1)S(1)}, u32[]{:S(2)}, u32[]{:S(2)}) collective-permute-start(bf16[4,256,128]{2,1,0:T(8,128)(2,1)S(1)} %dynamic-slice_bitcast_fusion.refs_0_), channel_id=1, source_target_pairs={{0,16},{1,17},{2,18},{3,19},{4,20},{5,21},{6,22},{7,23},{8,24},{9,... | collective-permute-start | bytes 786440 | tf_op jit(solution)/shard_map/ppermute | solution.py:50
  31.5 5.6 %collective-permute-start.3 = (s32[8,256]{1,0:T(8,128)S(1)}, s32[8,256]{1,0:T(8,128)S(1)}, u32[]{:S(2)}, u32[]{:S(2)}) collective-permute-start(s32[8,256]{1,0:T(8,128)S(1)} %pad_add_fusion.4.mine_ref), channel_id=1, source_target_pairs={{0,2},{1,3},{2,0},{3,1},{4,6},{5,7},{6,4},{7,5},{8,10},{9,11},{10,... | collective-permute-start | bytes 24584 | tf_op jit(solution)/shard_map/ppermute | solution.py:399
  45.3 8.6 %collective-permute-start.7 = (s32[16,256]{1,0:T(8,128)S(1)}, s32[16,256]{1,0:T(8,128)S(1)}, u32[]{:S(2)}, u32[]{:S(2)}) collective-permute-start(s32[16,256]{1,0:T(8,128)S(1)} %get-tuple-element.14), channel_id=1, source_target_pairs={{0,4},{1,5},{2,6},{3,7},{4,0},{5,1},{6,2},{7,3},{8,12},{9,13},{10,... | collective-permute-start | bytes 49160 | tf_op jit(solution)/shard_map/ppermute | solution.py:399
  60.6 14.3 %collective-permute-start.8 = (bf16[1024,256]{1,0:T(8,128)(2,1)S(1)}, bf16[1024,256]{1,0:T(8,128)(2,1)S(1)}, u32[]{:S(2)}, u32[]{:S(2)}) collective-permute-start(bf16[1024,256]{1,0:T(8,128)(2,1)S(1)} %get-tuple-element.16.rest_0_), channel_id=1, source_target_pairs={{0,8},{1,9},{2,10},{3,11},{4,12},{5,13},{6,14},{7,15},{8,16},{9,17... | collective-permute-start | bytes 1572872 | tf_op jit(solution)/shard_map/ppermute | solution.py:50
  61.1 15.4 %collective-permute-start.9 = (bf16[1024,256]{1,0:T(8,128)(2,1)S(1)}, bf16[1024,256]{1,0:T(8,128)(2,1)S(1)}, u32[]{:S(2)}, u32[]{:S(2)}) collective-permute-start(bf16[1024,256]{1,0:T(8,128)(2,1)S(1)} %get-tuple-element.16.rest_0_), channel_id=1, source_target_pairs={{0,24},{1,25},{2,26},{3,27},{4,28},{5,29},{6,30},{7,31},{8,0},{9,1... | collective-permute-start | bytes 1572872 | tf_op jit(solution)/shard_map/ppermute | solution.py:50
  74.9 10.2 %collective-permute-start.10 = (bf16[512,256]{1,0:T(8,128)(2,1)S(1)}, bf16[512,256]{1,0:T(8,128)(2,1)S(1)}, u32[]{:S(2)}, u32[]{:S(2)}) collective-permute-start(bf16[512,256]{1,0:T(8,128)(2,1)S(1)} %slice.70), channel_id=1, source_target_pairs={{0,8},{1,9},{2,10},{3,11},{4,12},{5,13},{6,14},{7,15},{8,16},{9,17... | collective-permute-start | bytes 786440 | tf_op jit(solution)/shard_map/ppermute | solution.py:50
  76.5 8.7 %collective-permute-start.11 = (bf16[512,256]{1,0:T(8,128)(2,1)S(1)}, bf16[512,256]{1,0:T(8,128)(2,1)S(1)}, u32[]{:S(2)}, u32[]{:S(2)}) collective-permute-start(bf16[512,256]{1,0:T(8,128)(2,1)S(1)} %slice.71), channel_id=1, source_target_pairs={{0,24},{1,25},{2,26},{3,27},{4,28},{5,29},{6,30},{7,31},{8,0},{9,1... | collective-permute-start | bytes 786440 | tf_op jit(solution)/shard_map/ppermute | solution.py:50
  85.2 31.2 %copy-start.3 = (bf16[1,128,1024]{2,1,0:T(8,128)(2,1)S(1)}, bf16[1,128,1024]{2,1,0:T(8,128)(2,1)}, u32[]{:S(2)}) copy-start(bf16[1,128,1024]{2,1,0:T(8,128)(2,1)} %hist_ref.3) | copy-start | bytes 786436
  85.2 31.2 %copy-start.5 = (bf16[1,32,1024]{2,1,0:T(8,128)(2,1)S(1)}, bf16[1,32,1024]{2,1,0:T(8,128)(2,1)}, u32[]{:S(2)}) copy-start(bf16[1,32,1024]{2,1,0:T(8,128)(2,1)} %cand_ref.3) | copy-start | bytes 196612
  89.9 26.5 %all-to-all-start.1 = ((bf16[8,160,256]{2,1,0:T(8,128)(2,1)}), bf16[8,160,256]{2,1,0:T(8,128)(2,1)S(1)}, u32[]{:S(2)}, u32[]{:S(2)}) async-start(bf16[8,160,256]{2,1,0:T(8,128)(2,1)} %attend.5), calls=%async_computation.1 | async-start | bytes 1310720 | tf_op jit(solution)/shard_map/all_to_all | solution.py:456
  116.4 1.6 %copy-start = (bf16[1024,1024]{1,0:T(8,128)(2,1)S(1)}, bf16[1024,1024]{1,0:T(8,128)(2,1)}, u32[]{:S(2)}) copy-start(bf16[1024,1024]{1,0:T(8,128)(2,1)} %all-gather.4.cloned.1.call-done.w_hbm) | copy-start | bytes 6291460
  (1 other events, 0.7 us)
Sparse Core Ops, SparseCore 0:
  12.9 43.5 all-gather.5
  58.9 40.1 all-gather.3

commit v7 on v6

--- a/solution.py
+++ b/solution.py
@@ -81,7 +81,6 @@
         in_specs=[VM] * 4 + [HBM],
         out_specs=[VM] * 3,
         scratch_shapes=[pltpu.VMEM((DEPTH, HD), BF16), pltpu.SemaphoreType.DMA(())],
-        compiler_params=params(6),
         cost_estimate=pl.CostEstimate(flops=8 * ROWS * D, bytes_accessed=4 * ROWS * D, transcendentals=0),
         name="norm_rows",
     )(hist, cand, events, requests, w_proj)
@@ -93,7 +92,8 @@
     first = lax.axis_index("seq") >> bit & 1 == 0
     out_ref[:count] = jnp.where(first, mine_ref[...], other_ref[...])
     out_ref[count:] = jnp.where(first, other_ref[...], mine_ref[...])
-    wout_out[...] = wout_ref[...]
+    half = wout_out.shape[0]
+    wout_out[...] = wout_ref[pl.ds(pl.multiple_of(position()[2] * half, half), half), :]
 
 
 def merge(mine, other, bit, w_out, ties):
@@ -101,7 +101,7 @@
         functools.partial(merge_kernel, bit=bit),
         out_shape=[
             jax.ShapeDtypeStruct((2 * mine.shape[0], mine.shape[1]), mine.dtype),
-            jax.ShapeDtypeStruct(w_out.shape, w_out.dtype),
+            jax.ShapeDtypeStruct((w_out.shape[0] // NC, D), w_out.dtype),
         ],
         in_specs=[VM] * (3 + len(ties)),
         out_specs=[VM] * 2,
@@ -345,35 +345,41 @@
     )(*tables, *queries, sums, col, *kvs, *tks, *gates)
 
 
-def finish_kernel(hist_ref, cand_ref, pair_ref, w_hbm, hist_out, cand_out, w_ref, sem):
-    copy = pltpu.make_async_copy(w_hbm, w_ref, sem)
-    copy.start()
+def finish_kernel(hist_ref, cand_ref, pair_ref, mine_ref, other_ref, hist_out, cand_out, w_ref, sems):
+    core = position()[2]
+    copies = [
+        pltpu.make_async_copy(mine_ref, w_ref.at[:, core], sems.at[0]),
+        pltpu.make_async_copy(other_ref, w_ref.at[:, 1 - core], sems.at[1]),
+    ]
+    for copy in copies:
+        copy.start()
     parts = [pair_ref[h, :, :HD].astype(F32) for h in range(HEADS)]
     center = sum(jnp.sum(part, axis=-1, keepdims=True) for part in parts) * (1.0 / D)
     parts = [part - center for part in parts]
     spread = sum(jnp.sum(part * part, axis=-1, keepdims=True) for part in parts) * (1.0 / D)
     scale = lax.rsqrt(spread + 1e-6)
     parts = [(part * scale * pair_ref[h, :, HD:].astype(F32)).astype(BF16) for h, part in enumerate(parts)]
-    copy.wait()
-    total = jnp.dot(jnp.concatenate(parts, axis=1), w_ref[...], preferred_element_type=F32)
+    for copy in copies:
+        copy.wait()
+    total = jnp.dot(jnp.concatenate(parts, axis=1), w_ref[...].reshape(D, D), preferred_element_type=F32)
     hist_out[0] = (hist_ref[0].astype(F32) + total[:HIST]).astype(BF16)
     cand_out[0] = (cand_ref[0].astype(F32) + total[HIST:]).astype(BF16)
 
 
-def finish(hist, cand, w_out, pairs):
+def finish(hist, cand, mine, other, pairs):
     return pl.pallas_call(
         finish_kernel,
         out_shape=[
             jax.ShapeDtypeStruct((1, HIST, D), BF16),
             jax.ShapeDtypeStruct((1, CAND, D), BF16),
         ],
-        in_specs=[VM] * 3 + [HBM],
+        in_specs=[VM] * 3 + [HBM] * 2,
         out_specs=[VM, VM],
-        scratch_shapes=[pltpu.VMEM((D, D), BF16), pltpu.SemaphoreType.DMA(())],
+        scratch_shapes=[pltpu.VMEM((NB, NC, D // NB // NC, D), BF16), pltpu.SemaphoreType.DMA((2,))],
         compiler_params=params(12),
         cost_estimate=pl.CostEstimate(flops=2 * ROWS * D * D, bytes_accessed=4 << 20, transcendentals=0),
         name="finish",
-    )(hist, cand, pairs, w_out)
+    )(hist, cand, pairs, mine, other)
 
 
 def gather_weights(shards, z):
@@ -399,7 +405,8 @@
         other = lax.ppermute(times, "seq", [(s, s ^ (1 << bit)) for s in range(NS)])
         if bit == order[-2]:
             times, w_mine = merge(times, other, bit, w_out, w_parts[1:])
-            w_full = lax.all_gather(w_mine, "batch", axis=0, tiled=True)
+            w_half = lax.all_gather(w_mine, "batch")
+            w_other = shift(w_half, flip=True)
         else:
             first = seq >> bit & 1 == 0
             times = jnp.concatenate([jnp.where(first, times, other), jnp.where(first, other, times)], axis=0)
@@ -454,7 +461,7 @@
     sums = attend(tables, queries, sums, col, [[kv1], [kv2]], tks[1:3], 1)
     att = attend(tables, queries, sums, col, [[kv3a, kv3b]], tks[3:], 3, gates)
     atts = lax.all_to_all(att, "seq", 0, 0, axis_index_groups=SAME_X)
-    return tuple(finish(history, candidates, w_full, atts))
+    return tuple(finish(history, candidates, w_half, w_other, atts))
 
 
 def solution(mesh):

time: 128 us -> 125 us (0.977)
  local copies, waits for them, and re-layouts: 8.9 us -> 4.22 us
  Pallas kernels: 27.6 us -> 29 us
    unnamed x18 -> x8, local copies, waits for them, and re-layouts: 5.92 us -> 1.24 us
    ppermute x7 -> x8, waiting for transfers between devices: 7.58 us -> 11.3 us  [shift(): return lax.ppermute(array, 'seq', seq_perm(dx, dz, flip))]
    all_gather x1, waiting for transfers between devices: 4.07 us -> 0.92 us  [body(): w_half = lax.all_gather(w_mine, 'batch')]
    pallas_call x1, Pallas kernels: 1.22 us -> 2.82 us  [norm_rows(): pl.pallas_call(norm_kernel, out_shape=[jax.ShapeDtypeStruct((ROWS, D), BF...]
    ppermute x7 -> x8, starting transfers between devices: 7.55 us -> 7.56 us  [shift(): return lax.ppermute(array, 'seq', seq_perm(dx, dz, flip))]
  transfers between devices with their start and end apart: 16 -> 17, of which waited for: 9 -> 10; matrix products, arithmetic and copies ran while one was open for 8% -> 9% of each run, Pallas kernels for 19% -> 20%
where the time goes in v7:
time: 125 us; the launch traced here: 124 us
  waiting for transfers between devices  36.9 us (30%)
  starting transfers between devices  31 us (25%)
  Pallas kernels  29 us (23%)
  between operations  15 us (12%)
  other arithmetic  7.88 us (6%)
  local copies, waits for them, and re-layouts  4.22 us (3%)
    pallas_call x3, Pallas kernels, attend(): pl.pallas_call(functools.partial(attend_kernel, fresh=fresh, last=last, c...  19.8 us
    all_to_all x1, waiting for transfers between devices, body(): atts = lax.all_to_all(att, 'seq', 0, 0, axis_index_groups=SAME_X)  17.4 us
    ppermute x5, starting transfers between devices, body(): other = lax.ppermute(times, 'seq', [(s, s ^ 1 << bit) for s in range(NS)])  11.9 us
    ppermute x8, waiting for transfers between devices, shift(): return lax.ppermute(array, 'seq', seq_perm(dx, dz, flip))  11.3 us
    ppermute x8, starting transfers between devices, shift(): return lax.ppermute(array, 'seq', seq_perm(dx, dz, flip))  7.56 us
    ppermute x5, waiting for transfers between devices, body(): other = lax.ppermute(times, 'seq', [(s, s ^ 1 << bit) for s in range(NS)])  6.17 us
    all_to_all x1, starting transfers between devices, gather_weights(): shards = lax.all_to_all(shards, 'batch', 0, 0)  6.05 us
    all_to_all x1, starting transfers between devices, body(): atts = lax.all_to_all(att, 'seq', 0, 0, axis_index_groups=SAME_X)  5.43 us
  transfers between devices with their start and end apart: 17, of which 10 were waited for; matrix products, arithmetic and copies ran while one was open for 9% of the time, Pallas kernels for 20%

profile of v7, /device:TPU:30, one launch (start us, length us, event | category | flops | bytes accessed | tf_op | source)
XLA Modules:
  0.0 124.0 jit_solution(3384014982595648122)
XLA Ops:
  7.2 2.8 %norm_rows.1 = (bf16[160,1024]{1,0:T(8,128)(2,1)}, s32[1,256]{1,0:T(1,128)}, bf16[8,256,128]{2,1,0:T(8,128)(2,1)}) custom-call(bf16[1,128,1024]{2,1,0:T(8,128)(2,1)} %hist_ref.3, bf16[1,32,1024]{2,1,0:T(8,128)(2,1)} %cand_ref.3, s32[1,128]{1,0:T(1,128)} %events_ref.1, s32[1,32]{1,0:T(1,128)} %requests_ref.1, bf16[1024,512]{1,0:T(8,128)(2,1)} %proj_ref.1), custom_call_target="tpu_custom_call" | custom-call | flops 1310720 | bytes 655360 | tf_op jit(solution)/shard_map/norm_rows/pallas_call | solution.py:74
  10.1 6.1 %all-to-all-start = ((bf16[8,256,128]{2,1,0:T(8,128)(2,1)}), bf16[8,256,128]{2,1,0:T(8,128)(2,1)S(1)}, u32[]{:S(2)}, u32[]{:S(2)}) async-start(bf16[8,256,128]{2,1,0:T(8,128)(2,1)} %get-tuple-element.13), calls=%async_computation | async-start | bytes 1048576 | tf_op jit(solution)/shard_map/all_to_all | solution.py:386
  18.2 1.5 %convert_reduce_fusion = (s32[4,10,8]{2,1,0:T(8,128)S(1)}, s32[4,10,8]{2,1,0:T(8,128)S(1)}) fusion(s32[4,10,8]{2,1,0:T(8,128)S(1)} %get-tuple-element.50, s32[12]{0:T(128)S(1)} %get-tuple-element.59, s32[4,10,8]{2,1,0:T(8,128)S(1)} %get-tuple-element.49), kind=kLoop, calls=%fused_computation.9 | loop fusion | flops 22400 | bytes 5168 | tf_op jit(solution)/shard_map/reduce_sum | solution.py:430
  20.8 1.3 %collective-permute-start.1 = (s32[2,256]{1,0:T(2,128)S(1)}, s32[2,256]{1,0:T(2,128)S(1)}, u32[]{:S(2)}, u32[]{:S(2)}) collective-permute-start(s32[2,256]{1,0:T(2,128)S(1)} %pad_add_fusion.6), channel_id=1, source_target_pairs={{0,16},{1,17},{2,18},{3,19},{4,20},{5,21},{6,22},{7,23},{8,24},{9,... | collective-permute-start | bytes 6152 | tf_op jit(solution)/shard_map/ppermute | solution.py:405
  22.1 3.8 %collective-permute-done.1 = s32[2,256]{1,0:T(2,128)S(1)} collective-permute-done((s32[2,256]{1,0:T(2,128)S(1)}, s32[2,256]{1,0:T(2,128)S(1)}, u32[]{:S(2)}, u32[]{:S(2)}) %collective-permute-start.1) | collective-permute-done | bytes 2080 | tf_op jit(solution)/shard_map/ppermute | solution.py:405
  26.1 1.2 collective-permute-start.4
  28.2 1.2 %collective-permute-start.6 = (bf16[4,256,128]{2,1,0:T(8,128)(2,1)S(1)}, bf16[4,256,128]{2,1,0:T(8,128)(2,1)S(1)}, u32[]{:S(2)}, u32[]{:S(2)}) collective-permute-start(bf16[4,256,128]{2,1,0:T(8,128)(2,1)S(1)} %dynamic-slice_bitcast_fusion.refs_0_), channel_id=1, source_target_pairs={{0,16},{1,17},{2,18},{3,19},{4,20},{5,21},{6,22},{7,23},{8,24},{9,... | collective-permute-start | bytes 786440 | tf_op jit(solution)/shard_map/ppermute | solution.py:50
  29.5 3.4 %collective-permute-start.3 = (s32[8,256]{1,0:T(8,128)S(1)}, s32[8,256]{1,0:T(8,128)S(1)}, u32[]{:S(2)}, u32[]{:S(2)}) collective-permute-start(s32[8,256]{1,0:T(8,128)S(1)} %pad_add_fusion.4.mine_ref), channel_id=1, source_target_pairs={{0,2},{1,3},{2,0},{3,1},{4,6},{5,7},{6,4},{7,5},{8,10},{9,11},{10,... | collective-permute-start | bytes 24584 | tf_op jit(solution)/shard_map/ppermute | solution.py:405
  32.9 1.8 %collective-permute-done.3.other_ref = s32[8,256]{1,0:T(8,128)S(1)} collective-permute-done((s32[8,256]{1,0:T(8,128)S(1)}, s32[8,256]{1,0:T(8,128)S(1)}, u32[]{:S(2)}, u32[]{:S(2)}) %collective-permute-start.3) | collective-permute-done | bytes 8224 | tf_op jit(solution)/shard_map/ppermute | solution.py:405
  35.3 7.3 %collective-permute-done.5.rest_1_.refs_2_ = bf16[4,256,128]{2,1,0:T(8,128)(2,1)S(1)} collective-permute-done((bf16[4,256,128]{2,1,0:T(8,128)(2,1)S(1)}, bf16[4,256,128]{2,1,0:T(8,128)(2,1)S(1)}, u32[]{:S(2)}, u32[]{:S(2)}) %collective-permute-start.5) | collective-permute-done | bytes 262176 | tf_op jit(solution)/shard_map/ppermute | solution.py:50
  43.2 6.3 %collective-permute-start.7 = (s32[16,256]{1,0:T(8,128)S(1)}, s32[16,256]{1,0:T(8,128)S(1)}, u32[]{:S(2)}, u32[]{:S(2)}) collective-permute-start(s32[16,256]{1,0:T(8,128)S(1)} %get-tuple-element.14), channel_id=1, source_target_pairs={{0,4},{1,5},{2,6},{3,7},{4,0},{5,1},{6,2},{7,3},{8,12},{9,13},{10,... | collective-permute-start | bytes 49160 | tf_op jit(solution)/shard_map/ppermute | solution.py:405
  52.7 1.1 all-gather.5.cloned.1.call-done
  53.8 3.5 %project.1 = (bf16[1024,128]{1,0:T(8,128)(2,1)S(1)}, bf16[256,128]{1,0:T(8,128)(2,1)S(1)}, bf16[1024,256]{1,0:T(8,128)(2,1)S(1)}, f32[256,128]{1,0:T(8,128)S(1)}, bf16[8,160,128]{2,1,0:T(8,128)(2,1)S(1)}) custom-call(bf16[8,160,1024]{2,1,0:T(8,128)(2,1)} %bitcast.41, bf16[4,256,128]{2,1,0:T(8,128)(2,1)S(1)} %dynamic-slice_bitcast_fusion.refs_0_, ...), custom_call_target="tpu_custom_call" | custom-call | flops 1342177280 | bytes 6291456 | tf_op jit(solution)/shard_map/project/pallas_call | solution.py:192
  58.4 1.5 %collective-permute-start.9 = (bf16[1024,256]{1,0:T(8,128)(2,1)S(1)}, bf16[1024,256]{1,0:T(8,128)(2,1)S(1)}, u32[]{:S(2)}, u32[]{:S(2)}) collective-permute-start(bf16[1024,256]{1,0:T(8,128)(2,1)S(1)} %get-tuple-element.16.rest_0_), channel_id=1, source_target_pairs={{0,24},{1,25},{2,26},{3,27},{4,28},{5,29},{6,30},{7,31},{8,0},{9,1... | collective-permute-start | bytes 1572872 | tf_op jit(solution)/shard_map/ppermute | solution.py:50
  61.1 1.5 %convert_reduce_fusion.2 = (s32[4,10,8]{2,1,0:T(8,128)S(1)}, s32[4,10,8]{2,1,0:T(8,128)S(1)}) fusion(s32[4,10,8]{2,1,0:T(8,128)S(1)} %broadcast_subtract_fusion, s32[12]{0:T(128)S(1)} %get-tuple-element.60, s32[4,10,8]{2,1,0:T(8,128)S(1)} %broadcast_subtract_fusion.1), kind=kLoop, calls=%fused_computation.11 | loop fusion | flops 22400 | bytes 5168 | tf_op jit(solution)/shard_map/reduce_sum | solution.py:430
  64.8 7.4 %attend.3.sums_in = f32[1280,128]{1,0:T(8,128)S(1)} custom-call(s32[20]{0:T(128)S(1)} %reshape.404.count_ref, s32[320]{0:T(512)S(1)} %reshape_reshape.4.work_ref, f32[320]{0:T(512)S(1)} %select_n.330.base_ref, f32[24]{0:T(128)S(1)} %fusion.12.steps_ref, bf16[1024,128]{1,0:T(8,128)(2,1)S(1)} %get-tuple-element.17.qh_ref, ...), custom_call_target="tpu_custom_call" | custom-call | flops 2684354560 | bytes 5242880 | tf_op jit(solution)/shard_map/attend/pallas_call | solution.py:334
  72.2 1.6 %collective-permute-start.10 = (bf16[512,256]{1,0:T(8,128)(2,1)S(1)}, bf16[512,256]{1,0:T(8,128)(2,1)S(1)}, u32[]{:S(2)}, u32[]{:S(2)}) collective-permute-start(bf16[512,256]{1,0:T(8,128)(2,1)S(1)} %slice.70), channel_id=1, source_target_pairs={{0,8},{1,9},{2,10},{3,11},{4,12},{5,13},{6,14},{7,15},{8,16},{9,17... | collective-permute-start | bytes 786440 | tf_op jit(solution)/shard_map/ppermute | solution.py:50
  74.4 7.7 %attend.4.sums_in = f32[1280,128]{1,0:T(8,128)S(1)} custom-call(s32[20]{0:T(128)S(1)} %reshape.404.count_ref, s32[320]{0:T(512)S(1)} %reshape_reshape.4.work_ref, f32[320]{0:T(512)S(1)} %select_n.330.base_ref, f32[24]{0:T(128)S(1)} %fusion.12.steps_ref, bf16[1024,128]{1,0:T(8,128)(2,1)S(1)} %get-tuple-element.17.qh_ref, ...), custom_call_target="tpu_custom_call" | custom-call | flops 5368709120 | bytes 10485760 | tf_op jit(solution)/shard_map/attend/pallas_call | solution.py:334
  82.6 4.7 %attend.5 = bf16[8,160,256]{2,1,0:T(8,128)(2,1)} custom-call(s32[20]{0:T(128)S(1)} %reshape.404.count_ref, s32[320]{0:T(512)S(1)} %reshape_reshape.4.work_ref, f32[320]{0:T(512)S(1)} %select_n.330.base_ref, f32[24]{0:T(128)S(1)} %fusion.12.steps_ref, bf16[1024,128]{1,0:T(8,128)(2,1)S(1)} %get-tuple-element.17.qh_ref, ...), custom_call_target="tpu_custom_call" | custom-call | flops 2684354560 | bytes 5242880 | tf_op jit(solution)/shard_map/attend/pallas_call | solution.py:334
  87.4 5.4 %all-to-all-start.1 = ((bf16[8,160,256]{2,1,0:T(8,128)(2,1)}), bf16[8,160,256]{2,1,0:T(8,128)(2,1)S(1)}, u32[]{:S(2)}, u32[]{:S(2)}) async-start(bf16[8,160,256]{2,1,0:T(8,128)(2,1)} %attend.5), calls=%async_computation.1 | async-start | bytes 1310720 | tf_op jit(solution)/shard_map/all_to_all | solution.py:463
  93.7 2.9 %collective-permute-done.12.other_ref = bf16[8,64,1024]{2,1,0:T(8,128)(2,1)S(1)} collective-permute-done((bf16[8,64,1024]{2,1,0:T(8,128)(2,1)}, bf16[8,64,1024]{2,1,0:T(8,128)(2,1)S(1)}, u32[]{:S(2)}, u32[]{:S(2)}) %collective-permute-start.12) | collective-permute-done | bytes 1048608 | tf_op jit(solution)/shard_map/ppermute | solution.py:50
  96.6 17.4 %all-to-all-done.1.pair_ref = bf16[8,160,256]{2,1,0:T(8,128)(2,1)S(1)} async-done(((bf16[8,160,256]{2,1,0:T(8,128)(2,1)}), bf16[8,160,256]{2,1,0:T(8,128)(2,1)S(1)}, u32[]{:S(2)}, u32[]{:S(2)}) %all-to-all-start.1) | async-done | bytes 655392 | tf_op jit(solution)/shard_map/all_to_all | solution.py:463
  114.0 1.2 copy-done
  115.2 1.9 %finish.1 = (bf16[1,128,1024]{2,1,0:T(8,128)(2,1)}, bf16[1,32,1024]{2,1,0:T(8,128)(2,1)}) custom-call(bf16[1,128,1024]{2,1,0:T(8,128)(2,1)S(1)} %copy-done.1, bf16[1,32,1024]{2,1,0:T(8,128)(2,1)S(1)} %copy-done.2, bf16[8,160,256]{2,1,0:T(8,128)(2,1)S(1)} %all-to-all-done.1.pair_ref, bf16[8,64,1024]{2,1,0:T(8,128)(2,1)S(1)} %bitcast.34, ...), custom_call_target="tpu_custom_call" | custom-call | flops 335544320 | bytes 4194304 | tf_op jit(solution)/shard_map/finish/pallas_call | solution.py:370
  (107 shorter events, 14.3 us)
Async XLA Ops:
  7.2 35.4 %copy-start.3 = (bf16[128,1024]{1,0:T(8,128)(2,1)S(1)}, bf16[128,1024]{1,0:T(8,128)(2,1)}, u32[]{:S(2)}) copy-start(bf16[128,1024]{1,0:T(8,128)(2,1)} %wout_ref.1) | copy-start | bytes 786436
  7.2 46.7 %all-gather.5.cloned.1.call-start = ((), (), s32[]{:S(2)}) async-start(), calls=%async_computation.2 | async-start | bytes 2949120 | tf_op jit(solution)/shard_map/all_gather | solution.py:397
  10.1 16.0 %all-to-all-start = ((bf16[8,256,128]{2,1,0:T(8,128)(2,1)}), bf16[8,256,128]{2,1,0:T(8,128)(2,1)S(1)}, u32[]{:S(2)}, u32[]{:S(2)}) async-start(bf16[8,256,128]{2,1,0:T(8,128)(2,1)} %get-tuple-element.13), calls=%async_computation | async-start | bytes 1048576 | tf_op jit(solution)/shard_map/all_to_all | solution.py:386
  16.1 77.6 %all-gather.7.cloned.1.call-start = ((), (), s32[]{:S(2)}) async-start(), calls=%async_computation.3 | async-start | bytes 1179648 | tf_op jit(solution)/shard_map/all_gather | solution.py:408
  16.1 3.9 %collective-permute-start = (s32[1,256]{1,0:T(1,128)}, s32[1,256]{1,0:T(1,128)S(1)}, u32[]{:S(2)}, u32[]{:S(2)}) collective-permute-start(s32[1,256]{1,0:T(1,128)} %get-tuple-element.12), channel_id=1, source_target_pairs={{0,8},{1,9},{2,10},{3,11},{4,12},{5,13},{6,14},{7,15},{8,0},{9,1},... | collective-permute-start | bytes 3080 | tf_op jit(solution)/shard_map/ppermute | solution.py:405
  20.8 5.2 %collective-permute-start.1 = (s32[2,256]{1,0:T(2,128)S(1)}, s32[2,256]{1,0:T(2,128)S(1)}, u32[]{:S(2)}, u32[]{:S(2)}) collective-permute-start(s32[2,256]{1,0:T(2,128)S(1)} %pad_add_fusion.6), channel_id=1, source_target_pairs={{0,16},{1,17},{2,18},{3,19},{4,20},{5,21},{6,22},{7,23},{8,24},{9,... | collective-permute-start | bytes 6152 | tf_op jit(solution)/shard_map/ppermute | solution.py:405
  26.0 3.5 %collective-permute-start.2 = (s32[4,256]{1,0:T(4,128)S(1)}, s32[4,256]{1,0:T(4,128)S(1)}, u32[]{:S(2)}, u32[]{:S(2)}) collective-permute-start(s32[4,256]{1,0:T(4,128)S(1)} %pad_add_fusion.5), channel_id=1, source_target_pairs={{0,1},{1,0},{2,3},{3,2},{4,5},{5,4},{6,7},{7,6},{8,9},{9,8},{10,11... | collective-permute-start | bytes 12296 | tf_op jit(solution)/shard_map/ppermute | solution.py:405
  26.1 9.2 %collective-permute-start.4 = (bf16[4,256,128]{2,1,0:T(8,128)(2,1)S(1)}, bf16[4,256,128]{2,1,0:T(8,128)(2,1)S(1)}, u32[]{:S(2)}, u32[]{:S(2)}) collective-permute-start(bf16[4,256,128]{2,1,0:T(8,128)(2,1)S(1)} %dynamic-slice_bitcast_fusion.refs_0_), channel_id=1, source_target_pairs={{0,8},{1,9},{2,10},{3,11},{4,12},{5,13},{6,14},{7,15},{8,16},{9,17... | collective-permute-start | bytes 786440 | tf_op jit(solution)/shard_map/ppermute | solution.py:50
  27.3 15.2 %collective-permute-start.5 = (bf16[4,256,128]{2,1,0:T(8,128)(2,1)S(1)}, bf16[4,256,128]{2,1,0:T(8,128)(2,1)S(1)}, u32[]{:S(2)}, u32[]{:S(2)}) collective-permute-start(bf16[4,256,128]{2,1,0:T(8,128)(2,1)S(1)} %dynamic-slice_bitcast_fusion.refs_0_), channel_id=1, source_target_pairs={{0,24},{1,25},{2,26},{3,27},{4,28},{5,29},{6,30},{7,31},{8,0},{9,1... | collective-permute-start | bytes 786440 | tf_op jit(solution)/shard_map/ppermute | solution.py:50
  28.2 14.4 %collective-permute-start.6 = (bf16[4,256,128]{2,1,0:T(8,128)(2,1)S(1)}, bf16[4,256,128]{2,1,0:T(8,128)(2,1)S(1)}, u32[]{:S(2)}, u32[]{:S(2)}) collective-permute-start(bf16[4,256,128]{2,1,0:T(8,128)(2,1)S(1)} %dynamic-slice_bitcast_fusion.refs_0_), channel_id=1, source_target_pairs={{0,16},{1,17},{2,18},{3,19},{4,20},{5,21},{6,22},{7,23},{8,24},{9,... | collective-permute-start | bytes 786440 | tf_op jit(solution)/shard_map/ppermute | solution.py:50
  29.5 5.1 %collective-permute-start.3 = (s32[8,256]{1,0:T(8,128)S(1)}, s32[8,256]{1,0:T(8,128)S(1)}, u32[]{:S(2)}, u32[]{:S(2)}) collective-permute-start(s32[8,256]{1,0:T(8,128)S(1)} %pad_add_fusion.4.mine_ref), channel_id=1, source_target_pairs={{0,2},{1,3},{2,0},{3,1},{4,6},{5,7},{6,4},{7,5},{8,10},{9,11},{10,... | collective-permute-start | bytes 24584 | tf_op jit(solution)/shard_map/ppermute | solution.py:405
  43.2 8.4 %collective-permute-start.7 = (s32[16,256]{1,0:T(8,128)S(1)}, s32[16,256]{1,0:T(8,128)S(1)}, u32[]{:S(2)}, u32[]{:S(2)}) collective-permute-start(s32[16,256]{1,0:T(8,128)S(1)} %get-tuple-element.14), channel_id=1, source_target_pairs={{0,4},{1,5},{2,6},{3,7},{4,0},{5,1},{6,2},{7,3},{8,12},{9,13},{10,... | collective-permute-start | bytes 49160 | tf_op jit(solution)/shard_map/ppermute | solution.py:405
  57.9 14.3 %collective-permute-start.8 = (bf16[1024,256]{1,0:T(8,128)(2,1)S(1)}, bf16[1024,256]{1,0:T(8,128)(2,1)S(1)}, u32[]{:S(2)}, u32[]{:S(2)}) collective-permute-start(bf16[1024,256]{1,0:T(8,128)(2,1)S(1)} %get-tuple-element.16.rest_0_), channel_id=1, source_target_pairs={{0,8},{1,9},{2,10},{3,11},{4,12},{5,13},{6,14},{7,15},{8,16},{9,17... | collective-permute-start | bytes 1572872 | tf_op jit(solution)/shard_map/ppermute | solution.py:50
  58.4 15.4 %collective-permute-start.9 = (bf16[1024,256]{1,0:T(8,128)(2,1)S(1)}, bf16[1024,256]{1,0:T(8,128)(2,1)S(1)}, u32[]{:S(2)}, u32[]{:S(2)}) collective-permute-start(bf16[1024,256]{1,0:T(8,128)(2,1)S(1)} %get-tuple-element.16.rest_0_), channel_id=1, source_target_pairs={{0,24},{1,25},{2,26},{3,27},{4,28},{5,29},{6,30},{7,31},{8,0},{9,1... | collective-permute-start | bytes 1572872 | tf_op jit(solution)/shard_map/ppermute | solution.py:50
  72.2 10.0 %collective-permute-start.10 = (bf16[512,256]{1,0:T(8,128)(2,1)S(1)}, bf16[512,256]{1,0:T(8,128)(2,1)S(1)}, u32[]{:S(2)}, u32[]{:S(2)}) collective-permute-start(bf16[512,256]{1,0:T(8,128)(2,1)S(1)} %slice.70), channel_id=1, source_target_pairs={{0,8},{1,9},{2,10},{3,11},{4,12},{5,13},{6,14},{7,15},{8,16},{9,17... | collective-permute-start | bytes 786440 | tf_op jit(solution)/shard_map/ppermute | solution.py:50
  73.9 8.8 %collective-permute-start.11 = (bf16[512,256]{1,0:T(8,128)(2,1)S(1)}, bf16[512,256]{1,0:T(8,128)(2,1)S(1)}, u32[]{:S(2)}, u32[]{:S(2)}) collective-permute-start(bf16[512,256]{1,0:T(8,128)(2,1)S(1)} %slice.71), channel_id=1, source_target_pairs={{0,24},{1,25},{2,26},{3,27},{4,28},{5,29},{6,30},{7,31},{8,0},{9,1... | collective-permute-start | bytes 786440 | tf_op jit(solution)/shard_map/ppermute | solution.py:50
  82.6 31.4 %copy-start.1 = (bf16[1,128,1024]{2,1,0:T(8,128)(2,1)S(1)}, bf16[1,128,1024]{2,1,0:T(8,128)(2,1)}, u32[]{:S(2)}) copy-start(bf16[1,128,1024]{2,1,0:T(8,128)(2,1)} %hist_ref.3) | copy-start | bytes 786436
  82.6 31.4 %copy-start.2 = (bf16[1,32,1024]{2,1,0:T(8,128)(2,1)S(1)}, bf16[1,32,1024]{2,1,0:T(8,128)(2,1)}, u32[]{:S(2)}) copy-start(bf16[1,32,1024]{2,1,0:T(8,128)(2,1)} %cand_ref.3) | copy-start | bytes 196612
  87.4 26.6 %all-to-all-start.1 = ((bf16[8,160,256]{2,1,0:T(8,128)(2,1)}), bf16[8,160,256]{2,1,0:T(8,128)(2,1)S(1)}, u32[]{:S(2)}, u32[]{:S(2)}) async-start(bf16[8,160,256]{2,1,0:T(8,128)(2,1)} %attend.5), calls=%async_computation.1 | async-start | bytes 1310720 | tf_op jit(solution)/shard_map/all_to_all | solution.py:463
  93.7 2.9 %collective-permute-start.12 = (bf16[8,64,1024]{2,1,0:T(8,128)(2,1)}, bf16[8,64,1024]{2,1,0:T(8,128)(2,1)S(1)}, u32[]{:S(2)}, u32[]{:S(2)}) collective-permute-start(bf16[8,64,1024]{2,1,0:T(8,128)(2,1)} %bitcast.33), channel_id=1, source_target_pairs={{0,1},{1,0},{2,3},{3,2},{4,5},{5,4},{6,7},{7,6},{8,9},{9,8},{10,11... | collective-permute-start | bytes 3145736 | tf_op jit(solution)/shard_map/ppermute | solution.py:50
  114.0 1.2 copy-start
Sparse Core Ops, SparseCore 0:
  10.2 43.5 all-gather.4
  56.2 37.4 all-gather.6

commit v8 on v7

--- a/solution.py
+++ b/solution.py
@@ -420,11 +420,10 @@
 
     steps = 0.5 * lax.dynamic_slice(bias_steps, (0, head), (2 * LEVELS, 1))[:, 0]
     level = jnp.arange(LEVELS, dtype=I32)
-    tie = (kv0[0, 0] * 0).astype(I32)
-    tk = jnp.stack(tks) + tie
-    tq = jnp.concatenate([k0, cand_times, jnp.zeros((6, 128), I32)], axis=0) + tie
-    first_q = jnp.concatenate([k0[:, 0], jnp.min(cand_times, axis=1)]) + tie
-    last_q = jnp.concatenate([k0[:, -1], jnp.max(cand_times, axis=1)]) + tie
+    tk = jnp.stack(tks)
+    tq = jnp.concatenate([k0, cand_times, jnp.zeros((6, 128), I32)], axis=0)
+    first_q = jnp.concatenate([k0[:, 0], jnp.min(cand_times, axis=1)])
+    last_q = jnp.concatenate([k0[:, -1], jnp.max(cand_times, axis=1)])
 
     def passed(gap, marks):
         return jnp.sum((gap[..., None] >= marks).astype(I32), axis=-1)

time: 125 us -> 125 us (level)
  starting transfers between devices: 31 us -> 32.5 us
    ppermute x8, waiting for transfers between devices: 11.3 us -> 12.7 us  [shift(): return lax.ppermute(array, 'seq', seq_perm(dx, dz, flip))]
  transfers between devices with their start and end apart: 17 -> 17, of which waited for: 10 -> 9; matrix products, arithmetic and copies ran while one was open for 9% -> 8% of each run, Pallas kernels for 20% -> 19%
where the time goes in v8:
time: 125 us
  waiting for transfers between devices  37.3 us (30%)
  starting transfers between devices  32.5 us (26%)
  Pallas kernels  29 us (23%)
  between operations  14.4 us (12%)
  other arithmetic  7.88 us (6%)
  local copies, waits for them, and re-layouts  3.71 us (3%)
    pallas_call x3, Pallas kernels, attend(): pl.pallas_call(functools.partial(attend_kernel, fresh=fresh, last=last, c...  19.8 us
    all_to_all x1, waiting for transfers between devices, body(): atts = lax.all_to_all(att, 'seq', 0, 0, axis_index_groups=SAME_X)  18.2 us
    ppermute x8, waiting for transfers between devices, shift(): return lax.ppermute(array, 'seq', seq_perm(dx, dz, flip))  12.7 us
    ppermute x5, starting transfers between devices, body(): other = lax.ppermute(times, 'seq', [(s, s ^ 1 << bit) for s in range(NS)])  11.9 us
    ppermute x8, starting transfers between devices, shift(): return lax.ppermute(array, 'seq', seq_perm(dx, dz, flip))  8.26 us
    all_to_all x1, starting transfers between devices, body(): atts = lax.all_to_all(att, 'seq', 0, 0, axis_index_groups=SAME_X)  6.34 us
    ppermute x5, waiting for transfers between devices, body(): other = lax.ppermute(times, 'seq', [(s, s ^ 1 << bit) for s in range(NS)])  6.27 us
    all_to_all x1, starting transfers between devices, gather_weights(): shards = lax.all_to_all(shards, 'batch', 0, 0)  6.04 us
  transfers between devices with their start and end apart: 17, of which 9 were waited for; matrix products, arithmetic and copies ran while one was open for 8% of the time, Pallas kernels for 19%

profile of v8, /device:TPU:30, one launch (start us, length us, event | category | flops | bytes accessed | tf_op | source)
XLA Modules:
  0.0 124.8 jit_solution(6831164288824418063)
XLA Ops:
  7.2 2.8 %norm_rows.1 = (bf16[160,1024]{1,0:T(8,128)(2,1)}, s32[1,256]{1,0:T(1,128)}, bf16[8,256,128]{2,1,0:T(8,128)(2,1)}) custom-call(bf16[1,128,1024]{2,1,0:T(8,128)(2,1)} %hist_ref.3, bf16[1,32,1024]{2,1,0:T(8,128)(2,1)} %cand_ref.3, s32[1,128]{1,0:T(1,128)} %events_ref.1, s32[1,32]{1,0:T(1,128)} %requests_ref.1, bf16[1024,512]{1,0:T(8,128)(2,1)} %proj_ref.1), custom_call_target="tpu_custom_call" | custom-call | flops 1310720 | bytes 655360 | tf_op jit(solution)/shard_map/norm_rows/pallas_call | solution.py:74
  11.0 6.0 %all-to-all-start = ((bf16[8,256,128]{2,1,0:T(8,128)(2,1)}), bf16[8,256,128]{2,1,0:T(8,128)(2,1)S(1)}, u32[]{:S(2)}, u32[]{:S(2)}) async-start(bf16[8,256,128]{2,1,0:T(8,128)(2,1)} %get-tuple-element.13), calls=%async_computation | async-start | bytes 1048576 | tf_op jit(solution)/shard_map/all_to_all | solution.py:386
  18.3 1.5 %convert_reduce_fusion = (s32[4,10,8]{2,1,0:T(8,128)S(1)}, s32[4,10,8]{2,1,0:T(8,128)S(1)}) fusion(s32[4,10,8]{2,1,0:T(8,128)S(1)} %get-tuple-element.50, s32[12]{0:T(128)S(1)} %get-tuple-element.59, s32[4,10,8]{2,1,0:T(8,128)S(1)} %get-tuple-element.49), kind=kLoop, calls=%fused_computation.9 | loop fusion | flops 22400 | bytes 5168 | tf_op jit(solution)/shard_map/reduce_sum | solution.py:429
  20.9 1.2 collective-permute-start.1
  22.1 4.0 %collective-permute-done.1 = s32[2,256]{1,0:T(2,128)S(1)} collective-permute-done((s32[2,256]{1,0:T(2,128)S(1)}, s32[2,256]{1,0:T(2,128)S(1)}, u32[]{:S(2)}, u32[]{:S(2)}) %collective-permute-start.1) | collective-permute-done | bytes 2080 | tf_op jit(solution)/shard_map/ppermute | solution.py:405
  26.2 1.2 collective-permute-start.4
  28.3 1.2 collective-permute-start.6
  29.6 3.4 %collective-permute-start.3 = (s32[8,256]{1,0:T(8,128)S(1)}, s32[8,256]{1,0:T(8,128)S(1)}, u32[]{:S(2)}, u32[]{:S(2)}) collective-permute-start(s32[8,256]{1,0:T(8,128)S(1)} %pad_add_fusion.5.mine_ref), channel_id=1, source_target_pairs={{0,2},{1,3},{2,0},{3,1},{4,6},{5,7},{6,4},{7,5},{8,10},{9,11},{10,... | collective-permute-start | bytes 24584 | tf_op jit(solution)/shard_map/ppermute | solution.py:405
  32.9 1.8 %collective-permute-done.3.other_ref = s32[8,256]{1,0:T(8,128)S(1)} collective-permute-done((s32[8,256]{1,0:T(8,128)S(1)}, s32[8,256]{1,0:T(8,128)S(1)}, u32[]{:S(2)}, u32[]{:S(2)}) %collective-permute-start.3) | collective-permute-done | bytes 8224 | tf_op jit(solution)/shard_map/ppermute | solution.py:405
  35.4 7.3 %collective-permute-done.5.rest_1_.refs_2_ = bf16[4,256,128]{2,1,0:T(8,128)(2,1)S(1)} collective-permute-done((bf16[4,256,128]{2,1,0:T(8,128)(2,1)S(1)}, bf16[4,256,128]{2,1,0:T(8,128)(2,1)S(1)}, u32[]{:S(2)}, u32[]{:S(2)}) %collective-permute-start.5) | collective-permute-done | bytes 262176 | tf_op jit(solution)/shard_map/ppermute | solution.py:50
  43.3 6.3 %collective-permute-start.7 = (s32[16,256]{1,0:T(8,128)S(1)}, s32[16,256]{1,0:T(8,128)S(1)}, u32[]{:S(2)}, u32[]{:S(2)}) collective-permute-start(s32[16,256]{1,0:T(8,128)S(1)} %get-tuple-element.14), channel_id=1, source_target_pairs={{0,4},{1,5},{2,6},{3,7},{4,0},{5,1},{6,2},{7,3},{8,12},{9,13},{10,... | collective-permute-start | bytes 49160 | tf_op jit(solution)/shard_map/ppermute | solution.py:405
  53.1 1.5 %convert_reduce_fusion.2 = (s32[4,10,8]{2,1,0:T(8,128)S(1)}, s32[4,10,8]{2,1,0:T(8,128)S(1)}) fusion(s32[4,10,8]{2,1,0:T(8,128)S(1)} %broadcast_subtract_fusion, s32[12]{0:T(128)S(1)} %get-tuple-element.60, s32[4,10,8]{2,1,0:T(8,128)S(1)} %broadcast_subtract_fusion.1), kind=kLoop, calls=%fused_computation.11 | loop fusion | flops 22400 | bytes 5168 | tf_op jit(solution)/shard_map/reduce_sum | solution.py:429
  55.9 3.5 %project.1 = (bf16[1024,128]{1,0:T(8,128)(2,1)S(1)}, bf16[256,128]{1,0:T(8,128)(2,1)S(1)}, bf16[1024,256]{1,0:T(8,128)(2,1)S(1)}, f32[256,128]{1,0:T(8,128)S(1)}, bf16[8,160,128]{2,1,0:T(8,128)(2,1)S(1)}) custom-call(bf16[8,160,1024]{2,1,0:T(8,128)(2,1)} %bitcast.39, bf16[4,256,128]{2,1,0:T(8,128)(2,1)S(1)} %dynamic-slice_bitcast_fusion.refs_0_, ...), custom_call_target="tpu_custom_call" | custom-call | flops 1342177280 | bytes 6291456 | tf_op jit(solution)/shard_map/project/pallas_call | solution.py:192
  60.3 1.4 %collective-permute-start.9 = (bf16[1024,256]{1,0:T(8,128)(2,1)S(1)}, bf16[1024,256]{1,0:T(8,128)(2,1)S(1)}, u32[]{:S(2)}, u32[]{:S(2)}) collective-permute-start(bf16[1024,256]{1,0:T(8,128)(2,1)S(1)} %get-tuple-element.19.rest_0_), channel_id=1, source_target_pairs={{0,24},{1,25},{2,26},{3,27},{4,28},{5,29},{6,30},{7,31},{8,0},{9,1... | collective-permute-start | bytes 1572872 | tf_op jit(solution)/shard_map/ppermute | solution.py:50
  62.8 7.4 %attend.3.sums_in = f32[1280,128]{1,0:T(8,128)S(1)} custom-call(s32[20]{0:T(128)S(1)} %reshape.370.count_ref, s32[320]{0:T(512)S(1)} %reshape_reshape.4.work_ref, f32[320]{0:T(512)S(1)} %select_n.330.base_ref, f32[24]{0:T(128)S(1)} %fusion.12.steps_ref, bf16[1024,128]{1,0:T(8,128)(2,1)S(1)} %get-tuple-element.16.qh_ref, ...), custom_call_target="tpu_custom_call" | custom-call | flops 2684354560 | bytes 5242880 | tf_op jit(solution)/shard_map/attend/pallas_call | solution.py:334
  70.3 2.3 %collective-permute-done.8.rest_0_ = bf16[1024,256]{1,0:T(8,128)(2,1)S(1)} collective-permute-done((bf16[1024,256]{1,0:T(8,128)(2,1)S(1)}, bf16[1024,256]{1,0:T(8,128)(2,1)S(1)}, u32[]{:S(2)}, u32[]{:S(2)}) %collective-permute-start.8) | collective-permute-done | bytes 524320 | tf_op jit(solution)/shard_map/ppermute | solution.py:50
  72.6 1.9 %collective-permute-start.10 = (bf16[512,256]{1,0:T(8,128)(2,1)S(1)}, bf16[512,256]{1,0:T(8,128)(2,1)S(1)}, u32[]{:S(2)}, u32[]{:S(2)}) collective-permute-start(bf16[512,256]{1,0:T(8,128)(2,1)S(1)} %slice.66), channel_id=1, source_target_pairs={{0,8},{1,9},{2,10},{3,11},{4,12},{5,13},{6,14},{7,15},{8,16},{9,17... | collective-permute-start | bytes 786440 | tf_op jit(solution)/shard_map/ppermute | solution.py:50
  74.8 7.6 %attend.4.sums_in = f32[1280,128]{1,0:T(8,128)S(1)} custom-call(s32[20]{0:T(128)S(1)} %reshape.370.count_ref, s32[320]{0:T(512)S(1)} %reshape_reshape.4.work_ref, f32[320]{0:T(512)S(1)} %select_n.330.base_ref, f32[24]{0:T(128)S(1)} %fusion.12.steps_ref, bf16[1024,128]{1,0:T(8,128)(2,1)S(1)} %get-tuple-element.16.qh_ref, ...), custom_call_target="tpu_custom_call" | custom-call | flops 5368709120 | bytes 10485760 | tf_op jit(solution)/shard_map/attend/pallas_call | solution.py:334
  82.5 4.8 %attend.5 = bf16[8,160,256]{2,1,0:T(8,128)(2,1)} custom-call(s32[20]{0:T(128)S(1)} %reshape.370.count_ref, s32[320]{0:T(512)S(1)} %reshape_reshape.4.work_ref, f32[320]{0:T(512)S(1)} %select_n.330.base_ref, f32[24]{0:T(128)S(1)} %fusion.12.steps_ref, bf16[1024,128]{1,0:T(8,128)(2,1)S(1)} %get-tuple-element.16.qh_ref, ...), custom_call_target="tpu_custom_call" | custom-call | flops 2684354560 | bytes 5242880 | tf_op jit(solution)/shard_map/attend/pallas_call | solution.py:334
  87.2 6.3 %all-to-all-start.1 = ((bf16[8,160,256]{2,1,0:T(8,128)(2,1)}), bf16[8,160,256]{2,1,0:T(8,128)(2,1)S(1)}, u32[]{:S(2)}, u32[]{:S(2)}) async-start(bf16[8,160,256]{2,1,0:T(8,128)(2,1)} %attend.5), calls=%async_computation.1 | async-start | bytes 1310720 | tf_op jit(solution)/shard_map/all_to_all | solution.py:462
  94.1 2.5 %collective-permute-done.12.other_ref = bf16[8,64,1024]{2,1,0:T(8,128)(2,1)S(1)} collective-permute-done((bf16[8,64,1024]{2,1,0:T(8,128)(2,1)}, bf16[8,64,1024]{2,1,0:T(8,128)(2,1)S(1)}, u32[]{:S(2)}, u32[]{:S(2)}) %collective-permute-start.12) | collective-permute-done | bytes 1048608 | tf_op jit(solution)/shard_map/ppermute | solution.py:50
  96.6 18.2 %all-to-all-done.1.pair_ref = bf16[8,160,256]{2,1,0:T(8,128)(2,1)S(1)} async-done(((bf16[8,160,256]{2,1,0:T(8,128)(2,1)}), bf16[8,160,256]{2,1,0:T(8,128)(2,1)S(1)}, u32[]{:S(2)}, u32[]{:S(2)}) %all-to-all-start.1) | async-done | bytes 655392 | tf_op jit(solution)/shard_map/all_to_all | solution.py:462
  114.8 1.2 copy-done
  116.0 1.9 %finish.1 = (bf16[1,128,1024]{2,1,0:T(8,128)(2,1)}, bf16[1,32,1024]{2,1,0:T(8,128)(2,1)}) custom-call(bf16[1,128,1024]{2,1,0:T(8,128)(2,1)S(1)} %copy-done.1, bf16[1,32,1024]{2,1,0:T(8,128)(2,1)S(1)} %copy-done.2, bf16[8,160,256]{2,1,0:T(8,128)(2,1)S(1)} %all-to-all-done.1.pair_ref, bf16[8,64,1024]{2,1,0:T(8,128)(2,1)S(1)} %bitcast.32, ...), custom_call_target="tpu_custom_call" | custom-call | flops 335544320 | bytes 4194304 | tf_op jit(solution)/shard_map/finish/pallas_call | solution.py:370
  (106 shorter events, 13.1 us)
Async XLA Ops:
  7.2 35.5 %copy-start.3 = (bf16[128,1024]{1,0:T(8,128)(2,1)S(1)}, bf16[128,1024]{1,0:T(8,128)(2,1)}, u32[]{:S(2)}) copy-start(bf16[128,1024]{1,0:T(8,128)(2,1)} %wout_ref.1) | copy-start | bytes 786436
  7.2 48.8 %all-gather.5.cloned.1.call-start = ((), (), s32[]{:S(2)}) async-start(), calls=%async_computation.2 | async-start | bytes 2949120 | tf_op jit(solution)/shard_map/all_gather | solution.py:397
  10.1 10.1 %collective-permute-start = (s32[1,256]{1,0:T(1,128)}, s32[1,256]{1,0:T(1,128)S(1)}, u32[]{:S(2)}, u32[]{:S(2)}) collective-permute-start(s32[1,256]{1,0:T(1,128)} %get-tuple-element.12), channel_id=1, source_target_pairs={{0,8},{1,9},{2,10},{3,11},{4,12},{5,13},{6,14},{7,15},{8,0},{9,1},... | collective-permute-start | bytes 3080 | tf_op jit(solution)/shard_map/ppermute | solution.py:405
  11.0 15.2 %all-to-all-start = ((bf16[8,256,128]{2,1,0:T(8,128)(2,1)}), bf16[8,256,128]{2,1,0:T(8,128)(2,1)S(1)}, u32[]{:S(2)}, u32[]{:S(2)}) async-start(bf16[8,256,128]{2,1,0:T(8,128)(2,1)} %get-tuple-element.13), calls=%async_computation | async-start | bytes 1048576 | tf_op jit(solution)/shard_map/all_to_all | solution.py:386
  17.0 76.6 %all-gather.7.cloned.1.call-start = ((), (), s32[]{:S(2)}) async-start(), calls=%async_computation.3 | async-start | bytes 1179648 | tf_op jit(solution)/shard_map/all_gather | solution.py:408
  20.9 5.2 %collective-permute-start.1 = (s32[2,256]{1,0:T(2,128)S(1)}, s32[2,256]{1,0:T(2,128)S(1)}, u32[]{:S(2)}, u32[]{:S(2)}) collective-permute-start(s32[2,256]{1,0:T(2,128)S(1)} %pad_add_fusion.7), channel_id=1, source_target_pairs={{0,16},{1,17},{2,18},{3,19},{4,20},{5,21},{6,22},{7,23},{8,24},{9,... | collective-permute-start | bytes 6152 | tf_op jit(solution)/shard_map/ppermute | solution.py:405
  26.1 3.5 %collective-permute-start.2 = (s32[4,256]{1,0:T(4,128)S(1)}, s32[4,256]{1,0:T(4,128)S(1)}, u32[]{:S(2)}, u32[]{:S(2)}) collective-permute-start(s32[4,256]{1,0:T(4,128)S(1)} %pad_add_fusion.6), channel_id=1, source_target_pairs={{0,1},{1,0},{2,3},{3,2},{4,5},{5,4},{6,7},{7,6},{8,9},{9,8},{10,11... | collective-permute-start | bytes 12296 | tf_op jit(solution)/shard_map/ppermute | solution.py:405
  26.2 9.2 %collective-permute-start.4 = (bf16[4,256,128]{2,1,0:T(8,128)(2,1)S(1)}, bf16[4,256,128]{2,1,0:T(8,128)(2,1)S(1)}, u32[]{:S(2)}, u32[]{:S(2)}) collective-permute-start(bf16[4,256,128]{2,1,0:T(8,128)(2,1)S(1)} %dynamic-slice_bitcast_fusion.refs_0_), channel_id=1, source_target_pairs={{0,8},{1,9},{2,10},{3,11},{4,12},{5,13},{6,14},{7,15},{8,16},{9,17... | collective-permute-start | bytes 786440 | tf_op jit(solution)/shard_map/ppermute | solution.py:50
  27.4 15.2 %collective-permute-start.5 = (bf16[4,256,128]{2,1,0:T(8,128)(2,1)S(1)}, bf16[4,256,128]{2,1,0:T(8,128)(2,1)S(1)}, u32[]{:S(2)}, u32[]{:S(2)}) collective-permute-start(bf16[4,256,128]{2,1,0:T(8,128)(2,1)S(1)} %dynamic-slice_bitcast_fusion.refs_0_), channel_id=1, source_target_pairs={{0,24},{1,25},{2,26},{3,27},{4,28},{5,29},{6,30},{7,31},{8,0},{9,1... | collective-permute-start | bytes 786440 | tf_op jit(solution)/shard_map/ppermute | solution.py:50
  28.3 14.4 %collective-permute-start.6 = (bf16[4,256,128]{2,1,0:T(8,128)(2,1)S(1)}, bf16[4,256,128]{2,1,0:T(8,128)(2,1)S(1)}, u32[]{:S(2)}, u32[]{:S(2)}) collective-permute-start(bf16[4,256,128]{2,1,0:T(8,128)(2,1)S(1)} %dynamic-slice_bitcast_fusion.refs_0_), channel_id=1, source_target_pairs={{0,16},{1,17},{2,18},{3,19},{4,20},{5,21},{6,22},{7,23},{8,24},{9,... | collective-permute-start | bytes 786440 | tf_op jit(solution)/shard_map/ppermute | solution.py:50
  29.6 5.1 %collective-permute-start.3 = (s32[8,256]{1,0:T(8,128)S(1)}, s32[8,256]{1,0:T(8,128)S(1)}, u32[]{:S(2)}, u32[]{:S(2)}) collective-permute-start(s32[8,256]{1,0:T(8,128)S(1)} %pad_add_fusion.5.mine_ref), channel_id=1, source_target_pairs={{0,2},{1,3},{2,0},{3,1},{4,6},{5,7},{6,4},{7,5},{8,10},{9,11},{10,... | collective-permute-start | bytes 24584 | tf_op jit(solution)/shard_map/ppermute | solution.py:405
  43.3 8.3 %collective-permute-start.7 = (s32[16,256]{1,0:T(8,128)S(1)}, s32[16,256]{1,0:T(8,128)S(1)}, u32[]{:S(2)}, u32[]{:S(2)}) collective-permute-start(s32[16,256]{1,0:T(8,128)S(1)} %get-tuple-element.14), channel_id=1, source_target_pairs={{0,4},{1,5},{2,6},{3,7},{4,0},{5,1},{6,2},{7,3},{8,12},{9,13},{10,... | collective-permute-start | bytes 49160 | tf_op jit(solution)/shard_map/ppermute | solution.py:405
  59.5 13.1 %collective-permute-start.8 = (bf16[1024,256]{1,0:T(8,128)(2,1)S(1)}, bf16[1024,256]{1,0:T(8,128)(2,1)S(1)}, u32[]{:S(2)}, u32[]{:S(2)}) collective-permute-start(bf16[1024,256]{1,0:T(8,128)(2,1)S(1)} %get-tuple-element.19.rest_0_), channel_id=1, source_target_pairs={{0,8},{1,9},{2,10},{3,11},{4,12},{5,13},{6,14},{7,15},{8,16},{9,17... | collective-permute-start | bytes 1572872 | tf_op jit(solution)/shard_map/ppermute | solution.py:50
  60.3 14.2 %collective-permute-start.9 = (bf16[1024,256]{1,0:T(8,128)(2,1)S(1)}, bf16[1024,256]{1,0:T(8,128)(2,1)S(1)}, u32[]{:S(2)}, u32[]{:S(2)}) collective-permute-start(bf16[1024,256]{1,0:T(8,128)(2,1)S(1)} %get-tuple-element.19.rest_0_), channel_id=1, source_target_pairs={{0,24},{1,25},{2,26},{3,27},{4,28},{5,29},{6,30},{7,31},{8,0},{9,1... | collective-permute-start | bytes 1572872 | tf_op jit(solution)/shard_map/ppermute | solution.py:50
  72.6 9.9 %collective-permute-start.10 = (bf16[512,256]{1,0:T(8,128)(2,1)S(1)}, bf16[512,256]{1,0:T(8,128)(2,1)S(1)}, u32[]{:S(2)}, u32[]{:S(2)}) collective-permute-start(bf16[512,256]{1,0:T(8,128)(2,1)S(1)} %slice.66), channel_id=1, source_target_pairs={{0,8},{1,9},{2,10},{3,11},{4,12},{5,13},{6,14},{7,15},{8,16},{9,17... | collective-permute-start | bytes 786440 | tf_op jit(solution)/shard_map/ppermute | solution.py:50
  74.5 8.0 %collective-permute-start.11 = (bf16[512,256]{1,0:T(8,128)(2,1)S(1)}, bf16[512,256]{1,0:T(8,128)(2,1)S(1)}, u32[]{:S(2)}, u32[]{:S(2)}) collective-permute-start(bf16[512,256]{1,0:T(8,128)(2,1)S(1)} %slice.67), channel_id=1, source_target_pairs={{0,24},{1,25},{2,26},{3,27},{4,28},{5,29},{6,30},{7,31},{8,0},{9,1... | collective-permute-start | bytes 786440 | tf_op jit(solution)/shard_map/ppermute | solution.py:50
  82.5 32.3 %copy-start.1 = (bf16[1,128,1024]{2,1,0:T(8,128)(2,1)S(1)}, bf16[1,128,1024]{2,1,0:T(8,128)(2,1)}, u32[]{:S(2)}) copy-start(bf16[1,128,1024]{2,1,0:T(8,128)(2,1)} %hist_ref.3) | copy-start | bytes 786436
  82.5 32.3 %copy-start.2 = (bf16[1,32,1024]{2,1,0:T(8,128)(2,1)S(1)}, bf16[1,32,1024]{2,1,0:T(8,128)(2,1)}, u32[]{:S(2)}) copy-start(bf16[1,32,1024]{2,1,0:T(8,128)(2,1)} %cand_ref.3) | copy-start | bytes 196612
  87.2 27.5 %all-to-all-start.1 = ((bf16[8,160,256]{2,1,0:T(8,128)(2,1)}), bf16[8,160,256]{2,1,0:T(8,128)(2,1)S(1)}, u32[]{:S(2)}, u32[]{:S(2)}) async-start(bf16[8,160,256]{2,1,0:T(8,128)(2,1)} %attend.5), calls=%async_computation.1 | async-start | bytes 1310720 | tf_op jit(solution)/shard_map/all_to_all | solution.py:462
  93.6 3.0 %collective-permute-start.12 = (bf16[8,64,1024]{2,1,0:T(8,128)(2,1)}, bf16[8,64,1024]{2,1,0:T(8,128)(2,1)S(1)}, u32[]{:S(2)}, u32[]{:S(2)}) collective-permute-start(bf16[8,64,1024]{2,1,0:T(8,128)(2,1)} %bitcast.31), channel_id=1, source_target_pairs={{0,1},{1,0},{2,3},{3,2},{4,5},{5,4},{6,7},{7,6},{8,9},{9,8},{10,11... | collective-permute-start | bytes 3145736 | tf_op jit(solution)/shard_map/ppermute | solution.py:50
  114.8 1.2 copy-start
Sparse Core Ops, SparseCore 0:
  10.2 43.6 all-gather.4
  56.2 37.3 all-gather.6

commit v9 on v7

--- a/solution.py
+++ b/solution.py
@@ -50,13 +50,7 @@
     return lax.ppermute(array, "seq", seq_perm(dx, dz, flip))
 
 
-def norm_kernel(hist_ref, cand_ref, events_ref, requests_ref, proj_ref, out_ref, times_ref, shards_ref, part_ref, sem):
-    x, z, core = position()
-    column = pl.multiple_of((NC * z + core) % 4 * HD, HD)
-    copy = pltpu.make_async_copy(
-        proj_ref.at[pl.ds(pl.multiple_of(x * DEPTH, DEPTH), DEPTH), pl.ds(column, HD)], part_ref, sem
-    )
-    copy.start()
+def norm_kernel(hist_ref, cand_ref, events_ref, requests_ref, out_ref, times_ref):
     for ref, first, count in ((hist_ref, 0, HIST), (cand_ref, HIST, CAND)):
         rows = ref[0].astype(F32)
         rows = rows - jnp.mean(rows, axis=-1, keepdims=True)
@@ -65,25 +59,41 @@
     times_ref[...] = jnp.zeros_like(times_ref)
     times_ref[:, :HIST] = events_ref[...]
     times_ref[:, HIST:ROWS] = requests_ref[...]
+
+
+def norm_rows(hist, cand, events, requests):
+    return pl.pallas_call(
+        norm_kernel,
+        out_shape=[jax.ShapeDtypeStruct((ROWS, D), BF16), jax.ShapeDtypeStruct((1, 2 * HIST), I32)],
+        in_specs=[VM] * 4,
+        out_specs=[VM] * 2,
+        cost_estimate=pl.CostEstimate(flops=8 * ROWS * D, bytes_accessed=4 * ROWS * D, transcendentals=0),
+        name="norm_rows",
+    )(hist, cand, events, requests)
+
+
+def shards_kernel(tie_ref, proj_ref, shards_ref, part_ref, sem):
+    x, z, core = position()
+    column = pl.multiple_of((NC * z + core) % 4 * HD, HD)
+    copy = pltpu.make_async_copy(
+        proj_ref.at[pl.ds(pl.multiple_of(x * DEPTH, DEPTH), DEPTH), pl.ds(column, HD)], part_ref, sem
+    )
+    copy.start()
     copy.wait()
     for b in range(NB):
         shards_ref[b] = part_ref[...]
 
 
-def norm_rows(hist, cand, events, requests, w_proj):
-    return pl.pallas_call(
-        norm_kernel,
-        out_shape=[
-            jax.ShapeDtypeStruct((ROWS, D), BF16),
-            jax.ShapeDtypeStruct((1, 2 * HIST), I32),
-            jax.ShapeDtypeStruct((NB, DEPTH, HD), BF16),
-        ],
-        in_specs=[VM] * 4 + [HBM],
-        out_specs=[VM] * 3,
+def make_shards(tie, w_proj):
+    return pl.pallas_call(
+        shards_kernel,
+        out_shape=jax.ShapeDtypeStruct((NB, DEPTH, HD), BF16),
+        in_specs=[HBM] * 2,
+        out_specs=VM,
         scratch_shapes=[pltpu.VMEM((DEPTH, HD), BF16), pltpu.SemaphoreType.DMA(())],
-        cost_estimate=pl.CostEstimate(flops=8 * ROWS * D, bytes_accessed=4 * ROWS * D, transcendentals=0),
-        name="norm_rows",
-    )(hist, cand, events, requests, w_proj)
+        cost_estimate=pl.CostEstimate(flops=1 << 10, bytes_accessed=1 << 19, transcendentals=0),
+        name="make_shards",
+    )(tie, w_proj)
 
 
 def merge_kernel(mine_ref, other_ref, wout_ref, *rest, bit):
@@ -393,10 +403,10 @@
     head = NC * z + core
     xs = jnp.stack([(x + off) % NX for off in OFF])
 
-    n0, t0, shards = norm_rows(history, candidates, event_times, request_times, w_proj)
+    n0, t0 = norm_rows(history, candidates, event_times, request_times)
     rows = lax.all_gather(n0, "seq", axis_index_groups=SAME_X)
 
-    w0 = gather_weights(shards, z)
+    w0 = gather_weights(make_shards(t0, w_proj), z)
     w_parts = [w0, shift(w0, dx=1), shift(w0, dx=-1), shift(w0, dx=2)]
 
     times = t0

time: 125 us -> 125 us (level)
    pallas_call x0 -> x1, Pallas kernels: none -> 1.73 us  [make_shards(): pl.pallas_call(shards_kernel, out_shape=jax.ShapeDtypeStruct((NB, DEPTH,...]
    ppermute x5, waiting for transfers between devices: 6.17 us -> 7.76 us  [body(): other = lax.ppermute(times, 'seq', [(s, s ^ 1 << bit) for s in range(NS)])]
    ppermute x8, waiting for transfers between devices: 11.3 us -> 9.77 us  [shift(): return lax.ppermute(array, 'seq', seq_perm(dx, dz, flip))]
  transfers between devices with their start and end apart: 17 -> 17, of which waited for: 10 -> 6; matrix products, arithmetic and copies ran while one was open for 9% -> 8% of each run, Pallas kernels for 20% -> 21%
where the time goes in v9:
time: 125 us; the launch traced here: 124 us
  waiting for transfers between devices  35.8 us (29%)
  starting transfers between devices  32.2 us (26%)
  Pallas kernels  30 us (24%)
  between operations  15.1 us (12%)
  other arithmetic  7.2 us (6%)
  local copies, waits for them, and re-layouts  4.23 us (3%)
    pallas_call x3, Pallas kernels, attend(): pl.pallas_call(functools.partial(attend_kernel, fresh=fresh, last=last, c...  19.9 us
    all_to_all x1, waiting for transfers between devices, body(): atts = lax.all_to_all(att, 'seq', 0, 0, axis_index_groups=SAME_X)  18.2 us
    ppermute x5, starting transfers between devices, body(): other = lax.ppermute(times, 'seq', [(s, s ^ 1 << bit) for s in range(NS)])  11.9 us
    ppermute x8, waiting for transfers between devices, shift(): return lax.ppermute(array, 'seq', seq_perm(dx, dz, flip))  9.77 us
    ppermute x8, starting transfers between devices, shift(): return lax.ppermute(array, 'seq', seq_perm(dx, dz, flip))  8.03 us
    ppermute x5, waiting for transfers between devices, body(): other = lax.ppermute(times, 'seq', [(s, s ^ 1 << bit) for s in range(NS)])  7.76 us
    all_to_all x1, starting transfers between devices, body(): atts = lax.all_to_all(att, 'seq', 0, 0, axis_index_groups=SAME_X)  6.24 us
    all_to_all x1, starting transfers between devices, gather_weights(): shards = lax.all_to_all(shards, 'batch', 0, 0)  6.05 us
  transfers between devices with their start and end apart: 17, of which 6 were waited for; matrix products, arithmetic and copies ran while one was open for 8% of the time, Pallas kernels for 21%

profile of v9, /device:TPU:30, one launch (start us, length us, event | category | flops | bytes accessed | tf_op | source)
XLA Modules:
  0.0 124.5 jit_solution(10355812312410540249)
XLA Ops:
  7.2 2.0 %norm_rows.1 = (bf16[160,1024]{1,0:T(8,128)(2,1)}, s32[1,256]{1,0:T(1,128)}) custom-call(bf16[1,128,1024]{2,1,0:T(8,128)(2,1)} %hist_ref.3, bf16[1,32,1024]{2,1,0:T(8,128)(2,1)} %cand_ref.3, s32[1,128]{1,0:T(1,128)} %events_ref.1, s32[1,32]{1,0:T(1,128)} %requests_ref.1), custom_call_target="tpu_custom_call" | custom-call | flops 1310720 | bytes 655360 | tf_op jit(solution)/shard_map/norm_rows/pallas_call | solution.py:65
  10.2 1.7 %make_shards.1 = bf16[8,256,128]{2,1,0:T(8,128)(2,1)} custom-call(s32[1,256]{1,0:T(1,128)} %get-tuple-element.11.tie_ref, bf16[1024,512]{1,0:T(8,128)(2,1)} %proj_ref.1), custom_call_target="tpu_custom_call" | custom-call | flops 1024 | bytes 524288 | tf_op jit(solution)/shard_map/make_shards/pallas_call | solution.py:88
  11.9 6.1 %all-to-all-start = ((bf16[8,256,128]{2,1,0:T(8,128)(2,1)}), bf16[8,256,128]{2,1,0:T(8,128)(2,1)S(1)}, u32[]{:S(2)}, u32[]{:S(2)}) async-start(bf16[8,256,128]{2,1,0:T(8,128)(2,1)} %make_shards.1), calls=%async_computation | async-start | bytes 1048576 | tf_op jit(solution)/shard_map/all_to_all | solution.py:396
  19.2 1.5 %convert_reduce_fusion = (s32[4,10,8]{2,1,0:T(8,128)S(1)}, s32[4,10,8]{2,1,0:T(8,128)S(1)}) fusion(s32[4,10,8]{2,1,0:T(8,128)S(1)} %get-tuple-element.48, s32[12]{0:T(128)S(1)} %get-tuple-element.57, s32[4,10,8]{2,1,0:T(8,128)S(1)} %get-tuple-element.47), kind=kLoop, calls=%fused_computation.9 | loop fusion | flops 22400 | bytes 5168 | tf_op jit(solution)/shard_map/reduce_sum | solution.py:440
  22.3 4.0 %collective-permute-done.1 = s32[2,256]{1,0:T(2,128)S(1)} collective-permute-done((s32[2,256]{1,0:T(2,128)S(1)}, s32[2,256]{1,0:T(2,128)S(1)}, u32[]{:S(2)}, u32[]{:S(2)}) %collective-permute-start.1) | collective-permute-done | bytes 2080 | tf_op jit(solution)/shard_map/ppermute | solution.py:415
  26.5 1.2 collective-permute-start.4
  28.6 1.2 collective-permute-start.6
  29.9 3.4 %collective-permute-start.3 = (s32[8,256]{1,0:T(8,128)S(1)}, s32[8,256]{1,0:T(8,128)S(1)}, u32[]{:S(2)}, u32[]{:S(2)}) collective-permute-start(s32[8,256]{1,0:T(8,128)S(1)} %pad_add_fusion.4.mine_ref), channel_id=1, source_target_pairs={{0,2},{1,3},{2,0},{3,1},{4,6},{5,7},{6,4},{7,5},{8,10},{9,11},{10,... | collective-permute-start | bytes 24584 | tf_op jit(solution)/shard_map/ppermute | solution.py:415
  33.2 2.5 %collective-permute-done.3.other_ref = s32[8,256]{1,0:T(8,128)S(1)} collective-permute-done((s32[8,256]{1,0:T(8,128)S(1)}, s32[8,256]{1,0:T(8,128)S(1)}, u32[]{:S(2)}, u32[]{:S(2)}) %collective-permute-start.3) | collective-permute-done | bytes 8224 | tf_op jit(solution)/shard_map/ppermute | solution.py:415
  35.7 7.3 %collective-permute-done.5.rest_1_.refs_2_ = bf16[4,256,128]{2,1,0:T(8,128)(2,1)S(1)} collective-permute-done((bf16[4,256,128]{2,1,0:T(8,128)(2,1)S(1)}, bf16[4,256,128]{2,1,0:T(8,128)(2,1)S(1)}, u32[]{:S(2)}, u32[]{:S(2)}) %collective-permute-start.5) | collective-permute-done | bytes 262176 | tf_op jit(solution)/shard_map/ppermute | solution.py:50
  43.6 6.3 %collective-permute-start.7 = (s32[16,256]{1,0:T(8,128)S(1)}, s32[16,256]{1,0:T(8,128)S(1)}, u32[]{:S(2)}, u32[]{:S(2)}) collective-permute-start(s32[16,256]{1,0:T(8,128)S(1)} %get-tuple-element.12), channel_id=1, source_target_pairs={{0,4},{1,5},{2,6},{3,7},{4,0},{5,1},{6,2},{7,3},{8,12},{9,13},{10,... | collective-permute-start | bytes 49160 | tf_op jit(solution)/shard_map/ppermute | solution.py:415
  51.4 1.3 %collective-permute-done.7 = s32[16,256]{1,0:T(8,128)S(1)} collective-permute-done((s32[16,256]{1,0:T(8,128)S(1)}, s32[16,256]{1,0:T(8,128)S(1)}, u32[]{:S(2)}, u32[]{:S(2)}) %collective-permute-start.7) | collective-permute-done | bytes 16416 | tf_op jit(solution)/shard_map/ppermute | solution.py:415
  53.9 3.5 %project.1 = (bf16[1024,128]{1,0:T(8,128)(2,1)S(1)}, bf16[256,128]{1,0:T(8,128)(2,1)S(1)}, bf16[1024,256]{1,0:T(8,128)(2,1)S(1)}, f32[256,128]{1,0:T(8,128)S(1)}, bf16[8,160,128]{2,1,0:T(8,128)(2,1)S(1)}) custom-call(bf16[8,160,1024]{2,1,0:T(8,128)(2,1)} %bitcast.41, bf16[4,256,128]{2,1,0:T(8,128)(2,1)S(1)} %dynamic-slice_bitcast_fusion.refs_0_, ...), custom_call_target="tpu_custom_call" | custom-call | flops 1342177280 | bytes 6291456 | tf_op jit(solution)/shard_map/project/pallas_call | solution.py:202
  58.3 1.6 %collective-permute-start.9 = (bf16[1024,256]{1,0:T(8,128)(2,1)S(1)}, bf16[1024,256]{1,0:T(8,128)(2,1)S(1)}, u32[]{:S(2)}, u32[]{:S(2)}) collective-permute-start(bf16[1024,256]{1,0:T(8,128)(2,1)S(1)} %get-tuple-element.14.rest_0_), channel_id=1, source_target_pairs={{0,24},{1,25},{2,26},{3,27},{4,28},{5,29},{6,30},{7,31},{8,0},{9,1... | collective-permute-start | bytes 1572872 | tf_op jit(solution)/shard_map/ppermute | solution.py:50
  61.1 1.5 %convert_reduce_fusion.2 = (s32[4,10,8]{2,1,0:T(8,128)S(1)}, s32[4,10,8]{2,1,0:T(8,128)S(1)}) fusion(s32[4,10,8]{2,1,0:T(8,128)S(1)} %broadcast_subtract_fusion, s32[12]{0:T(128)S(1)} %get-tuple-element.58, s32[4,10,8]{2,1,0:T(8,128)S(1)} %broadcast_subtract_fusion.1), kind=kLoop, calls=%fused_computation.11 | loop fusion | flops 22400 | bytes 5168 | tf_op jit(solution)/shard_map/reduce_sum | solution.py:440
  64.8 7.4 %attend.3.sums_in = f32[1280,128]{1,0:T(8,128)S(1)} custom-call(s32[20]{0:T(128)S(1)} %reshape.404.count_ref, s32[320]{0:T(512)S(1)} %reshape_reshape.4.work_ref, f32[320]{0:T(512)S(1)} %select_n.330.base_ref, f32[24]{0:T(128)S(1)} %fusion.12.steps_ref, bf16[1024,128]{1,0:T(8,128)(2,1)S(1)} %get-tuple-element.15.qh_ref, ...), custom_call_target="tpu_custom_call" | custom-call | flops 2684354560 | bytes 5242880 | tf_op jit(solution)/shard_map/attend/pallas_call | solution.py:344
  73.2 1.3 %collective-permute-start.11 = (bf16[512,256]{1,0:T(8,128)(2,1)S(1)}, bf16[512,256]{1,0:T(8,128)(2,1)S(1)}, u32[]{:S(2)}, u32[]{:S(2)}) collective-permute-start(bf16[512,256]{1,0:T(8,128)(2,1)S(1)} %slice.71), channel_id=1, source_target_pairs={{0,24},{1,25},{2,26},{3,27},{4,28},{5,29},{6,30},{7,31},{8,0},{9,1... | collective-permute-start | bytes 786440 | tf_op jit(solution)/shard_map/ppermute | solution.py:50
  74.5 7.8 %attend.4.sums_in = f32[1280,128]{1,0:T(8,128)S(1)} custom-call(s32[20]{0:T(128)S(1)} %reshape.404.count_ref, s32[320]{0:T(512)S(1)} %reshape_reshape.4.work_ref, f32[320]{0:T(512)S(1)} %select_n.330.base_ref, f32[24]{0:T(128)S(1)} %fusion.12.steps_ref, bf16[1024,128]{1,0:T(8,128)(2,1)S(1)} %get-tuple-element.15.qh_ref, ...), custom_call_target="tpu_custom_call" | custom-call | flops 5368709120 | bytes 10485760 | tf_op jit(solution)/shard_map/attend/pallas_call | solution.py:344
  82.4 4.7 %attend.5 = bf16[8,160,256]{2,1,0:T(8,128)(2,1)} custom-call(s32[20]{0:T(128)S(1)} %reshape.404.count_ref, s32[320]{0:T(512)S(1)} %reshape_reshape.4.work_ref, f32[320]{0:T(512)S(1)} %select_n.330.base_ref, f32[24]{0:T(128)S(1)} %fusion.12.steps_ref, bf16[1024,128]{1,0:T(8,128)(2,1)S(1)} %get-tuple-element.15.qh_ref, ...), custom_call_target="tpu_custom_call" | custom-call | flops 2684354560 | bytes 5242880 | tf_op jit(solution)/shard_map/attend/pallas_call | solution.py:344
  87.1 6.2 %all-to-all-start.1 = ((bf16[8,160,256]{2,1,0:T(8,128)(2,1)}), bf16[8,160,256]{2,1,0:T(8,128)(2,1)S(1)}, u32[]{:S(2)}, u32[]{:S(2)}) async-start(bf16[8,160,256]{2,1,0:T(8,128)(2,1)} %attend.5), calls=%async_computation.1 | async-start | bytes 1310720 | tf_op jit(solution)/shard_map/all_to_all | solution.py:473
  93.8 2.5 %collective-permute-done.12.other_ref = bf16[8,64,1024]{2,1,0:T(8,128)(2,1)S(1)} collective-permute-done((bf16[8,64,1024]{2,1,0:T(8,128)(2,1)}, bf16[8,64,1024]{2,1,0:T(8,128)(2,1)S(1)}, u32[]{:S(2)}, u32[]{:S(2)}) %collective-permute-start.12) | collective-permute-done | bytes 1048608 | tf_op jit(solution)/shard_map/ppermute | solution.py:50
  96.3 18.2 %all-to-all-done.1.pair_ref = bf16[8,160,256]{2,1,0:T(8,128)(2,1)S(1)} async-done(((bf16[8,160,256]{2,1,0:T(8,128)(2,1)}), bf16[8,160,256]{2,1,0:T(8,128)(2,1)S(1)}, u32[]{:S(2)}, u32[]{:S(2)}) %all-to-all-start.1) | async-done | bytes 655392 | tf_op jit(solution)/shard_map/all_to_all | solution.py:473
  114.5 1.2 copy-done
  115.7 1.9 %finish.1 = (bf16[1,128,1024]{2,1,0:T(8,128)(2,1)}, bf16[1,32,1024]{2,1,0:T(8,128)(2,1)}) custom-call(bf16[1,128,1024]{2,1,0:T(8,128)(2,1)S(1)} %copy-done.1, bf16[1,32,1024]{2,1,0:T(8,128)(2,1)S(1)} %copy-done.2, bf16[8,160,256]{2,1,0:T(8,128)(2,1)S(1)} %all-to-all-done.1.pair_ref, bf16[8,64,1024]{2,1,0:T(8,128)(2,1)S(1)} %bitcast.34, ...), custom_call_target="tpu_custom_call" | custom-call | flops 335544320 | bytes 4194304 | tf_op jit(solution)/shard_map/finish/pallas_call | solution.py:380
  (110 shorter events, 13.0 us)
Async XLA Ops:
  7.2 35.8 %copy-start.3 = (bf16[128,1024]{1,0:T(8,128)(2,1)S(1)}, bf16[128,1024]{1,0:T(8,128)(2,1)}, u32[]{:S(2)}) copy-start(bf16[128,1024]{1,0:T(8,128)(2,1)} %wout_ref.1) | copy-start | bytes 786436
  7.2 46.7 %all-gather.5.cloned.1.call-start = ((), (), s32[]{:S(2)}) async-start(), calls=%async_computation.2 | async-start | bytes 2949120 | tf_op jit(solution)/shard_map/all_gather | solution.py:407
  9.2 11.9 %copy-start.4 = (s32[1,256]{1,0:T(1,128)S(1)}, s32[1,256]{1,0:T(1,128)}, u32[]{:S(2)}) copy-start(s32[1,256]{1,0:T(1,128)} %get-tuple-element.11.tie_ref) | copy-start | bytes 3076
  9.3 11.8 %collective-permute-start = (s32[1,256]{1,0:T(1,128)}, s32[1,256]{1,0:T(1,128)S(1)}, u32[]{:S(2)}, u32[]{:S(2)}) collective-permute-start(s32[1,256]{1,0:T(1,128)} %get-tuple-element.11.tie_ref), channel_id=1, source_target_pairs={{0,8},{1,9},{2,10},{3,11},{4,12},{5,13},{6,14},{7,15},{8,0},{9,1},... | collective-permute-start | bytes 3080 | tf_op jit(solution)/shard_map/ppermute | solution.py:415
  11.9 14.5 %all-to-all-start = ((bf16[8,256,128]{2,1,0:T(8,128)(2,1)}), bf16[8,256,128]{2,1,0:T(8,128)(2,1)S(1)}, u32[]{:S(2)}, u32[]{:S(2)}) async-start(bf16[8,256,128]{2,1,0:T(8,128)(2,1)} %make_shards.1), calls=%async_computation | async-start | bytes 1048576 | tf_op jit(solution)/shard_map/all_to_all | solution.py:396
  18.0 75.4 %all-gather.7.cloned.1.call-start = ((), (), s32[]{:S(2)}) async-start(), calls=%async_computation.3 | async-start | bytes 1179648 | tf_op jit(solution)/shard_map/all_gather | solution.py:418
  21.1 5.2 %collective-permute-start.1 = (s32[2,256]{1,0:T(2,128)S(1)}, s32[2,256]{1,0:T(2,128)S(1)}, u32[]{:S(2)}, u32[]{:S(2)}) collective-permute-start(s32[2,256]{1,0:T(2,128)S(1)} %pad_add_fusion.6), channel_id=1, source_target_pairs={{0,16},{1,17},{2,18},{3,19},{4,20},{5,21},{6,22},{7,23},{8,24},{9,... | collective-permute-start | bytes 6152 | tf_op jit(solution)/shard_map/ppermute | solution.py:415
  26.3 3.5 %collective-permute-start.2 = (s32[4,256]{1,0:T(4,128)S(1)}, s32[4,256]{1,0:T(4,128)S(1)}, u32[]{:S(2)}, u32[]{:S(2)}) collective-permute-start(s32[4,256]{1,0:T(4,128)S(1)} %pad_add_fusion.5), channel_id=1, source_target_pairs={{0,1},{1,0},{2,3},{3,2},{4,5},{5,4},{6,7},{7,6},{8,9},{9,8},{10,11... | collective-permute-start | bytes 12296 | tf_op jit(solution)/shard_map/ppermute | solution.py:415
  26.5 9.2 %collective-permute-start.4 = (bf16[4,256,128]{2,1,0:T(8,128)(2,1)S(1)}, bf16[4,256,128]{2,1,0:T(8,128)(2,1)S(1)}, u32[]{:S(2)}, u32[]{:S(2)}) collective-permute-start(bf16[4,256,128]{2,1,0:T(8,128)(2,1)S(1)} %dynamic-slice_bitcast_fusion.refs_0_), channel_id=1, source_target_pairs={{0,8},{1,9},{2,10},{3,11},{4,12},{5,13},{6,14},{7,15},{8,16},{9,17... | collective-permute-start | bytes 786440 | tf_op jit(solution)/shard_map/ppermute | solution.py:50
  27.7 15.2 %collective-permute-start.5 = (bf16[4,256,128]{2,1,0:T(8,128)(2,1)S(1)}, bf16[4,256,128]{2,1,0:T(8,128)(2,1)S(1)}, u32[]{:S(2)}, u32[]{:S(2)}) collective-permute-start(bf16[4,256,128]{2,1,0:T(8,128)(2,1)S(1)} %dynamic-slice_bitcast_fusion.refs_0_), channel_id=1, source_target_pairs={{0,24},{1,25},{2,26},{3,27},{4,28},{5,29},{6,30},{7,31},{8,0},{9,1... | collective-permute-start | bytes 786440 | tf_op jit(solution)/shard_map/ppermute | solution.py:50
  28.6 14.4 %collective-permute-start.6 = (bf16[4,256,128]{2,1,0:T(8,128)(2,1)S(1)}, bf16[4,256,128]{2,1,0:T(8,128)(2,1)S(1)}, u32[]{:S(2)}, u32[]{:S(2)}) collective-permute-start(bf16[4,256,128]{2,1,0:T(8,128)(2,1)S(1)} %dynamic-slice_bitcast_fusion.refs_0_), channel_id=1, source_target_pairs={{0,16},{1,17},{2,18},{3,19},{4,20},{5,21},{6,22},{7,23},{8,24},{9,... | collective-permute-start | bytes 786440 | tf_op jit(solution)/shard_map/ppermute | solution.py:50
  29.9 5.8 %collective-permute-start.3 = (s32[8,256]{1,0:T(8,128)S(1)}, s32[8,256]{1,0:T(8,128)S(1)}, u32[]{:S(2)}, u32[]{:S(2)}) collective-permute-start(s32[8,256]{1,0:T(8,128)S(1)} %pad_add_fusion.4.mine_ref), channel_id=1, source_target_pairs={{0,2},{1,3},{2,0},{3,1},{4,6},{5,7},{6,4},{7,5},{8,10},{9,11},{10,... | collective-permute-start | bytes 24584 | tf_op jit(solution)/shard_map/ppermute | solution.py:415
  43.6 9.1 %collective-permute-start.7 = (s32[16,256]{1,0:T(8,128)S(1)}, s32[16,256]{1,0:T(8,128)S(1)}, u32[]{:S(2)}, u32[]{:S(2)}) collective-permute-start(s32[16,256]{1,0:T(8,128)S(1)} %get-tuple-element.12), channel_id=1, source_target_pairs={{0,4},{1,5},{2,6},{3,7},{4,0},{5,1},{6,2},{7,3},{8,12},{9,13},{10,... | collective-permute-start | bytes 49160 | tf_op jit(solution)/shard_map/ppermute | solution.py:415
  57.9 14.3 %collective-permute-start.8 = (bf16[1024,256]{1,0:T(8,128)(2,1)S(1)}, bf16[1024,256]{1,0:T(8,128)(2,1)S(1)}, u32[]{:S(2)}, u32[]{:S(2)}) collective-permute-start(bf16[1024,256]{1,0:T(8,128)(2,1)S(1)} %get-tuple-element.14.rest_0_), channel_id=1, source_target_pairs={{0,8},{1,9},{2,10},{3,11},{4,12},{5,13},{6,14},{7,15},{8,16},{9,17... | collective-permute-start | bytes 1572872 | tf_op jit(solution)/shard_map/ppermute | solution.py:50
  58.3 14.9 %collective-permute-start.9 = (bf16[1024,256]{1,0:T(8,128)(2,1)S(1)}, bf16[1024,256]{1,0:T(8,128)(2,1)S(1)}, u32[]{:S(2)}, u32[]{:S(2)}) collective-permute-start(bf16[1024,256]{1,0:T(8,128)(2,1)S(1)} %get-tuple-element.14.rest_0_), channel_id=1, source_target_pairs={{0,24},{1,25},{2,26},{3,27},{4,28},{5,29},{6,30},{7,31},{8,0},{9,1... | collective-permute-start | bytes 1572872 | tf_op jit(solution)/shard_map/ppermute | solution.py:50
  72.3 10.0 %collective-permute-start.10 = (bf16[512,256]{1,0:T(8,128)(2,1)S(1)}, bf16[512,256]{1,0:T(8,128)(2,1)S(1)}, u32[]{:S(2)}, u32[]{:S(2)}) collective-permute-start(bf16[512,256]{1,0:T(8,128)(2,1)S(1)} %slice.70), channel_id=1, source_target_pairs={{0,8},{1,9},{2,10},{3,11},{4,12},{5,13},{6,14},{7,15},{8,16},{9,17... | collective-permute-start | bytes 786440 | tf_op jit(solution)/shard_map/ppermute | solution.py:50
  73.2 9.1 %collective-permute-start.11 = (bf16[512,256]{1,0:T(8,128)(2,1)S(1)}, bf16[512,256]{1,0:T(8,128)(2,1)S(1)}, u32[]{:S(2)}, u32[]{:S(2)}) collective-permute-start(bf16[512,256]{1,0:T(8,128)(2,1)S(1)} %slice.71), channel_id=1, source_target_pairs={{0,24},{1,25},{2,26},{3,27},{4,28},{5,29},{6,30},{7,31},{8,0},{9,1... | collective-permute-start | bytes 786440 | tf_op jit(solution)/shard_map/ppermute | solution.py:50
  82.3 32.1 %copy-start.1 = (bf16[1,128,1024]{2,1,0:T(8,128)(2,1)S(1)}, bf16[1,128,1024]{2,1,0:T(8,128)(2,1)}, u32[]{:S(2)}) copy-start(bf16[1,128,1024]{2,1,0:T(8,128)(2,1)} %hist_ref.3) | copy-start | bytes 786436
  82.4 32.1 %copy-start.2 = (bf16[1,32,1024]{2,1,0:T(8,128)(2,1)S(1)}, bf16[1,32,1024]{2,1,0:T(8,128)(2,1)}, u32[]{:S(2)}) copy-start(bf16[1,32,1024]{2,1,0:T(8,128)(2,1)} %cand_ref.3) | copy-start | bytes 196612
  87.1 27.4 %all-to-all-start.1 = ((bf16[8,160,256]{2,1,0:T(8,128)(2,1)}), bf16[8,160,256]{2,1,0:T(8,128)(2,1)S(1)}, u32[]{:S(2)}, u32[]{:S(2)}) async-start(bf16[8,160,256]{2,1,0:T(8,128)(2,1)} %attend.5), calls=%async_computation.1 | async-start | bytes 1310720 | tf_op jit(solution)/shard_map/all_to_all | solution.py:473
  93.3 3.0 %collective-permute-start.12 = (bf16[8,64,1024]{2,1,0:T(8,128)(2,1)}, bf16[8,64,1024]{2,1,0:T(8,128)(2,1)S(1)}, u32[]{:S(2)}, u32[]{:S(2)}) collective-permute-start(bf16[8,64,1024]{2,1,0:T(8,128)(2,1)} %bitcast.33), channel_id=1, source_target_pairs={{0,1},{1,0},{2,3},{3,2},{4,5},{5,4},{6,7},{7,6},{8,9},{9,8},{10,11... | collective-permute-start | bytes 3145736 | tf_op jit(solution)/shard_map/ppermute | solution.py:50
  114.5 1.2 copy-start
Sparse Core Ops, SparseCore 0:
  9.8 43.1 all-gather.4
  55.4 37.8 all-gather.6
